TPU v7x, 32 devices: a whole 2x2x4 slice. The times are simulated.
32 devices in a mesh: fsdp: 4 (over y, core), ctx: 8 (over z, x).
Axes of the slice: x: 2, y: 2, z: 4, core: 2. Of those that a mesh axis runs over, the one named last changes fastest.
Arguments:
- featurized: bfloat16 [1024, 3, 4096], P('ctx', None, 'fsdp'), may hold values from -6 to 6
- short_taps: float32 [3, 3, 4096], P(None, None, 'fsdp'), may hold values from -3 to 3
- residues: float32 [4096, 16], P('fsdp'), may hold values from -1.5 to 1.5
- decay_rates: float32 [4096, 16], P('fsdp'), may hold values from 0.00048828125 to 0.05
- w_out: bfloat16 [4096, 8192], P('fsdp', 'ctx'), may hold values from -0.09375 to 0.09375
- grad_out: bfloat16 [1024, 8192], P('ctx'), may hold values from -6 to 6
Outputs:
- block_output: bfloat16 [1024, 8192], P('ctx', 'fsdp')
- grad_features: bfloat16 [1024, 3, 4096], P('ctx', None, 'fsdp')
All inputs are finite; a program needn't handle non-finite values.
Results may differ from a plain program's by a relative error of at most 0.02.
Values may be sent and summed in bfloat16 or wider, within the bound.
No kernel may reach another device: no remote copies, remote signals or barrier semaphores. Data moves between devices by JAX's collectives and lax.ppermute only.
A program may use at most 128 MiB of HBM per device.

v0:
```python
import math

import jax
import jax.numpy as jnp
from jax import lax
from jax.sharding import PartitionSpec as P

HIGHEST = lax.Precision.HIGHEST


def swapped(block, axis, distance):
    count = lax.axis_size(axis)
    route = []
    for low in range(count):
        high = low | 1 << distance
        if high != low and high < count:
            route += [(low, high), (high, low)]
    return lax.ppermute(block, axis, route)


def shifted(block, axis, distance):
    devices = range(lax.axis_size(axis))
    route = [(i - distance, i) for i in devices if i - distance in devices]
    return lax.ppermute(block, axis, route)


def angles(product_index, modulus):
    phases = (product_index % modulus).astype(jnp.float32) * (2.0 * math.pi / modulus)
    return (jnp.cos(phases), jnp.sin(phases))


def complex_contract(pattern, table_re, table_im, real_part, imag_part):
    first_term = jnp.einsum(pattern, table_re, real_part, precision=HIGHEST)
    second_term = jnp.einsum(pattern, table_im, imag_part, precision=HIGHEST)
    third_term = jnp.einsum(pattern, table_re, imag_part, precision=HIGHEST)
    fourth_term = jnp.einsum(pattern, table_im, real_part, precision=HIGHEST)
    return (first_term - second_term, third_term + fourth_term)


def token_tables(tokens_here):
    positions_all = jnp.arange(tokens_here)
    return angles(positions_all[:, None] * positions_all[None, :], tokens_here)


def reversed_bits(my_rank, bit_count):
    result = jnp.zeros((), jnp.int32)
    for section_bit in range(bit_count):
        result = result + (my_rank >> section_bit & 1) * (1 << bit_count - 1 - section_bit)
    return result


def partner_step(values_now, section_bit, my_rank, inverse):
    partner_data = swapped(values_now.astype(jnp.bfloat16), "ctx", section_bit).astype(
        values_now.dtype
    )
    half_span = 1 << section_bit
    upper_side = my_rank >> section_bit & 1 == 1
    cos_turn, sin_turn = angles(my_rank % half_span, 2 * half_span)
    if inverse:
        spun_re = partner_data[0] * cos_turn - partner_data[1] * sin_turn
        spun_im = partner_data[1] * cos_turn + partner_data[0] * sin_turn
        lower_new = jnp.stack([values_now[0] + spun_re, values_now[1] + spun_im]) * 0.5
        mine_re = values_now[0] * cos_turn - values_now[1] * sin_turn
        mine_im = values_now[1] * cos_turn + values_now[0] * sin_turn
        upper_new = jnp.stack([partner_data[0] - mine_re, partner_data[1] - mine_im]) * 0.5
    else:
        lower_new = values_now + partner_data
        differ = partner_data - values_now
        upper_new = jnp.stack(
            [
                differ[0] * cos_turn + differ[1] * sin_turn,
                differ[1] * cos_turn - differ[0] * sin_turn,
            ]
        )
    return jnp.where(upper_side, upper_new, lower_new)


def forward_partners(signal):
    tokens_here = signal.shape[0]
    devices = lax.axis_size("ctx")
    bit_count = devices.bit_length() - 1
    my_rank = lax.axis_index("ctx")
    full_length = 2 * devices * tokens_here
    half_turn = my_rank.astype(jnp.float32) * (math.pi / devices)
    values_now = jnp.stack(
        [
            jnp.stack([signal, signal * jnp.cos(half_turn)]),
            jnp.stack([jnp.zeros_like(signal), -signal * jnp.sin(half_turn)]),
        ]
    )
    for section_bit in reversed(range(bit_count)):
        values_now = partner_step(values_now, section_bit, my_rank, False)
    spectral_rows = 2 * reversed_bits(my_rank, bit_count) + jnp.arange(2)
    cos_twist, sin_twist = angles(
        spectral_rows[:, None] * jnp.arange(tokens_here)[None, :], full_length
    )
    cos_twist = cos_twist[:, :, None, None]
    sin_twist = sin_twist[:, :, None, None]
    twist_re = values_now[0] * cos_twist + values_now[1] * sin_twist
    twist_im = values_now[1] * cos_twist - values_now[0] * sin_twist
    cos_tokens, sin_tokens = token_tables(tokens_here)
    return complex_contract("ks,esgc->ekgc", cos_tokens, -sin_tokens, twist_re, twist_im)


def inverse_partners(spec_re, spec_im):
    tokens_here = spec_re.shape[1]
    devices = lax.axis_size("ctx")
    bit_count = devices.bit_length() - 1
    my_rank = lax.axis_index("ctx")
    full_length = 2 * devices * tokens_here
    cos_tokens, sin_tokens = token_tables(tokens_here)
    plain_re, plain_im = complex_contract("sk,ekgc->esgc", cos_tokens, sin_tokens, spec_re, spec_im)
    spectral_rows = 2 * reversed_bits(my_rank, bit_count) + jnp.arange(2)
    cos_twist, sin_twist = angles(
        spectral_rows[:, None] * jnp.arange(tokens_here)[None, :], full_length
    )
    cos_twist = cos_twist[:, :, None, None]
    sin_twist = sin_twist[:, :, None, None]
    twist_re = plain_re * cos_twist - plain_im * sin_twist
    twist_im = plain_re * sin_twist + plain_im * cos_twist
    values_now = jnp.stack([twist_re, twist_im])
    for section_bit in range(bit_count):
        values_now = partner_step(values_now, section_bit, my_rank, True)
    half_turn = my_rank.astype(jnp.float32) * (math.pi / devices)
    real_part = (
        values_now[0, 0]
        + values_now[0, 1] * jnp.cos(half_turn)
        - values_now[1, 1] * jnp.sin(half_turn)
    )
    return real_part / (2.0 * tokens_here)


def to_spectrum(signal):
    return forward_partners(signal)


def from_spectrum(spec_re, spec_im):
    return inverse_partners(spec_re, spec_im)


def modal_spectrum(residues, decay_rates, spectral_rows, tokens_here, devices):
    full_length = 2 * devices * tokens_here
    sequence = devices * tokens_here
    frequency = spectral_rows[:, None] + 2 * devices * jnp.arange(tokens_here)[None, :]
    angle_now = frequency.astype(jnp.float32) * (math.pi / full_length)
    half_sine = jnp.sin(angle_now)[:, :, None]
    full_sine = jnp.sin(2.0 * angle_now)[:, :, None]
    parity_sign = (1 - 2 * (spectral_rows % 2)).astype(jnp.float32)[:, None, None]

    def add_mode(mode_index, totals):
        rates_now = lax.dynamic_slice_in_dim(decay_rates, mode_index, 1, 1)[:, 0]
        weight = lax.dynamic_slice_in_dim(residues, mode_index, 1, 1)[:, 0] * jnp.sqrt(rates_now)
        decay_now = jnp.exp(-rates_now)
        numerator = 1.0 - parity_sign * jnp.exp(-rates_now * sequence)
        denom_re = -jnp.expm1(-rates_now) + 2.0 * decay_now * half_sine * half_sine
        denom_im = decay_now * full_sine
        scaled = weight * numerator / (denom_re * denom_re + denom_im * denom_im)
        return (totals[0] + scaled * denom_re, totals[1] - scaled * denom_im)

    empty = jnp.zeros((spectral_rows.shape[0], tokens_here, residues.shape[0]), jnp.float32)
    spec_re, spec_im = lax.fori_loop(0, residues.shape[1], add_mode, (empty, empty))
    return (spec_re[:, :, None, :], spec_im[:, :, None, :])


def own_filter(residues, decay_rates, tokens_here):
    devices = lax.axis_size("ctx")
    my_rank = lax.axis_index("ctx")
    pair_rank = reversed_bits(my_rank, devices.bit_length() - 1)
    return modal_spectrum(
        residues, decay_rates, 2 * pair_rank + jnp.arange(2), tokens_here, devices
    )


def per_device(featurized, short_taps, residues, decay_rates, w_out, grad_out):
    tokens_here = featurized.shape[0]
    before = shifted(featurized[tokens_here - 2 :], "ctx", 1)
    raw_values = featurized.astype(jnp.float32)
    extended = jnp.concatenate([before.astype(jnp.float32), raw_values], axis=0)
    mixed_in = (
        short_taps[0] * extended[2:]
        + short_taps[1] * extended[1 : tokens_here + 1]
        + short_taps[2] * extended[:tokens_here]
    )
    query_part = mixed_in[:, 0]
    key_part = mixed_in[:, 1]
    value_part = mixed_in[:, 2]
    carried = key_part * value_part
    signal_re, signal_im = to_spectrum(carried[:, None, :])
    filter_re, filter_im = own_filter(residues, decay_rates, tokens_here)
    conv_re = signal_re * filter_re - signal_im * filter_im
    conv_im = signal_re * filter_im + signal_im * filter_re
    convolved = from_spectrum(conv_re, conv_im)[:, 0]
    gated_out = (query_part * convolved).astype(jnp.bfloat16)
    w_full = lax.all_gather(w_out, "ctx", axis=1, tiled=True)
    partial_sum = jnp.dot(gated_out, w_full, preferred_element_type=jnp.float32)
    block_output = lax.psum_scatter(
        partial_sum.astype(jnp.bfloat16), "fsdp", scatter_dimension=1, tiled=True
    )
    grad_gated = lax.dot_general(
        grad_out, w_full, (((1,), (1,)), ((), ())), preferred_element_type=jnp.float32
    )
    grad_query = grad_gated * convolved
    grad_conv = grad_gated * query_part
    delta_re, delta_im = to_spectrum(grad_conv[:, None, :])
    back_re = filter_re * delta_re + filter_im * delta_im
    back_im = filter_re * delta_im - filter_im * delta_re
    grad_carried = from_spectrum(back_re, back_im)[:, 0]
    grad_mixed = jnp.stack([grad_query, grad_carried * value_part, grad_carried * key_part], axis=1)
    following = shifted(grad_mixed[:2], "ctx", -1)
    padded = jnp.concatenate([grad_mixed, following], axis=0)
    grad_features = (
        short_taps[0] * padded[:tokens_here]
        + short_taps[1] * padded[1 : tokens_here + 1]
        + short_taps[2] * padded[2:]
    ).astype(jnp.bfloat16)
    return (block_output, grad_features)


def solution(mesh):
    placed = (
        P("ctx", None, "fsdp"),
        P(None, None, "fsdp"),
        P("fsdp", None),
        P("fsdp", None),
        P("fsdp", "ctx"),
        P("ctx", None),
    )
    return jax.shard_map(
        per_device,
        mesh=mesh,
        in_specs=placed,
        out_specs=(P("ctx", "fsdp"), P("ctx", None, "fsdp")),
        check_vma=False,
    )
```

profile of v0, /device:TPU:4, one launch (start us, length us, event | category | flops | bytes accessed | tf_op | source)
XLA Modules:
  0.0 635.5 jit_solution(9236700009221196365)
XLA Ops:
  8.5 3.4 collective-permute-start
  11.9 1.3 convert_element_type.242
  13.5 3.3 fusion.30
  20.3 4.1 collective-permute-start.1
  24.4 259.0 %all-gather.2.cloned.1.call-done = bf16[1024,8192]{1,0:T(8,128)(2,1)} async-done(((bf16[1024,1024]{1,0:T(8,128)(2,1)}), bf16[1024,8192]{1,0:T(8,128)(2,1)}) %all-gather.2.cloned.1.call-update) | async-done | bytes 16777232 | tf_op jit(solution)/shard_map/all_gather | solution.py:194
  283.4 11.4 %fusion.229 = f32[128,1024]{1,0:T(8,128)S(1)} fusion(bf16[128,8192]{1,0:T(8,128)(2,1)S(1)} %copy-done, bf16[1024,8192]{1,0:T(8,128)(2,1)} %all-gather.2.cloned.1.call-done), kind=kOutput, calls=%fused_computation.350 | convolution fusion | flops 2147483648 | bytes 19398656 | tf_op jit(solution)/shard_map/dot_general | solution.py:199
  294.8 1.4 fusion.205
  297.7 1.5 collective-permute-start.7
  299.5 2.2 convert_subtract_fusion.5
  301.7 43.6 %collective-permute-done.7 = bf16[2,2,128,1,1024]{4,2,1,3,0:T(8,128)(2,1)} collective-permute-done((bf16[2,2,128,1,1024]{4,2,1,3,0:T(8,128)(2,1)}, bf16[2,2,128,1,1024]{4,2,1,3,0:T(8,128)(2,1)}, u32[]{:S(2)}, u32[]{:S(2)}) %collective-permute-start.7) | collective-permute-done | bytes 1048608 | tf_op jit(solution)/shard_map/ppermute | solution.py:18
  345.3 1.5 convert_subtract_fusion.2
  346.8 2.1 multiply_add_fusion.5
  348.9 3.5 fusion.223
  352.4 28.9 %while.18 = (s32[]{:T(128)}, f32[2,128,1024]{2,1,0:T(8,128)S(1)}, f32[2,128,1024]{2,1,0:T(8,128)S(1)}, f32[1024,16]{0,1:T(8,128)}, f32[1024,16]{0,1:T(8,128)}, /...) while((s32[]{:T(128)}, f32[2,128,1024]{2,1,0:T(8,128)S(1)}, ...), condition=%wide.region_1.2_spmd.clone.clone.clone, body=%wide.region_0.1_spmd.clone.clone.clone.sunk | while | flops 3682337 | bytes 4268687 | solution.py:161
  381.5 4.8 fusion.215
  386.3 2.0 collective-permute-start.8
  388.3 1.5 convert_subtract_fusion.4
  390.1 3.5 fusion.221
  394.3 1.4 copy.10
  396.1 15.5 %collective-permute-done.8 = bf16[2,2,128,1,1024]{4,2,1,3,0:T(8,128)(2,1)S(1)} collective-permute-done((bf16[2,2,128,1,1024]{4,2,1,3,0:T(8,128)(2,1)}, bf16[2,2,128,1,1024]{4,2,1,3,0:T(8,128)(2,1)S(1)}, u32[]{:S(2)}, u32[]{:S(2)}) %collective-permute-start.8) | collective-permute-done | bytes 1048608 | tf_op jit(solution)/shard_map/ppermute | solution.py:18
  412.6 2.3 convert_subtract_fusion.1
  418.5 1.6 convert_subtract_fusion.3
  420.3 2.0 fusion.17
  422.3 2.0 fusion.88
  424.3 2.0 fusion.89
  426.4 15.4 %collective-permute-done.9 = bf16[2,2,128,1,1024]{4,2,1,3,0:T(8,128)(2,1)S(1)} collective-permute-done((bf16[2,2,128,1,1024]{4,2,1,3,0:T(8,128)(2,1)S(1)}, bf16[2,2,128,1,1024]{4,2,1,3,0:T(8,128)(2,1)S(1)}, u32[]{:S(2)}, u32[]{:S(2)}) %collective-permute-start.9) | collective-permute-done | bytes 1048608 | tf_op jit(solution)/shard_map/ppermute | solution.py:18
  442.9 2.0 fusion.90
  445.0 2.2 fusion.91
  447.2 2.0 fusion.42
  449.2 2.0 fusion.41
  451.3 2.0 fusion.38
  453.3 2.3 fusion.73
  457.0 1.5 fusion.69
  458.5 1.3 fusion.39
  461.1 1.3 fusion.52
  462.4 1.3 fusion.36
  463.7 1.3 fusion.35
  465.0 1.8 fusion.77
  467.6 22.9 %collective-permute-done.4 = bf16[2,2,128,1,1024]{4,2,1,3,0:T(8,128)(2,1)S(1)} collective-permute-done((bf16[2,2,128,1,1024]{4,2,1,3,0:T(8,128)(2,1)S(1)}, bf16[2,2,128,1,1024]{4,2,1,3,0:T(8,128)(2,1)S(1)}, u32[]{:S(2)}, u32[]{:S(2)}) %collective-permute-start.4) | collective-permute-done | bytes 1048608 | tf_op jit(solution)/shard_map/ppermute | solution.py:18
  494.0 20.7 %collective-permute-done.5 = bf16[2,2,128,1,1024]{4,2,1,3,0:T(8,128)(2,1)S(1)} collective-permute-done((bf16[2,2,128,1,1024]{4,2,1,3,0:T(8,128)(2,1)S(1)}, bf16[2,2,128,1,1024]{4,2,1,3,0:T(8,128)(2,1)S(1)}, u32[]{:S(2)}, u32[]{:S(2)}) %collective-permute-start.5) | collective-permute-done | bytes 1048608 | tf_op jit(solution)/shard_map/ppermute | solution.py:18
  518.1 2.2 fusion.211
  521.4 40.2 %collective-permute-done.6 = bf16[2,2,128,1,1024]{4,2,1,3,0:T(8,128)(2,1)S(1)} collective-permute-done((bf16[2,2,128,1,1024]{4,2,1,3,0:T(8,128)(2,1)S(1)}, bf16[2,2,128,1,1024]{4,2,1,3,0:T(8,128)(2,1)S(1)}, u32[]{:S(2)}, u32[]{:S(2)}) %collective-permute-start.6) | collective-permute-done | bytes 1048608 | tf_op jit(solution)/shard_map/ppermute | solution.py:18
  565.7 3.7 convolution_convert_fusion
  569.4 1.6 convert_element_type.272
  573.1 45.7 %collective-permute-done.12 = bf16[2,2,128,1,1024]{4,2,1,3,0:T(8,128)(2,1)S(1)} collective-permute-done((bf16[2,2,128,1,1024]{4,2,1,3,0:T(8,128)(2,1)S(1)}, bf16[2,2,128,1,1024]{4,2,1,3,0:T(8,128)(2,1)S(1)}, u32[]{:S(2)}, u32[]{:S(2)}) %collective-permute-start.12) | collective-permute-done | bytes 1048608 | tf_op jit(solution)/shard_map/ppermute | solution.py:18
  620.9 1.3 collective-permute-start.13
  622.2 4.4 collective-permute-done.13
  626.8 1.4 fusion.32
  (216 shorter events, 60.9 us)
Async XLA Ops:
  7.2 276.2 %copy-start = (bf16[128,8192]{1,0:T(8,128)(2,1)S(1)}, bf16[128,8192]{1,0:T(8,128)(2,1)}, u32[]{:S(2)}) copy-start(bf16[128,8192]{1,0:T(8,128)(2,1)} %param.13) | copy-start | bytes 6291460
  7.2 1.3 copy-start.19
  7.2 4.7 copy-start.20
  7.2 276.2 %all-gather.2.cloned.1.call-start = ((), (), s32[]{:S(2)}) async-start(), calls=%async_computation.1 | async-start | bytes 18874368 | tf_op jit(solution)/shard_map/all_gather | solution.py:194
  7.9 620.2 %reduce-scatter.2.cloned.1.call-start = ((), (), s32[]{:S(2)}) async-start(), calls=%async_computation.2 | async-start | bytes 2621440 | tf_op jit(solution)/shard_map/reduce_scatter | solution.py:196
  8.5 4.9 collective-permute-start
  16.7 1.2 copy-start.11
  17.9 2.3 copy-start.7
  18.0 1.1 copy-start.9
  20.3 279.2 %collective-permute-start.1 = (bf16[2,2,128,1,1024]{4,2,1,3,0:T(8,128)(2,1)}, bf16[2,2,128,1,1024]{4,2,1,3,0:T(8,128)(2,1)}, u32[]{:S(2)}, u32[]{:S(2)}) collective-permute-start(bf16[2,2,128,1,1024]{4,2,1,3,0:T(8,128)(2,1)} %fusion.44), channel_id=1, source_target_pairs={{0,4},{4,0},{1,5},{5,1},{2,6},{6,2},{3,7},{7,3},{8,12},{12,8},{9,1... | collective-permute-start | bytes 3145736 | tf_op jit(solution)/shard_map/ppermute | solution.py:18
  294.8 1.6 copy-start.14
  296.4 3.0 copy-start.5
  297.7 47.6 %collective-permute-start.7 = (bf16[2,2,128,1,1024]{4,2,1,3,0:T(8,128)(2,1)}, bf16[2,2,128,1,1024]{4,2,1,3,0:T(8,128)(2,1)}, u32[]{:S(2)}, u32[]{:S(2)}) collective-permute-start(bf16[2,2,128,1,1024]{4,2,1,3,0:T(8,128)(2,1)} %fusion.43), channel_id=1, source_target_pairs={{0,4},{4,0},{1,5},{5,1},{2,6},{6,2},{3,7},{7,3},{8,12},{12,8},{9,1... | collective-permute-start | bytes 3145736 | tf_op jit(solution)/shard_map/ppermute | solution.py:18
  299.4 45.8 %copy-start.6 = (f32[1,2,128,1,1024]{4,2,1,3,0:T(8,128)S(1)}, f32[1,2,128,1,1024]{4,2,1,3,0:T(8,128)}, u32[]{:S(2)}) copy-start(f32[1,2,128,1,1024]{4,2,1,3,0:T(8,128)} %copy-done.5) | copy-start | bytes 3145732
  346.8 2.1 copy-start.8
  346.8 2.1 copy-start.10
  352.4 35.9 %collective-permute-start.2 = (bf16[2,2,128,1,1024]{4,2,1,3,0:T(8,128)(2,1)}, bf16[2,2,128,1,1024]{4,2,1,3,0:T(8,128)(2,1)}, u32[]{:S(2)}, u32[]{:S(2)}) collective-permute-start(bf16[2,2,128,1,1024]{4,2,1,3,0:T(8,128)(2,1)} %get-tuple-element.277), channel_id=1, source_target_pairs={{0,2},{2,0},{1,3},{3,1},{4,6},{6,4},{5,7},{7,5},{8,10},{10,8},{9,1... | collective-permute-start | bytes 3145736 | tf_op jit(solution)/shard_map/ppermute | solution.py:18
  381.4 6.9 %copy-start.2 = (f32[2,2,128,1,1024]{4,2,1,3,0:T(8,128)S(1)}, f32[2,2,128,1,1024]{4,2,1,3,0:T(8,128)}, u32[]{:S(2)}) copy-start(f32[2,2,128,1,1024]{4,2,1,3,0:T(8,128)} %get-tuple-element.278) | copy-start | bytes 6291460
  386.3 25.3 %collective-permute-start.8 = (bf16[2,2,128,1,1024]{4,2,1,3,0:T(8,128)(2,1)}, bf16[2,2,128,1,1024]{4,2,1,3,0:T(8,128)(2,1)S(1)}, u32[]{:S(2)}, u32[]{:S(2)}) collective-permute-start(bf16[2,2,128,1,1024]{4,2,1,3,0:T(8,128)(2,1)} %get-tuple-element.265), channel_id=1, source_target_pairs={{0,2},{2,0},{1,3},{3,1},{4,6},{6,4},{5,7},{7,5},{8,10},{10,8},{9,1... | collective-permute-start | bytes 3145736 | tf_op jit(solution)/shard_map/ppermute | solution.py:18
  393.7 24.8 %collective-permute-start.3 = (bf16[2,2,128,1,1024]{4,2,1,3,0:T(8,128)(2,1)}, bf16[2,2,128,1,1024]{4,2,1,3,0:T(8,128)(2,1)}, u32[]{:S(2)}, u32[]{:S(2)}) collective-permute-start(bf16[2,2,128,1,1024]{4,2,1,3,0:T(8,128)(2,1)} %get-tuple-element.275), channel_id=1, source_target_pairs={{0,1},{1,0},{2,3},{3,2},{4,5},{5,4},{6,7},{7,6},{8,9},{9,8},{10,11... | collective-permute-start | bytes 3145736 | tf_op jit(solution)/shard_map/ppermute | solution.py:18
  411.6 1.0 copy-start.16
  414.9 1.6 copy-start.3
  414.9 1.8 copy-start.17
  416.7 1.8 copy-start.4
  417.3 24.4 %collective-permute-start.9 = (bf16[2,2,128,1,1024]{4,2,1,3,0:T(8,128)(2,1)S(1)}, bf16[2,2,128,1,1024]{4,2,1,3,0:T(8,128)(2,1)S(1)}, u32[]{:S(2)}, u32[]{:S(2)}) collective-permute-start(bf16[2,2,128,1,1024]{4,2,1,3,0:T(8,128)(2,1)S(1)} %get-tuple-element.263), channel_id=1, source_target_pairs={{0,1},{1,0},{2,3},{3,2},{4,5},{5,4},{6,7},{7,6},{8,9},{9,8},{10,11... | collective-permute-start | bytes 3145736 | tf_op jit(solution)/shard_map/ppermute | solution.py:18
  451.3 2.1 copy-start.18
  467.0 23.5 %collective-permute-start.4 = (bf16[2,2,128,1,1024]{4,2,1,3,0:T(8,128)(2,1)S(1)}, bf16[2,2,128,1,1024]{4,2,1,3,0:T(8,128)(2,1)S(1)}, u32[]{:S(2)}, u32[]{:S(2)}) collective-permute-start(bf16[2,2,128,1,1024]{4,2,1,3,0:T(8,128)(2,1)S(1)} %pad_maximum_fusion.5), channel_id=1, source_target_pairs={{0,1},{1,0},{2,3},{3,2},{4,5},{5,4},{6,7},{7,6},{8,9},{9,8},{10,11... | collective-permute-start | bytes 3145736 | tf_op jit(solution)/shard_map/ppermute | solution.py:18
  492.1 22.6 %collective-permute-start.5 = (bf16[2,2,128,1,1024]{4,2,1,3,0:T(8,128)(2,1)S(1)}, bf16[2,2,128,1,1024]{4,2,1,3,0:T(8,128)(2,1)S(1)}, u32[]{:S(2)}, u32[]{:S(2)}) collective-permute-start(bf16[2,2,128,1,1024]{4,2,1,3,0:T(8,128)(2,1)S(1)} %get-tuple-element.269), channel_id=1, source_target_pairs={{0,2},{2,0},{1,3},{3,1},{4,6},{6,4},{5,7},{7,5},{8,10},{10,8},{9,1... | collective-permute-start | bytes 3145736 | tf_op jit(solution)/shard_map/ppermute | solution.py:18
  493.3 23.7 %collective-permute-start.10 = (bf16[2,2,128,1,1024]{4,2,1,3,0:T(8,128)(2,1)S(1)}, bf16[2,2,128,1,1024]{4,2,1,3,0:T(8,128)(2,1)S(1)}, u32[]{:S(2)}, u32[]{:S(2)}) collective-permute-start(bf16[2,2,128,1,1024]{4,2,1,3,0:T(8,128)(2,1)S(1)} %pad_maximum_fusion.6), channel_id=1, source_target_pairs={{0,1},{1,0},{2,3},{3,2},{4,5},{5,4},{6,7},{7,6},{8,9},{9,8},{10,11... | collective-permute-start | bytes 3145736 | tf_op jit(solution)/shard_map/ppermute | solution.py:18
  516.6 45.0 %collective-permute-start.6 = (bf16[2,2,128,1,1024]{4,2,1,3,0:T(8,128)(2,1)S(1)}, bf16[2,2,128,1,1024]{4,2,1,3,0:T(8,128)(2,1)S(1)}, u32[]{:S(2)}, u32[]{:S(2)}) collective-permute-start(bf16[2,2,128,1,1024]{4,2,1,3,0:T(8,128)(2,1)S(1)} %get-tuple-element.267), channel_id=1, source_target_pairs={{0,4},{4,0},{1,5},{5,1},{2,6},{6,2},{3,7},{7,3},{8,12},{12,8},{9,1... | collective-permute-start | bytes 3145736 | tf_op jit(solution)/shard_map/ppermute | solution.py:18
  517.3 46.6 %slice-start = ((s8[16777216]{0:T(1024)(128)(4,1)}), s8[4194304]{0:T(1024)(128)(4,1)S(1)}, s32[]{:S(2)}) async-start(s8[16777216]{0:T(1024)(128)(4,1)} %bitcast.345), calls=%async_computation.3 | async-start | bytes 8388608
  518.0 45.8 %slice-start.1 = ((s8[16777216]{0:T(1024)(128)(4,1)}), s8[4194304]{0:T(1024)(128)(4,1)S(1)}, s32[]{:S(2)}) async-start(s8[16777216]{0:T(1024)(128)(4,1)} %bitcast.345), calls=%async_computation.4 | async-start | bytes 8388608
  520.2 43.7 %slice-start.2 = ((s8[16777216]{0:T(1024)(128)(4,1)}), s8[4194304]{0:T(1024)(128)(4,1)S(1)}, s32[]{:S(2)}) async-start(s8[16777216]{0:T(1024)(128)(4,1)} %bitcast.345), calls=%async_computation.5 | async-start | bytes 8388608
  520.2 49.2 %collective-permute-start.11 = (bf16[2,2,128,1,1024]{4,2,1,3,0:T(8,128)(2,1)}, bf16[2,2,128,1,1024]{4,2,1,3,0:T(8,128)(2,1)}, u32[]{:S(2)}, u32[]{:S(2)}) collective-permute-start(bf16[2,2,128,1,1024]{4,2,1,3,0:T(8,128)(2,1)} %get-tuple-element.257), channel_id=1, source_target_pairs={{0,2},{2,0},{1,3},{3,1},{4,6},{6,4},{5,7},{7,5},{8,10},{10,8},{9,1... | collective-permute-start | bytes 3145736 | tf_op jit(solution)/shard_map/ppermute | solution.py:18
  562.6 1.0 copy-start.15
  562.6 2.3 slice-start.3
  563.7 2.0 copy-start.12
  569.4 1.9 copy-start.13
  573.0 45.8 %collective-permute-start.12 = (bf16[2,2,128,1,1024]{4,2,1,3,0:T(8,128)(2,1)S(1)}, bf16[2,2,128,1,1024]{4,2,1,3,0:T(8,128)(2,1)S(1)}, u32[]{:S(2)}, u32[]{:S(2)}) collective-permute-start(bf16[2,2,128,1,1024]{4,2,1,3,0:T(8,128)(2,1)S(1)} %get-tuple-element.255), channel_id=1, source_target_pairs={{0,4},{4,0},{1,5},{5,1},{2,6},{6,2},{3,7},{7,3},{8,12},{12,8},{9,1... | collective-permute-start | bytes 3145736 | tf_op jit(solution)/shard_map/ppermute | solution.py:18
  620.9 5.7 collective-permute-start.13
  626.6 1.6 copy-start.1
Sparse Core Ops, SparseCore 0:
  10.2 273.1 all-gather.1
  569.5 27.6 reduce-scatter.1
where the time goes:
time: 645 us; the launch traced here: 635 us
  waiting for transfers between devices  469 us (73%)
  other arithmetic  79.8 us (12%)
  matrix products  42.9 us (7%)
  starting transfers between devices  17.7 us (3%)
  between operations  15.8 us (2%)
  local copies, waits for them, and re-layouts  9.57 us (1%)
    all_gather x1, waiting for transfers between devices, per_device(): w_full = lax.all_gather(w_out, 'ctx', axis=1, tiled=True)  259 us
    ppermute x12, waiting for transfers between devices, swapped(): return lax.ppermute(block, axis, route)  204 us
    convert_element_type x10, other arithmetic, partner_step(): values_now.astype(jnp.bfloat16)  19.5 us
    mul x16, other arithmetic, add_mode(): lax.dynamic_slice_in_dim(residues, mode_index, 1, 1)[:, 0]  13.1 us
    ppermute x12, starting transfers between devices, swapped(): return lax.ppermute(block, axis, route)  12.9 us
  transfers between devices with their start and end apart: 16, of which 10 were waited for; matrix products, arithmetic and copies ran while one was open for 14% of the time, Pallas kernels for 0%

commit v1 on v0

v1 whole, which is shorter than its diff:
```python
import functools

import jax
import jax.numpy as jnp
from jax import lax
from jax.experimental import pallas as pl
from jax.experimental.pallas import tpu as pltpu
from jax.sharding import PartitionSpec as P

LANES = 128
F32 = jnp.float32
BF16 = jnp.bfloat16
VMEM = pl.BlockSpec(memory_space=pltpu.VMEM)
SMEM = pl.BlockSpec(memory_space=pltpu.SMEM)


def swapped(block, axis, mask):
    count = lax.axis_size(axis)
    return lax.ppermute(block, axis, [(i, i ^ mask) for i in range(count)])


def shifted(block, axis, distance):
    devices = range(lax.axis_size(axis))
    route = [(i - distance, i) for i in devices if i - distance in devices]
    return lax.ppermute(block, axis, route)


def tree_sum(terms):
    terms = list(terms)
    while len(terms) > 1:
        paired = [terms[i] + terms[i + 1] for i in range(0, len(terms) - 1, 2)]
        terms = paired + terms[len(terms) - len(terms) % 2 :]
    return terms[0]


def kernel_call(body, out_shape, in_specs, scratch_shapes=(), flops=0, moved=0):
    return pl.pallas_call(
        body,
        out_shape=out_shape,
        in_specs=in_specs,
        out_specs=jax.tree.map(lambda _: VMEM, out_shape),
        scratch_shapes=scratch_shapes,
        compiler_params=pltpu.CompilerParams(vmem_limit_bytes=48 * 1024 * 1024),
        cost_estimate=pl.CostEstimate(flops=flops, bytes_accessed=moved, transcendentals=0),
    )


def chunk_state_kernel(tokens, x_ref, taps_ref, rates_ref, mixed_ref, state_ref):
    modes = rates_ref.shape[0]
    decays = [jnp.exp(-rates_ref[n]) for n in range(modes)]

    def mix(t):
        parts = []
        for j in range(3):
            part = (
                taps_ref[0, j] * x_ref[t + 2, j]
                + taps_ref[1, j] * x_ref[t + 1, j]
                + taps_ref[2, j] * x_ref[t, j]
            )
            mixed_ref[t, j] = part
            parts.append(part)
        return parts[1] * parts[2]

    def step(t, states):
        carried = mix(t)
        return tuple(decays[n] * states[n] + carried for n in range(modes))

    empty = jnp.zeros(state_ref.shape[1:], F32)
    states = lax.fori_loop(0, tokens, step, (empty,) * modes, unroll=4)
    for n in range(modes):
        state_ref[n] = states[n]
    mix(tokens)
    mix(tokens + 1)


def incoming(tokens, rates, arrived, distance_ref, n):
    total = None
    for k, block in enumerate(arrived):
        reach = jnp.exp(-rates * (tokens * distance_ref[0, k])) * distance_ref[1, k]
        term = reach * block[n].astype(F32)
        total = term if total is None else total + term
    return total


def convolve_kernel(tokens, peers, distance_ref, rates_ref, residues_ref, mixed_ref, *refs):
    arrived, (gated_ref, convolved_ref, rows_ref) = refs[:peers], refs[peers:]
    modes, tall = rates_ref.shape[0], rates_ref.shape[1]
    decays = [jnp.exp(-rates_ref[n]) for n in range(modes)]
    weights = [residues_ref[n] * jnp.sqrt(rates_ref[n]) for n in range(modes)]
    states = tuple(
        incoming(tokens, rates_ref[n], arrived, distance_ref, n) for n in range(modes)
    )

    def advance(t, states):
        carried = mixed_ref[t, 1] * mixed_ref[t, 2]
        states = tuple(decays[n] * states[n] + carried for n in range(modes))
        convolved = tree_sum([weights[n] * states[n] for n in range(modes)])
        convolved_ref[t] = convolved
        return states, convolved

    def step(t, states):
        states, convolved = advance(t, states)
        rows_ref[pl.ds(pl.multiple_of(t * tall, tall), tall), :] = mixed_ref[t, 0] * convolved
        return states

    states = lax.fori_loop(0, tokens, step, states, unroll=4)
    states, _ = advance(tokens, states)
    advance(tokens + 1, states)
    for start in range(0, tokens, 16):
        for s in range(tall):
            rows = rows_ref[pl.ds(start * tall + s, 16, stride=tall), :]
            gated_ref[start : start + 16, s * LANES : (s + 1) * LANES] = rows.astype(BF16)


def back_state_kernel(tokens, peers, half_ref, rates_ref, mixed_ref, *refs):
    terms, (grads_ref, state_ref, head_ref) = refs[: peers + 1], refs[peers + 1 :]
    modes, tall = rates_ref.shape[0], rates_ref.shape[1]
    decays = [jnp.exp(-rates_ref[n]) for n in range(modes)]
    offset = half_ref[0] * (tokens // 2)
    for start in range(0, tokens, 16):
        own = pl.multiple_of((start + offset) % tokens, 16)
        for s in range(tall):
            lanes = slice(s * LANES, (s + 1) * LANES)
            total = tree_sum([term[pl.ds(own, 16), lanes].astype(F32) for term in terms])
            grads_ref[pl.ds(start * tall + s, 16, stride=tall), :] = total

    def step(i, states):
        t = tokens - 1 - i
        here = grads_ref[pl.ds(pl.multiple_of(t * tall, tall), tall), :] * mixed_ref[t, 0]
        return tuple(decays[n] * states[n] + here for n in range(modes))

    empty = jnp.zeros(state_ref.shape[1:], F32)
    states = lax.fori_loop(0, tokens, step, (empty,) * modes, unroll=4)
    for n in range(modes):
        state_ref[n] = states[n].astype(state_ref.dtype)
    head_ref[0] = grads_ref[0:tall, :]
    head_ref[1] = grads_ref[tall : 2 * tall, :]


def adjoint_kernel(
    tokens, peers, distance_ref, rates_ref, residues_ref, taps_ref, mixed_ref, convolved_ref,
    grads_ref, after_ref, *refs
):
    arrived, (out_ref,) = refs[:peers], refs[peers:]
    modes, tall = rates_ref.shape[0], rates_ref.shape[1]
    decays = [jnp.exp(-rates_ref[n]) for n in range(modes)]
    weights = [residues_ref[n] * jnp.sqrt(rates_ref[n]) for n in range(modes)]

    def spread(t, grad, states):
        grad_carried = tree_sum([weights[n] * states[n] for n in range(modes)])
        return (
            grad * convolved_ref[t],
            grad_carried * mixed_ref[t, 2],
            grad_carried * mixed_ref[t, 1],
        )

    states = tuple(
        incoming(tokens, rates_ref[n], arrived, distance_ref, n) for n in range(modes)
    )
    first = spread(tokens, after_ref[0], states)
    after_that = tuple(
        (states[n] - after_ref[0] * mixed_ref[tokens, 0]) * jnp.exp(rates_ref[n])
        for n in range(modes)
    )
    second = spread(tokens + 1, after_ref[1], after_that)

    def step(i, carry):
        states, first, second = carry
        t = tokens - 1 - i
        grad = grads_ref[pl.ds(pl.multiple_of(t * tall, tall), tall), :]
        here = grad * mixed_ref[t, 0]
        states = tuple(decays[n] * states[n] + here for n in range(modes))
        mine = spread(t, grad, states)
        for j in range(3):
            out_ref[t, j] = (
                taps_ref[0, j] * mine[j] + taps_ref[1, j] * first[j] + taps_ref[2, j] * second[j]
            )
        return states, mine, first

    lax.fori_loop(0, tokens, step, (states, first, second), unroll=4)


def per_device(featurized, short_taps, residues, decay_rates, w_out, grad_out):
    tokens, _, wide = featurized.shape
    tall = wide // LANES
    modes = residues.shape[1]
    n_ctx, n_fsdp = lax.axis_size("ctx"), lax.axis_size("fsdp")
    me, group = lax.axis_index("ctx"), lax.axis_index("fsdp")
    pair, side = me // 2, me % 2
    core, line = group % 2, group // 2
    n_pair, n_line = n_ctx // 2, n_fsdp // 2
    width = w_out.shape[1]
    half = tokens // 2
    masks = range(1, n_ctx)

    before = shifted(featurized[tokens - 2 :], "ctx", 1)
    after = shifted(featurized[:2], "ctx", -1)

    own_rows = lax.dynamic_slice_in_dim(grad_out, core * half, half, 0)

    def columns(source, owner_pair):
        mine = lax.dynamic_slice_in_dim(source, (2 * owner_pair + side) * width, width, 1)
        other = lax.dynamic_slice_in_dim(source, (2 * owner_pair + 1 - side) * width, width, 1)
        return mine, other

    near = [None] * n_pair
    for k in range(1, n_pair):
        near[k] = swapped(jnp.concatenate(columns(own_rows, pair ^ k), axis=1), "ctx", 2 * k)
    far = [None] + [swapped(near[k], "fsdp", 1) for k in range(1, n_pair)]
    w_other = swapped(w_out, "ctx", 1)

    extended = jnp.concatenate([before, featurized, after], axis=0).astype(F32)
    extended = extended.reshape(tokens + 4, 3, tall, LANES)
    taps = short_taps.reshape(3, 3, tall, LANES)
    rates = decay_rates.T.reshape(modes, tall, LANES)
    weights = residues.T.reshape(modes, tall, LANES)
    state_shape = jax.ShapeDtypeStruct((modes, tall, LANES), F32)
    mixed, state = kernel_call(
        functools.partial(chunk_state_kernel, tokens),
        (jax.ShapeDtypeStruct((tokens + 2, 3, tall, LANES), F32), state_shape),
        [VMEM] * 3,
        flops=50 * tokens * wide,
        moved=8 * tokens * 3 * wide,
    )(extended, taps, rates)
    arrived = [swapped(state, "ctx", k) for k in masks]
    partners = me ^ jnp.arange(1, n_ctx)
    ahead = me - partners
    distance = jnp.stack([jnp.maximum(ahead - 1, 0), ahead > 0]).astype(F32)
    back_distance = jnp.stack([jnp.maximum(-ahead - 1, 0), ahead < 0]).astype(F32)
    gated, convolved = kernel_call(
        functools.partial(convolve_kernel, tokens, len(arrived)),
        (
            jax.ShapeDtypeStruct((tokens, wide), BF16),
            jax.ShapeDtypeStruct((tokens + 2, tall, LANES), F32),
        ),
        [SMEM] + [VMEM] * (3 + len(arrived)),
        [pltpu.VMEM((tokens * tall, LANES), F32)],
        flops=64 * tokens * wide,
        moved=8 * tokens * 3 * wide,
    )(distance, rates, weights, mixed, *arrived)

    blocks = jnp.stack([gated] + [swapped(gated, "ctx", 2 * k) for k in range(1, n_pair)])
    kept = lax.dynamic_slice_in_dim(blocks, core * n_line, n_line, 0)
    given = lax.dynamic_slice_in_dim(blocks, (1 - core) * n_line, n_line, 0)
    route = []
    for f in range(n_fsdp):
        for p in range(n_pair):
            for x in range(2):
                target = p ^ ((f % 2) * n_line + f // 2)
                route.append((f * n_ctx + 2 * p + x, p * n_ctx + 2 * target + x))

    def project(columns_here):
        product = functools.partial(
            lax.dot_general,
            dimension_numbers=(((2,), (0,)), ((), ())),
            preferred_element_type=F32,
        )
        sent = swapped(product(given, columns_here).astype(BF16), "fsdp", 1)
        summed = product(kept, columns_here) + sent.astype(F32)
        total = lax.dynamic_index_in_dim(summed, line, 0, False)
        for m in range(1, n_line):
            block = lax.dynamic_index_in_dim(summed, line ^ m, 0, False).astype(BF16)
            total = total + swapped(block, "fsdp", 2 * m).astype(F32)
        return lax.ppermute(total.astype(BF16), ("fsdp", "ctx"), route)

    out_mine, out_other = project(w_out), project(w_other)
    block_output = jnp.where(
        side == 0,
        jnp.concatenate([out_mine, out_other], axis=1),
        jnp.concatenate([out_other, out_mine], axis=1),
    )

    def pull(rows):
        contract = (((1,), (1,)), ((), ()))
        return lax.dot_general(
            rows[:, :width], w_out, contract, preferred_element_type=F32
        ) + lax.dot_general(rows[:, width:], w_other, contract, preferred_element_type=F32)

    terms = []
    for k in range(1, n_pair):
        term = jnp.concatenate([pull(near[k]), pull(far[k])], axis=0).astype(BF16)
        terms.append(swapped(term, "ctx", 2 * k))
    mine, other = columns(grad_out, pair)
    rest = lax.dynamic_slice_in_dim(grad_out, (1 - core) * half, half, 0)
    here = jnp.concatenate([own_rows, rest], axis=0)
    own = pull(jnp.concatenate(columns(here, pair), axis=1))
    grads, back_state, head = kernel_call(
        functools.partial(back_state_kernel, tokens, len(terms)),
        (
            jax.ShapeDtypeStruct((tokens * tall, LANES), F32),
            state_shape,
            jax.ShapeDtypeStruct((2, tall, LANES), F32),
        ),
        [SMEM] + [VMEM] * (3 + len(terms)),
        flops=40 * tokens * wide,
        moved=8 * tokens * 3 * wide,
    )(core[None].astype(jnp.int32), rates, mixed, own, *terms)
    back_arrived = [swapped(back_state, "ctx", k) for k in masks]
    following = shifted(head, "ctx", -1)
    out = kernel_call(
        functools.partial(adjoint_kernel, tokens, len(back_arrived)),
        (jax.ShapeDtypeStruct((tokens, 3, tall, LANES), F32),),
        [SMEM] + [VMEM] * (7 + len(back_arrived)),
        flops=80 * tokens * wide,
        moved=8 * tokens * 3 * wide,
    )(
        back_distance, rates, weights, taps, mixed, convolved, grads, following, *back_arrived
    )[0]
    grad_features = out.reshape(tokens, 3, wide).astype(BF16)
    return (block_output, grad_features)


def solution(mesh):
    placed = (
        P("ctx", None, "fsdp"),
        P(None, None, "fsdp"),
        P("fsdp", None),
        P("fsdp", None),
        P("fsdp", "ctx"),
        P("ctx", None),
    )
    return jax.shard_map(
        per_device,
        mesh=mesh,
        in_specs=placed,
        out_specs=(P("ctx", "fsdp"), P("ctx", None, "fsdp")),
        check_vma=False,
    )
```

time: 645 us -> 163 us (0.25); the launches traced: 635 us -> 160 us
  waiting for transfers between devices: 469 us -> 54.1 us
  other arithmetic: 79.8 us -> 5.82 us
  starting transfers between devices: 17.7 us -> 58 us
  matrix products: 42.9 us -> 28 us
  between operations: 15.8 us -> 1.17 us
    all_gather x1 -> x0, waiting for transfers between devices: 259 us -> none  [per_device(): w_full = lax.all_gather(w_out, 'ctx', axis=1, tiled=True)]
    ppermute x12 -> x33, waiting for transfers between devices: 204 us -> 53.5 us  [the longest x31 53.5 us: swapped(): return lax.ppermute(block, axis, [(i, i ^ mask) for i in range(count)])]
    ppermute x12 -> x33, starting transfers between devices: 12.9 us -> 52 us  [the longest x31 40.3 us: swapped(): return lax.ppermute(block, axis, [(i, i ^ mask) for i in range(count)])]
    convert_element_type x19 -> x8, other arithmetic: 25 us -> 1.08 us  [the longest x2 0.84 us: project(): return lax.ppermute(total.astype(BF16), ('fsdp', 'ctx'), route)]
    sub x24 -> x0, other arithmetic: 22.6 us -> none  [the longest x16 11.4 us: add_mode(): return (totals[0] + scaled * denom_re, totals[1] - scaled * denom_im)]
    mul x84 -> x0, other arithmetic: 16.9 us -> none  [the longest x16 13.1 us: add_mode(): lax.dynamic_slice_in_dim(residues, mode_index, 1, 1)[:, 0]]
    dot_general x18, matrix products: 42.9 us -> 28 us  [the longest x7 16.5 us: pull(): lax.dot_general(rows[:, width:], w_other, contract, preferred_element_typ...]
    add x9 -> x0, other arithmetic: 8.16 us -> none  [the longest x1 3.28 us: per_device(): short_taps[0] * extended[2:] + short_taps[1] * extended[1:tokens_here + 1]]
  transfers between devices with their start and end apart: 16 -> 36, of which waited for: 10 -> 14; matrix products, arithmetic and copies ran while one was open for 14% -> 23% of each run, Pallas kernels for 0% -> 3%
where the time goes in v1:
time: 163 us; the launch traced here: 160 us
  starting transfers between devices  58 us (36%)
  waiting for transfers between devices  54.1 us (33%)
  matrix products  28 us (17%)
  local copies, waits for them, and re-layouts  6.43 us (4%)
  Pallas kernels  6.38 us (4%)
  other arithmetic  5.82 us (4%)
    ppermute x31, waiting for transfers between devices, swapped(): return lax.ppermute(block, axis, [(i, i ^ mask) for i in range(count)])  53.5 us
    ppermute x31, starting transfers between devices, swapped(): return lax.ppermute(block, axis, [(i, i ^ mask) for i in range(count)])  40.3 us
    dot_general x7, matrix products, pull(): lax.dot_general(rows[:, width:], w_other, contract, preferred_element_typ...  16.5 us
    ppermute x2, starting transfers between devices, project(): return lax.ppermute(total.astype(BF16), ('fsdp', 'ctx'), route)  11.7 us
    ppermute x3, starting transfers between devices, shifted(): return lax.ppermute(block, axis, route)  5.97 us
    dot_general x7, matrix products, pull(): lax.dot_general(rows[:, :width], w_out, contract, preferred_element_type=...  5.43 us
  transfers between devices with their start and end apart: 36, of which 14 were waited for; matrix products, arithmetic and copies ran while one was open for 23% of the time, Pallas kernels for 3%

profile of v1, /device:TPU:4, one launch (start us, length us, event | category | flops | bytes accessed | tf_op | source)
XLA Modules:
  0.0 159.9 jit_solution(11168842511108806594)
XLA Ops:
  1.6 3.4 %collective-permute-start = (bf16[2,3,1024]{2,0,1:T(2,128)(2,1)S(1)}, bf16[2,3,1024]{2,0,1:T(2,128)(2,1)S(1)}, u32[]{:S(2)}, u32[]{:S(2)}) collective-permute-start(bf16[2,3,1024]{2,0,1:T(2,128)(2,1)S(1)} %get-tuple-element.28), channel_id=1, source_target_pairs={{0,1},{1,2},{2,3},{3,4},{4,5},{5,6},{6,7},{8,9},{9,10},{10,11},{11... | collective-permute-start | bytes 36872 | tf_op jit(solution)/shard_map/ppermute | solution.py:25
  5.0 1.3 collective-permute-start.1
  6.4 1.8 %fusion.65 = (bf16[64,1024]{1,0:T(8,128)(2,1)S(1)}, bf16[64,1024]{1,0:T(8,128)(2,1)S(1)}, bf16[64,1024]{1,0:T(8,128)(2,1)S(1)}, bf16[64,1024]{1,0:T(8,128)(2,1)S...) fusion(bf16[128,8192]{1,0:T(8,128)(2,1)} %param.11, s32[]{:T(128)S(6)} %select_n.99, s32[]{:T(128)S(6)} %select_n.109, ...), kind=kLoop, calls=%fused_computation.88 | loop fusion | bytes 1572892 | tf_op jit(solution)/shard_map/dynamic_slice | solution.py:202
  10.7 1.0 shard_map.77
  11.7 2.5 %collective-permute-start.2 = (f32[16,8,128]{2,1,0:T(8,128)S(1)}, f32[16,8,128]{2,1,0:T(8,128)S(1)}, u32[]{:S(2)}, u32[]{:S(2)}) collective-permute-start(f32[16,8,128]{2,1,0:T(8,128)S(1)} %get-tuple-element.10), channel_id=1, source_target_pairs={{0,1},{1,0},{2,3},{3,2},{4,5},{5,4},{6,7},{7,6},{8,9},{9,8},{10,11... | collective-permute-start | bytes 196616 | tf_op jit(solution)/shard_map/ppermute | solution.py:19
  14.2 1.6 collective-permute-start.3
  16.3 3.0 %collective-permute-start.5 = (f32[16,8,128]{2,1,0:T(8,128)S(1)}, f32[16,8,128]{2,1,0:T(8,128)S(1)}, u32[]{:S(2)}, u32[]{:S(2)}) collective-permute-start(f32[16,8,128]{2,1,0:T(8,128)S(1)} %get-tuple-element.10), channel_id=1, source_target_pairs={{0,4},{1,5},{2,6},{3,7},{4,0},{5,1},{6,2},{7,3},{8,12},{9,13},{10,... | collective-permute-start | bytes 196616 | tf_op jit(solution)/shard_map/ppermute | solution.py:19
  20.1 3.2 %collective-permute-start.7 = (f32[16,8,128]{2,1,0:T(8,128)S(1)}, f32[16,8,128]{2,1,0:T(8,128)S(1)}, u32[]{:S(2)}, u32[]{:S(2)}) collective-permute-start(f32[16,8,128]{2,1,0:T(8,128)S(1)} %get-tuple-element.10), channel_id=1, source_target_pairs={{0,6},{1,7},{2,4},{3,5},{4,2},{5,3},{6,0},{7,1},{8,14},{9,15},{10,... | collective-permute-start | bytes 196616 | tf_op jit(solution)/shard_map/ppermute | solution.py:19
  23.3 0.9 collective-permute-start.8
  24.2 3.8 %collective-permute-start.25 = (bf16[64,2048]{1,0:T(8,128)(2,1)}, bf16[64,2048]{1,0:T(8,128)(2,1)S(1)}, u32[]{:S(2)}, u32[]{:S(2)}) collective-permute-start(bf16[64,2048]{1,0:T(8,128)(2,1)} %pad_maximum_fusion.5), channel_id=1, source_target_pairs={{0,6},{1,7},{2,4},{3,5},{4,2},{5,3},{6,0},{7,1},{8,14},{9,15},{10,... | collective-permute-start | bytes 786440 | tf_op jit(solution)/shard_map/ppermute | solution.py:19
  28.0 5.3 %collective-permute-done.5.refs_3_ = f32[16,8,128]{2,1,0:T(8,128)S(1)} collective-permute-done((f32[16,8,128]{2,1,0:T(8,128)S(1)}, f32[16,8,128]{2,1,0:T(8,128)S(1)}, u32[]{:S(2)}, u32[]{:S(2)}) %collective-permute-start.5) | collective-permute-done | bytes 65568 | tf_op jit(solution)/shard_map/ppermute | solution.py:19
  33.4 1.5 collective-permute-done.6.refs_4_
  34.9 2.2 %shard_map.78 = (bf16[128,1024]{1,0:T(8,128)(2,1)S(1)}, f32[130,8,128]{2,1,0:T(8,128)S(1)}) custom-call(f32[2,7]{1,0:T(2,128)S(1)} %add_convert_fusion.distance_ref, f32[16,8,128]{2,1,0:T(8,128)S(1)} %bitcast.62, f32[16,8,128]{2,1,0:T(8,128)S(1)} %bitcast.65, f32[130,3,8,128]{3,2,1,0:T(8,128)S(1)} %get-tuple-element.9.mixed_ref, ...), custom_call_target="tpu_custom_call" | custom-call | flops 8388608 | bytes 3145728 | tf_op jit(solution)/shard_map/pallas_call | solution.py:230
  37.1 3.4 %collective-permute-start.9 = (bf16[128,1024]{1,0:T(8,128)(2,1)S(1)}, bf16[128,1024]{1,0:T(8,128)(2,1)}, u32[]{:S(2)}, u32[]{:S(2)}) collective-permute-start(bf16[128,1024]{1,0:T(8,128)(2,1)S(1)} %get-tuple-element.11), channel_id=1, source_target_pairs={{0,2},{1,3},{2,0},{3,1},{4,6},{5,7},{6,4},{7,5},{8,10},{9,11},{10,... | collective-permute-start | bytes 786440 | tf_op jit(solution)/shard_map/ppermute | solution.py:19
  40.5 1.2 collective-permute-start.10
  41.7 1.4 collective-permute-start.11
  43.9 7.4 %collective-permute-done.9 = bf16[128,1024]{1,0:T(8,128)(2,1)} collective-permute-done((bf16[128,1024]{1,0:T(8,128)(2,1)S(1)}, bf16[128,1024]{1,0:T(8,128)(2,1)}, u32[]{:S(2)}, u32[]{:S(2)}) %collective-permute-start.9) | collective-permute-done | bytes 262176 | tf_op jit(solution)/shard_map/ppermute | solution.py:19
  51.2 15.2 %collective-permute-done.10 = bf16[128,1024]{1,0:T(8,128)(2,1)} collective-permute-done((bf16[128,1024]{1,0:T(8,128)(2,1)S(1)}, bf16[128,1024]{1,0:T(8,128)(2,1)}, u32[]{:S(2)}, u32[]{:S(2)}) %collective-permute-start.10) | collective-permute-done | bytes 262176 | tf_op jit(solution)/shard_map/ppermute | solution.py:19
  67.2 1.2 pad_maximum_fusion
  73.4 3.1 %collective-permute-done.22 = bf16[64,2048]{1,0:T(8,128)(2,1)S(1)} collective-permute-done((bf16[64,2048]{1,0:T(8,128)(2,1)}, bf16[64,2048]{1,0:T(8,128)(2,1)S(1)}, u32[]{:S(2)}, u32[]{:S(2)}) %collective-permute-start.22) | collective-permute-done | bytes 262176 | tf_op jit(solution)/shard_map/ppermute | solution.py:19
  76.5 1.7 %collective-permute-done.19 = bf16[64,2048]{1,0:T(8,128)(2,1)S(1)} collective-permute-done((bf16[64,2048]{1,0:T(8,128)(2,1)S(1)}, bf16[64,2048]{1,0:T(8,128)(2,1)S(1)}, u32[]{:S(2)}, u32[]{:S(2)}) %collective-permute-start.19) | collective-permute-done | bytes 262176 | tf_op jit(solution)/shard_map/ppermute | solution.py:19
  78.3 2.1 %collective-permute-done.13 = bf16[128,1024]{1,0:T(8,128)(2,1)S(1)} collective-permute-done((bf16[128,1024]{1,0:T(8,128)(2,1)S(1)}, bf16[128,1024]{1,0:T(8,128)(2,1)S(1)}, u32[]{:S(2)}, u32[]{:S(2)}) %collective-permute-start.13) | collective-permute-done | bytes 262176 | tf_op jit(solution)/shard_map/ppermute | solution.py:19
  80.4 7.6 %collective-permute-start.14 = (bf16[128,1024]{1,0:T(8,128)(2,1)S(1)}, bf16[128,1024]{1,0:T(8,128)(2,1)S(1)}, u32[]{:S(2)}, u32[]{:S(2)}) collective-permute-start(bf16[128,1024]{1,0:T(8,128)(2,1)S(1)} %fusion.27), channel_id=1, source_target_pairs={{0,0},{1,1},{2,10},{3,11},{4,20},{5,21},{6,30},{7,31},{8,4},{9,5},... | collective-permute-start | bytes 786440 | tf_op jit(solution)/shard_map/ppermute | solution.py:264
  88.0 2.4 %fusion.42 = f32[64,1024]{1,0:T(8,128)S(1)} fusion(bf16[1024,1024]{1,0:T(8,128)(2,1)} %collective-permute-done.15, bf16[64,2048]{1,0:T(8,128)(2,1)S(1)} %collective-permute-done.25), kind=kOutput, calls=%fused_computation.56 | convolution fusion | flops 134217728 | bytes 2490368 | tf_op jit(solution)/shard_map/dot_general | solution.py:277
  90.4 2.4 %fusion.39 = f32[64,1024]{1,0:T(8,128)S(1)} fusion(bf16[1024,1024]{1,0:T(8,128)(2,1)} %collective-permute-done.15, bf16[64,2048]{1,0:T(8,128)(2,1)S(1)} %collective-permute-done.26), kind=kOutput, calls=%fused_computation.53 | convolution fusion | flops 134217728 | bytes 2490368 | tf_op jit(solution)/shard_map/dot_general | solution.py:277
  94.3 2.5 %collective-permute-start.27 = (bf16[128,1024]{1,0:T(8,128)(2,1)S(1)}, bf16[128,1024]{1,0:T(8,128)(2,1)S(1)}, u32[]{:S(2)}, u32[]{:S(2)}) collective-permute-start(bf16[128,1024]{1,0:T(8,128)(2,1)S(1)} %pad_maximum_fusion.6), channel_id=1, source_target_pairs={{0,6},{1,7},{2,4},{3,5},{4,2},{5,3},{6,0},{7,1},{8,14},{9,15},{10,... | collective-permute-start | bytes 786440 | tf_op jit(solution)/shard_map/ppermute | solution.py:19
  96.8 2.3 %fusion.48 = f32[64,1024]{1,0:T(8,128)S(1)} fusion(bf16[1024,1024]{1,0:T(8,128)(2,1)} %collective-permute-done.15, bf16[64,2048]{1,0:T(8,128)(2,1)S(1)} %collective-permute-done.22), kind=kOutput, calls=%fused_computation.62 | convolution fusion | flops 134217728 | bytes 2490368 | tf_op jit(solution)/shard_map/dot_general | solution.py:277
  99.2 2.3 %fusion.45 = f32[64,1024]{1,0:T(8,128)S(1)} fusion(bf16[1024,1024]{1,0:T(8,128)(2,1)} %collective-permute-done.15, bf16[64,2048]{1,0:T(8,128)(2,1)S(1)} %collective-permute-done.23), kind=kOutput, calls=%fused_computation.59 | convolution fusion | flops 134217728 | bytes 2490368 | tf_op jit(solution)/shard_map/dot_general | solution.py:277
  103.1 2.3 %fusion.17 = bf16[2,128,1024]{2,1,0:T(8,128)(2,1)S(1)} fusion(bf16[1024,1024]{1,0:T(8,128)(2,1)} %collective-permute-done.15, bf16[4,128,1024]{2,1,0:T(8,128)(2,1)S(1)} %pad_maximum_fusion, s32[]{:T(128)S(6)} %select_n.89), kind=kOutput, calls=%fused_computation.15 | convolution fusion | flops 537133056 | bytes 3145732 | tf_op jit(solution)/shard_map/dot_general | solution.py:258
  105.6 2.3 %fusion.51 = f32[64,1024]{1,0:T(8,128)S(1)} fusion(bf16[1024,1024]{1,0:T(8,128)(2,1)} %collective-permute-done.15, bf16[64,2048]{1,0:T(8,128)(2,1)S(1)} %collective-permute-done.20), kind=kOutput, calls=%fused_computation.65 | convolution fusion | flops 134217728 | bytes 2490368 | tf_op jit(solution)/shard_map/dot_general | solution.py:277
  108.7 2.4 %fusion.54 = f32[64,1024]{1,0:T(8,128)S(1)} fusion(bf16[1024,1024]{1,0:T(8,128)(2,1)} %collective-permute-done.15, bf16[64,2048]{1,0:T(8,128)(2,1)S(1)} %collective-permute-done.19), kind=kOutput, calls=%fused_computation.68 | convolution fusion | flops 134217728 | bytes 2490368 | tf_op jit(solution)/shard_map/dot_general | solution.py:277
  111.8 2.0 %collective-permute-start.21 = (bf16[128,1024]{1,0:T(8,128)(2,1)S(1)}, bf16[128,1024]{1,0:T(8,128)(2,1)S(1)}, u32[]{:S(2)}, u32[]{:S(2)}) collective-permute-start(bf16[128,1024]{1,0:T(8,128)(2,1)S(1)} %pad_maximum_fusion.2), channel_id=1, source_target_pairs={{0,2},{1,3},{2,0},{3,1},{4,6},{5,7},{6,4},{7,5},{8,10},{9,11},{10,... | collective-permute-start | bytes 786440 | tf_op jit(solution)/shard_map/ppermute | solution.py:19
  113.8 2.3 %fusion.11 = f32[2,128,1024]{2,1,0:T(8,128)S(1)} fusion(bf16[1024,1024]{1,0:T(8,128)(2,1)} %collective-permute-done.15, bf16[2,128,1024]{2,1,0:T(8,128)(2,1)S(1)} %collective-permute-done.16, bf16[4,128,1024]{2,1,0:T(8,128)(2,1)S(1)} %pad_maximum_fusion, s32[]{:T(128)S(6)} %select_n.88), kind=kOutput, calls=%fused_computation.13 | convolution fusion | flops 537395200 | bytes 4194308 | tf_op jit(solution)/shard_map/dot_general | solution.py:259
  116.2 2.2 %collective-permute-start.17 = (bf16[128,1024]{1,0:T(8,128)(2,1)S(1)}, bf16[128,1024]{1,0:T(8,128)(2,1)S(1)}, u32[]{:S(2)}, u32[]{:S(2)}) collective-permute-start(bf16[128,1024]{1,0:T(8,128)(2,1)S(1)} %fusion.38), channel_id=1, source_target_pairs={{0,16},{8,24},{16,0},{24,8},{1,17},{9,25},{17,1},{25,9},{2,18},{10... | collective-permute-start | bytes 786440 | tf_op jit(solution)/shard_map/ppermute | solution.py:19
  118.3 2.4 %convolution_add_fusion.refs_0_ = f32[128,1024]{1,0:T(8,128)S(1)} fusion(f32[128,1024]{1,0:T(8,128)S(1)} %fusion.35, bf16[1024,1024]{1,0:T(8,128)(2,1)} %collective-permute-done.15, s32[]{:T(128)S(6)} %select_n.98, bf16[64,8192]{1,0:T(8,128)(2,1)S(1)} %get-tuple-element.27, bf16[64,8192]{1,0:T(8,128)(2,1)S(1)} %get-tuple-element.26), kind=kOutput, calls=%fused_computation.16 | convolution fusion | flops 269090816 | bytes 5242884 | tf_op jit(solution)/shard_map/dot_general | solution.py:277
  120.8 3.6 %collective-permute-done.21.refs_1_ = bf16[128,1024]{1,0:T(8,128)(2,1)S(1)} collective-permute-done((bf16[128,1024]{1,0:T(8,128)(2,1)S(1)}, bf16[128,1024]{1,0:T(8,128)(2,1)S(1)}, u32[]{:S(2)}, u32[]{:S(2)}) %collective-permute-start.21) | collective-permute-done | bytes 262176 | tf_op jit(solution)/shard_map/ppermute | solution.py:19
  125.2 1.2 collective-permute-start.29
  126.5 1.3 collective-permute-start.28
  128.5 4.1 %collective-permute-start.18 = (bf16[128,1024]{1,0:T(8,128)(2,1)}, bf16[128,1024]{1,0:T(8,128)(2,1)}, u32[]{:S(2)}, u32[]{:S(2)}) collective-permute-start(bf16[128,1024]{1,0:T(8,128)(2,1)} %fusion.26), channel_id=1, source_target_pairs={{0,0},{1,1},{2,10},{3,11},{4,20},{5,21},{6,30},{7,31},{8,4},{9,5},... | collective-permute-start | bytes 786440 | tf_op jit(solution)/shard_map/ppermute | solution.py:264
  133.5 1.2 collective-permute-start.31
  134.6 1.1 collective-permute-start.32
  135.7 8.3 %collective-permute-done.30.refs_1_ = f32[16,8,128]{2,1,0:T(8,128)S(1)} collective-permute-done((f32[16,8,128]{2,1,0:T(8,128)S(1)}, f32[16,8,128]{2,1,0:T(8,128)S(1)}, u32[]{:S(2)}, u32[]{:S(2)}) %collective-permute-start.30) | collective-permute-done | bytes 65568 | tf_op jit(solution)/shard_map/ppermute | solution.py:19
  144.1 2.5 %collective-permute-start.34 = (f32[16,8,128]{2,1,0:T(8,128)S(1)}, f32[16,8,128]{2,1,0:T(8,128)S(1)}, u32[]{:S(2)}, u32[]{:S(2)}) collective-permute-start(f32[16,8,128]{2,1,0:T(8,128)S(1)} %get-tuple-element.15), channel_id=1, source_target_pairs={{0,6},{1,7},{2,4},{3,5},{4,2},{5,3},{6,0},{7,1},{8,14},{9,15},{10,... | collective-permute-start | bytes 196616 | tf_op jit(solution)/shard_map/ppermute | solution.py:19
  146.6 2.9 %collective-permute-start.35 = (f32[16,8,128]{2,1,0:T(8,128)S(1)}, f32[16,8,128]{2,1,0:T(8,128)S(1)}, u32[]{:S(2)}, u32[]{:S(2)}) collective-permute-start(f32[16,8,128]{2,1,0:T(8,128)S(1)} %get-tuple-element.15), channel_id=1, source_target_pairs={{0,7},{1,6},{2,5},{3,4},{4,3},{5,2},{6,1},{7,0},{8,15},{9,14},{10,... | collective-permute-start | bytes 196616 | tf_op jit(solution)/shard_map/ppermute | solution.py:19
  150.6 3.1 %collective-permute-done.35.refs_6_ = f32[16,8,128]{2,1,0:T(8,128)S(1)} collective-permute-done((f32[16,8,128]{2,1,0:T(8,128)S(1)}, f32[16,8,128]{2,1,0:T(8,128)S(1)}, u32[]{:S(2)}, u32[]{:S(2)}) %collective-permute-start.35) | collective-permute-done | bytes 65568 | tf_op jit(solution)/shard_map/ppermute | solution.py:19
  153.7 2.4 %shard_map.80 = f32[128,3,8,128]{3,2,1,0:T(8,128)S(1)} custom-call(f32[2,7]{1,0:T(2,128)S(1)} %add_convert_fusion.1.distance_ref, f32[16,8,128]{2,1,0:T(8,128)S(1)} %bitcast.64, f32[16,8,128]{2,1,0:T(8,128)S(1)} %bitcast.66, f32[3,3,8,128]{3,2,1,0:T(8,128)S(1)} %reshape.66.taps_ref, f32[130,3,8,128]{3,2,1,0:T(8,128)S(1)} %get-tuple-element.9.mixed_ref, ...), custom_call_target="tpu_custom_call" | custom-call | flops 10485760 | bytes 3145728 | tf_op jit(solution)/shard_map/pallas_call | solution.py:300
  156.8 1.2 copy.17
  158.0 2.0 %maximum_select_fusion = bf16[128,2048]{1,0:T(8,128)(2,1)} fusion(bf16[128,1024]{1,0:T(8,128)(2,1)} %collective-permute-done.18, bf16[128,1024]{1,0:T(8,128)(2,1)S(1)} %collective-permute-done.14, pred[]{:T(512)S(6)} %eq.6), kind=kLoop, calls=%fused_computation.31 | loop fusion | flops 2359296 | bytes 1048577 | tf_op jit(solution)/shard_map/jit(_where)/select_n | solution.py:267
  (90 shorter events, 20.2 us)
Async XLA Ops:
  0.6 8.3 %copy-start.2 = (bf16[128,3,1024]{2,0,1:T(8,128)(2,1)S(1)}, bf16[128,3,1024]{2,0,1:T(8,128)(2,1)}, u32[]{:S(2)}) copy-start(bf16[128,3,1024]{2,0,1:T(8,128)(2,1)} %param.6) | copy-start | bytes 2359300
  0.6 8.7 %copy-start.3 = (f32[1024,16]{0,1:T(8,128)S(1)}, f32[1024,16]{0,1:T(8,128)}, u32[]{:S(2)}) copy-start(f32[1024,16]{0,1:T(8,128)} %param.9) | copy-start | bytes 196612
  1.6 8.3 %collective-permute-start = (bf16[2,3,1024]{2,0,1:T(2,128)(2,1)S(1)}, bf16[2,3,1024]{2,0,1:T(2,128)(2,1)S(1)}, u32[]{:S(2)}, u32[]{:S(2)}) collective-permute-start(bf16[2,3,1024]{2,0,1:T(2,128)(2,1)S(1)} %get-tuple-element.28), channel_id=1, source_target_pairs={{0,1},{1,2},{2,3},{3,4},{4,5},{5,6},{6,7},{8,9},{9,10},{10,11},{11... | collective-permute-start | bytes 36872 | tf_op jit(solution)/shard_map/ppermute | solution.py:25
  5.0 5.6 %collective-permute-start.1 = (bf16[2,3,1024]{2,0,1:T(2,128)(2,1)S(1)}, bf16[2,3,1024]{2,0,1:T(2,128)(2,1)S(1)}, u32[]{:S(2)}, u32[]{:S(2)}) collective-permute-start(bf16[2,3,1024]{2,0,1:T(2,128)(2,1)S(1)} %get-tuple-element.29), channel_id=1, source_target_pairs={{1,0},{2,1},{3,2},{4,3},{5,4},{6,5},{7,6},{9,8},{10,9},{11,10},{12... | collective-permute-start | bytes 36872 | tf_op jit(solution)/shard_map/ppermute | solution.py:25
  8.2 1.6 %copy-start.5 = (f32[3,3,1024]{2,1,0:T(4,128)S(1)}, f32[3,3,1024]{2,1,0:T(4,128)}, u32[]{:S(2)}) copy-start(f32[3,3,1024]{2,1,0:T(4,128)} %param.7) | copy-start | bytes 110596
  8.2 1.7 %copy-start.4 = (f32[1024,16]{0,1:T(8,128)S(1)}, f32[1024,16]{0,1:T(8,128)}, u32[]{:S(2)}) copy-start(f32[1024,16]{0,1:T(8,128)} %param.8) | copy-start | bytes 196612
  11.7 8.4 %collective-permute-start.2 = (f32[16,8,128]{2,1,0:T(8,128)S(1)}, f32[16,8,128]{2,1,0:T(8,128)S(1)}, u32[]{:S(2)}, u32[]{:S(2)}) collective-permute-start(f32[16,8,128]{2,1,0:T(8,128)S(1)} %get-tuple-element.10), channel_id=1, source_target_pairs={{0,1},{1,0},{2,3},{3,2},{4,5},{5,4},{6,7},{7,6},{8,9},{9,8},{10,11... | collective-permute-start | bytes 196616 | tf_op jit(solution)/shard_map/ppermute | solution.py:19
  14.2 9.1 %collective-permute-start.3 = (f32[16,8,128]{2,1,0:T(8,128)S(1)}, f32[16,8,128]{2,1,0:T(8,128)S(1)}, u32[]{:S(2)}, u32[]{:S(2)}) collective-permute-start(f32[16,8,128]{2,1,0:T(8,128)S(1)} %get-tuple-element.10), channel_id=1, source_target_pairs={{0,2},{1,3},{2,0},{3,1},{4,6},{5,7},{6,4},{7,5},{8,10},{9,11},{10,... | collective-permute-start | bytes 196616 | tf_op jit(solution)/shard_map/ppermute | solution.py:19
  15.8 8.4 %collective-permute-start.4 = (f32[16,8,128]{2,1,0:T(8,128)S(1)}, f32[16,8,128]{2,1,0:T(8,128)S(1)}, u32[]{:S(2)}, u32[]{:S(2)}) collective-permute-start(f32[16,8,128]{2,1,0:T(8,128)S(1)} %get-tuple-element.10), channel_id=1, source_target_pairs={{0,3},{1,2},{2,1},{3,0},{4,7},{5,6},{6,5},{7,4},{8,11},{9,10},{10,... | collective-permute-start | bytes 196616 | tf_op jit(solution)/shard_map/ppermute | solution.py:19
  16.3 17.0 %collective-permute-start.5 = (f32[16,8,128]{2,1,0:T(8,128)S(1)}, f32[16,8,128]{2,1,0:T(8,128)S(1)}, u32[]{:S(2)}, u32[]{:S(2)}) collective-permute-start(f32[16,8,128]{2,1,0:T(8,128)S(1)} %get-tuple-element.10), channel_id=1, source_target_pairs={{0,4},{1,5},{2,6},{3,7},{4,0},{5,1},{6,2},{7,3},{8,12},{9,13},{10,... | collective-permute-start | bytes 196616 | tf_op jit(solution)/shard_map/ppermute | solution.py:19
  19.3 15.6 %collective-permute-start.6 = (f32[16,8,128]{2,1,0:T(8,128)S(1)}, f32[16,8,128]{2,1,0:T(8,128)S(1)}, u32[]{:S(2)}, u32[]{:S(2)}) collective-permute-start(f32[16,8,128]{2,1,0:T(8,128)S(1)} %get-tuple-element.10), channel_id=1, source_target_pairs={{0,5},{1,4},{2,7},{3,6},{4,1},{5,0},{6,3},{7,2},{8,13},{9,12},{10,... | collective-permute-start | bytes 196616 | tf_op jit(solution)/shard_map/ppermute | solution.py:19
  20.1 14.8 %collective-permute-start.7 = (f32[16,8,128]{2,1,0:T(8,128)S(1)}, f32[16,8,128]{2,1,0:T(8,128)S(1)}, u32[]{:S(2)}, u32[]{:S(2)}) collective-permute-start(f32[16,8,128]{2,1,0:T(8,128)S(1)} %get-tuple-element.10), channel_id=1, source_target_pairs={{0,6},{1,7},{2,4},{3,5},{4,2},{5,3},{6,0},{7,1},{8,14},{9,15},{10,... | collective-permute-start | bytes 196616 | tf_op jit(solution)/shard_map/ppermute | solution.py:19
  23.3 11.6 %collective-permute-start.8 = (f32[16,8,128]{2,1,0:T(8,128)S(1)}, f32[16,8,128]{2,1,0:T(8,128)S(1)}, u32[]{:S(2)}, u32[]{:S(2)}) collective-permute-start(f32[16,8,128]{2,1,0:T(8,128)S(1)} %get-tuple-element.10), channel_id=1, source_target_pairs={{0,7},{1,6},{2,5},{3,4},{4,3},{5,2},{6,1},{7,0},{8,15},{9,14},{10,... | collective-permute-start | bytes 196616 | tf_op jit(solution)/shard_map/ppermute | solution.py:19
  24.2 49.1 %collective-permute-start.25 = (bf16[64,2048]{1,0:T(8,128)(2,1)}, bf16[64,2048]{1,0:T(8,128)(2,1)S(1)}, u32[]{:S(2)}, u32[]{:S(2)}) collective-permute-start(bf16[64,2048]{1,0:T(8,128)(2,1)} %pad_maximum_fusion.5), channel_id=1, source_target_pairs={{0,6},{1,7},{2,4},{3,5},{4,2},{5,3},{6,0},{7,1},{8,14},{9,15},{10,... | collective-permute-start | bytes 786440 | tf_op jit(solution)/shard_map/ppermute | solution.py:19
  33.4 54.6 %collective-permute-start.15 = (bf16[1024,1024]{1,0:T(8,128)(2,1)}, bf16[1024,1024]{1,0:T(8,128)(2,1)}, u32[]{:S(2)}, u32[]{:S(2)}) collective-permute-start(bf16[1024,1024]{1,0:T(8,128)(2,1)} %param.10), channel_id=1, source_target_pairs={{0,1},{1,0},{2,3},{3,2},{4,5},{5,4},{6,7},{7,6},{8,9},{9,8},{10,11... | collective-permute-start | bytes 6291464 | tf_op jit(solution)/shard_map/ppermute | solution.py:19
  37.1 14.2 %collective-permute-start.9 = (bf16[128,1024]{1,0:T(8,128)(2,1)S(1)}, bf16[128,1024]{1,0:T(8,128)(2,1)}, u32[]{:S(2)}, u32[]{:S(2)}) collective-permute-start(bf16[128,1024]{1,0:T(8,128)(2,1)S(1)} %get-tuple-element.11), channel_id=1, source_target_pairs={{0,2},{1,3},{2,0},{3,1},{4,6},{5,7},{6,4},{7,5},{8,10},{9,11},{10,... | collective-permute-start | bytes 786440 | tf_op jit(solution)/shard_map/ppermute | solution.py:19
  40.5 26.0 %collective-permute-start.10 = (bf16[128,1024]{1,0:T(8,128)(2,1)S(1)}, bf16[128,1024]{1,0:T(8,128)(2,1)}, u32[]{:S(2)}, u32[]{:S(2)}) collective-permute-start(bf16[128,1024]{1,0:T(8,128)(2,1)S(1)} %get-tuple-element.11), channel_id=1, source_target_pairs={{0,4},{1,5},{2,6},{3,7},{4,0},{5,1},{6,2},{7,3},{8,12},{9,13},{10,... | collective-permute-start | bytes 786440 | tf_op jit(solution)/shard_map/ppermute | solution.py:19
  41.7 25.5 %collective-permute-start.11 = (bf16[128,1024]{1,0:T(8,128)(2,1)S(1)}, bf16[128,1024]{1,0:T(8,128)(2,1)}, u32[]{:S(2)}, u32[]{:S(2)}) collective-permute-start(bf16[128,1024]{1,0:T(8,128)(2,1)S(1)} %get-tuple-element.11), channel_id=1, source_target_pairs={{0,6},{1,7},{2,4},{3,5},{4,2},{5,3},{6,0},{7,1},{8,14},{9,15},{10,... | collective-permute-start | bytes 786440 | tf_op jit(solution)/shard_map/ppermute | solution.py:19
  43.8 24.6 %copy-start = (bf16[1024,1024]{1,0:T(8,128)(2,1)S(1)}, bf16[1024,1024]{1,0:T(8,128)(2,1)}, u32[]{:S(2)}) copy-start(bf16[1024,1024]{1,0:T(8,128)(2,1)} %param.10) | copy-start | bytes 6291460
  51.2 25.3 %collective-permute-start.22 = (bf16[64,2048]{1,0:T(8,128)(2,1)}, bf16[64,2048]{1,0:T(8,128)(2,1)S(1)}, u32[]{:S(2)}, u32[]{:S(2)}) collective-permute-start(bf16[64,2048]{1,0:T(8,128)(2,1)} %pad_maximum_fusion.3), channel_id=1, source_target_pairs={{0,4},{1,5},{2,6},{3,7},{4,0},{5,1},{6,2},{7,3},{8,12},{9,13},{10,... | collective-permute-start | bytes 786440 | tf_op jit(solution)/shard_map/ppermute | solution.py:19
  66.5 11.8 %collective-permute-start.19 = (bf16[64,2048]{1,0:T(8,128)(2,1)S(1)}, bf16[64,2048]{1,0:T(8,128)(2,1)S(1)}, u32[]{:S(2)}, u32[]{:S(2)}) collective-permute-start(bf16[64,2048]{1,0:T(8,128)(2,1)S(1)} %pad_maximum_fusion.1), channel_id=1, source_target_pairs={{0,2},{1,3},{2,0},{3,1},{4,6},{5,7},{6,4},{7,5},{8,10},{9,11},{10,... | collective-permute-start | bytes 786440 | tf_op jit(solution)/shard_map/ppermute | solution.py:19
  68.4 1.6 copy-start.1
  69.2 2.0 %collective-permute-start.12 = (bf16[2,128,1024]{2,1,0:T(8,128)(2,1)S(1)}, bf16[2,128,1024]{2,1,0:T(8,128)(2,1)S(1)}, u32[]{:S(2)}, u32[]{:S(2)}) collective-permute-start(bf16[2,128,1024]{2,1,0:T(8,128)(2,1)S(1)} %fusion.14), channel_id=1, source_target_pairs={{0,8},{8,0},{16,24},{24,16},{1,9},{9,1},{17,25},{25,17},{2,10},{10... | collective-permute-start | bytes 1572872 | tf_op jit(solution)/shard_map/ppermute | solution.py:19
  71.9 8.4 %collective-permute-start.13 = (bf16[128,1024]{1,0:T(8,128)(2,1)S(1)}, bf16[128,1024]{1,0:T(8,128)(2,1)S(1)}, u32[]{:S(2)}, u32[]{:S(2)}) collective-permute-start(bf16[128,1024]{1,0:T(8,128)(2,1)S(1)} %fusion.37), channel_id=1, source_target_pairs={{0,16},{8,24},{16,0},{24,8},{1,17},{9,25},{17,1},{25,9},{2,18},{10... | collective-permute-start | bytes 786440 | tf_op jit(solution)/shard_map/ppermute | solution.py:19
  73.3 17.0 %collective-permute-start.26 = (bf16[64,2048]{1,0:T(8,128)(2,1)S(1)}, bf16[64,2048]{1,0:T(8,128)(2,1)S(1)}, u32[]{:S(2)}, u32[]{:S(2)}) collective-permute-start(bf16[64,2048]{1,0:T(8,128)(2,1)S(1)} %collective-permute-done.25), channel_id=1, source_target_pairs={{0,8},{8,0},{16,24},{24,16},{1,9},{9,1},{17,25},{25,17},{2,10},{10... | collective-permute-start | bytes 786440 | tf_op jit(solution)/shard_map/ppermute | solution.py:19
  76.5 22.6 %collective-permute-start.23 = (bf16[64,2048]{1,0:T(8,128)(2,1)S(1)}, bf16[64,2048]{1,0:T(8,128)(2,1)S(1)}, u32[]{:S(2)}, u32[]{:S(2)}) collective-permute-start(bf16[64,2048]{1,0:T(8,128)(2,1)S(1)} %collective-permute-done.22), channel_id=1, source_target_pairs={{0,8},{8,0},{16,24},{24,16},{1,9},{9,1},{17,25},{25,17},{2,10},{10... | collective-permute-start | bytes 786440 | tf_op jit(solution)/shard_map/ppermute | solution.py:19
  78.2 27.3 %collective-permute-start.20 = (bf16[64,2048]{1,0:T(8,128)(2,1)S(1)}, bf16[64,2048]{1,0:T(8,128)(2,1)S(1)}, u32[]{:S(2)}, u32[]{:S(2)}) collective-permute-start(bf16[64,2048]{1,0:T(8,128)(2,1)S(1)} %collective-permute-done.19), channel_id=1, source_target_pairs={{0,8},{8,0},{16,24},{24,16},{1,9},{9,1},{17,25},{25,17},{2,10},{10... | collective-permute-start | bytes 786440 | tf_op jit(solution)/shard_map/ppermute | solution.py:19
  80.4 77.6 %collective-permute-start.14 = (bf16[128,1024]{1,0:T(8,128)(2,1)S(1)}, bf16[128,1024]{1,0:T(8,128)(2,1)S(1)}, u32[]{:S(2)}, u32[]{:S(2)}) collective-permute-start(bf16[128,1024]{1,0:T(8,128)(2,1)S(1)} %fusion.27), channel_id=1, source_target_pairs={{0,0},{1,1},{2,10},{3,11},{4,20},{5,21},{6,30},{7,31},{8,4},{9,5},... | collective-permute-start | bytes 786440 | tf_op jit(solution)/shard_map/ppermute | solution.py:264
  94.3 26.5 %collective-permute-start.27 = (bf16[128,1024]{1,0:T(8,128)(2,1)S(1)}, bf16[128,1024]{1,0:T(8,128)(2,1)S(1)}, u32[]{:S(2)}, u32[]{:S(2)}) collective-permute-start(bf16[128,1024]{1,0:T(8,128)(2,1)S(1)} %pad_maximum_fusion.6), channel_id=1, source_target_pairs={{0,6},{1,7},{2,4},{3,5},{4,2},{5,3},{6,0},{7,1},{8,14},{9,15},{10,... | collective-permute-start | bytes 786440 | tf_op jit(solution)/shard_map/ppermute | solution.py:19
  103.1 17.7 %collective-permute-start.24 = (bf16[128,1024]{1,0:T(8,128)(2,1)S(1)}, bf16[128,1024]{1,0:T(8,128)(2,1)S(1)}, u32[]{:S(2)}, u32[]{:S(2)}) collective-permute-start(bf16[128,1024]{1,0:T(8,128)(2,1)S(1)} %pad_maximum_fusion.4), channel_id=1, source_target_pairs={{0,4},{1,5},{2,6},{3,7},{4,0},{5,1},{6,2},{7,3},{8,12},{9,13},{10,... | collective-permute-start | bytes 786440 | tf_op jit(solution)/shard_map/ppermute | solution.py:19
  105.5 8.3 %collective-permute-start.16 = (bf16[2,128,1024]{2,1,0:T(8,128)(2,1)S(1)}, bf16[2,128,1024]{2,1,0:T(8,128)(2,1)S(1)}, u32[]{:S(2)}, u32[]{:S(2)}) collective-permute-start(bf16[2,128,1024]{2,1,0:T(8,128)(2,1)S(1)} %fusion.17), channel_id=1, source_target_pairs={{0,8},{8,0},{16,24},{24,16},{1,9},{9,1},{17,25},{25,17},{2,10},{10... | collective-permute-start | bytes 1572872 | tf_op jit(solution)/shard_map/ppermute | solution.py:19
  111.8 12.6 %collective-permute-start.21 = (bf16[128,1024]{1,0:T(8,128)(2,1)S(1)}, bf16[128,1024]{1,0:T(8,128)(2,1)S(1)}, u32[]{:S(2)}, u32[]{:S(2)}) collective-permute-start(bf16[128,1024]{1,0:T(8,128)(2,1)S(1)} %pad_maximum_fusion.2), channel_id=1, source_target_pairs={{0,2},{1,3},{2,0},{3,1},{4,6},{5,7},{6,4},{7,5},{8,10},{9,11},{10,... | collective-permute-start | bytes 786440 | tf_op jit(solution)/shard_map/ppermute | solution.py:19
  116.2 11.6 %collective-permute-start.17 = (bf16[128,1024]{1,0:T(8,128)(2,1)S(1)}, bf16[128,1024]{1,0:T(8,128)(2,1)S(1)}, u32[]{:S(2)}, u32[]{:S(2)}) collective-permute-start(bf16[128,1024]{1,0:T(8,128)(2,1)S(1)} %fusion.38), channel_id=1, source_target_pairs={{0,16},{8,24},{16,0},{24,8},{1,17},{9,25},{17,1},{25,9},{2,18},{10... | collective-permute-start | bytes 786440 | tf_op jit(solution)/shard_map/ppermute | solution.py:19
  125.2 9.4 %collective-permute-start.29 = (f32[16,8,128]{2,1,0:T(8,128)S(1)}, f32[16,8,128]{2,1,0:T(8,128)S(1)}, u32[]{:S(2)}, u32[]{:S(2)}) collective-permute-start(f32[16,8,128]{2,1,0:T(8,128)S(1)} %get-tuple-element.15), channel_id=1, source_target_pairs={{0,1},{1,0},{2,3},{3,2},{4,5},{5,4},{6,7},{7,6},{8,9},{9,8},{10,11... | collective-permute-start | bytes 196616 | tf_op jit(solution)/shard_map/ppermute | solution.py:19
  126.5 7.0 %collective-permute-start.28 = (f32[2,8,128]{2,1,0:T(8,128)S(1)}, f32[2,8,128]{2,1,0:T(8,128)S(1)}, u32[]{:S(2)}, u32[]{:S(2)}) collective-permute-start(f32[2,8,128]{2,1,0:T(8,128)S(1)} %get-tuple-element.14), channel_id=1, source_target_pairs={{1,0},{2,1},{3,2},{4,3},{5,4},{6,5},{7,6},{9,8},{10,9},{11,10},{12... | collective-permute-start | bytes 24584 | tf_op jit(solution)/shard_map/ppermute | solution.py:25
  128.5 29.4 %collective-permute-start.18 = (bf16[128,1024]{1,0:T(8,128)(2,1)}, bf16[128,1024]{1,0:T(8,128)(2,1)}, u32[]{:S(2)}, u32[]{:S(2)}) collective-permute-start(bf16[128,1024]{1,0:T(8,128)(2,1)} %fusion.26), channel_id=1, source_target_pairs={{0,0},{1,1},{2,10},{3,11},{4,20},{5,21},{6,30},{7,31},{8,4},{9,5},... | collective-permute-start | bytes 786440 | tf_op jit(solution)/shard_map/ppermute | solution.py:264
  132.6 11.4 %collective-permute-start.30 = (f32[16,8,128]{2,1,0:T(8,128)S(1)}, f32[16,8,128]{2,1,0:T(8,128)S(1)}, u32[]{:S(2)}, u32[]{:S(2)}) collective-permute-start(f32[16,8,128]{2,1,0:T(8,128)S(1)} %get-tuple-element.15), channel_id=1, source_target_pairs={{0,2},{1,3},{2,0},{3,1},{4,6},{5,7},{6,4},{7,5},{8,10},{9,11},{10,... | collective-permute-start | bytes 196616 | tf_op jit(solution)/shard_map/ppermute | solution.py:19
  133.5 10.6 %collective-permute-start.31 = (f32[16,8,128]{2,1,0:T(8,128)S(1)}, f32[16,8,128]{2,1,0:T(8,128)S(1)}, u32[]{:S(2)}, u32[]{:S(2)}) collective-permute-start(f32[16,8,128]{2,1,0:T(8,128)S(1)} %get-tuple-element.15), channel_id=1, source_target_pairs={{0,3},{1,2},{2,1},{3,0},{4,7},{5,6},{6,5},{7,4},{8,11},{9,10},{10,... | collective-permute-start | bytes 196616 | tf_op jit(solution)/shard_map/ppermute | solution.py:19
  134.6 12.0 %collective-permute-start.32 = (f32[16,8,128]{2,1,0:T(8,128)S(1)}, f32[16,8,128]{2,1,0:T(8,128)S(1)}, u32[]{:S(2)}, u32[]{:S(2)}) collective-permute-start(f32[16,8,128]{2,1,0:T(8,128)S(1)} %get-tuple-element.15), channel_id=1, source_target_pairs={{0,4},{1,5},{2,6},{3,7},{4,0},{5,1},{6,2},{7,3},{8,12},{9,13},{10,... | collective-permute-start | bytes 196616 | tf_op jit(solution)/shard_map/ppermute | solution.py:19
  144.1 6.2 %collective-permute-start.33 = (f32[16,8,128]{2,1,0:T(8,128)S(1)}, f32[16,8,128]{2,1,0:T(8,128)S(1)}, u32[]{:S(2)}, u32[]{:S(2)}) collective-permute-start(f32[16,8,128]{2,1,0:T(8,128)S(1)} %get-tuple-element.15), channel_id=1, source_target_pairs={{0,5},{1,4},{2,7},{3,6},{4,1},{5,0},{6,3},{7,2},{8,13},{9,12},{10,... | collective-permute-start | bytes 196616 | tf_op jit(solution)/shard_map/ppermute | solution.py:19
  144.1 6.6 %collective-permute-start.34 = (f32[16,8,128]{2,1,0:T(8,128)S(1)}, f32[16,8,128]{2,1,0:T(8,128)S(1)}, u32[]{:S(2)}, u32[]{:S(2)}) collective-permute-start(f32[16,8,128]{2,1,0:T(8,128)S(1)} %get-tuple-element.15), channel_id=1, source_target_pairs={{0,6},{1,7},{2,4},{3,5},{4,2},{5,3},{6,0},{7,1},{8,14},{9,15},{10,... | collective-permute-start | bytes 196616 | tf_op jit(solution)/shard_map/ppermute | solution.py:19
  146.6 7.1 %collective-permute-start.35 = (f32[16,8,128]{2,1,0:T(8,128)S(1)}, f32[16,8,128]{2,1,0:T(8,128)S(1)}, u32[]{:S(2)}, u32[]{:S(2)}) collective-permute-start(f32[16,8,128]{2,1,0:T(8,128)S(1)} %get-tuple-element.15), channel_id=1, source_target_pairs={{0,7},{1,6},{2,5},{3,4},{4,3},{5,2},{6,1},{7,0},{8,15},{9,14},{10,... | collective-permute-start | bytes 196616 | tf_op jit(solution)/shard_map/ppermute | solution.py:19

commit v2 on v1

v2 whole, which is shorter than its diff:
```python
import functools

import jax
import jax.numpy as jnp
from jax import lax
from jax.experimental import pallas as pl
from jax.experimental.pallas import tpu as pltpu
from jax.sharding import PartitionSpec as P

LANES = 128
F32 = jnp.float32
BF16 = jnp.bfloat16
VMEM = pl.BlockSpec(memory_space=pltpu.VMEM)
SMEM = pl.BlockSpec(memory_space=pltpu.SMEM)
HBM = pl.BlockSpec(memory_space=pltpu.HBM)
ANYWHERE = pl.BlockSpec(memory_space=pl.ANY)


def swapped(block, axis, mask):
    count = lax.axis_size(axis)
    return lax.ppermute(block, axis, [(i, i ^ mask) for i in range(count)])


def shifted(block, axis, distance):
    devices = range(lax.axis_size(axis))
    route = [(i - distance, i) for i in devices if i - distance in devices]
    return lax.ppermute(block, axis, route)


def tree_sum(terms):
    terms = list(terms)
    while len(terms) > 1:
        paired = [terms[i] + terms[i + 1] for i in range(0, len(terms) - 1, 2)]
        terms = paired + terms[len(terms) - len(terms) % 2 :]
    return terms[0]


def kernel_call(body, out_shape, in_specs, scratch_shapes=(), flops=0, moved=0):
    return pl.pallas_call(
        body,
        out_shape=out_shape,
        in_specs=in_specs,
        out_specs=jax.tree.map(lambda _: VMEM, out_shape),
        scratch_shapes=scratch_shapes,
        compiler_params=pltpu.CompilerParams(vmem_limit_bytes=48 * 1024 * 1024),
        cost_estimate=pl.CostEstimate(flops=flops, bytes_accessed=moved, transcendentals=0),
    )


def chunk_state_kernel(tokens, x_ref, before_ref, taps_ref, rates_ref, mixed_ref, state_ref):
    modes = rates_ref.shape[0]
    decays = [jnp.exp(-rates_ref[n]) for n in range(modes)]

    def mix(t, rows):
        parts = []
        for j in range(3):
            part = tree_sum([taps_ref[i, j] * rows[i][j] for i in range(3)])
            mixed_ref[t, j] = part
            parts.append(part)
        return parts[1] * parts[2]

    def absorb(states, carried):
        return tuple(decays[n] * states[n] + carried for n in range(modes))

    def step(t, states):
        return absorb(states, mix(t, [x_ref.at[t - i] for i in range(3)]))

    states = (jnp.zeros(state_ref.shape[1:], F32),) * modes
    states = absorb(states, mix(0, [x_ref.at[0], before_ref.at[1], before_ref.at[0]]))
    states = absorb(states, mix(1, [x_ref.at[1], x_ref.at[0], before_ref.at[1]]))
    states = lax.fori_loop(2, tokens, step, states, unroll=3)
    for n in range(modes):
        state_ref[n] = states[n]


def incoming(rates, arrived, reach_ref, n):
    terms = []
    for k, block in enumerate(arrived):
        terms.append(jnp.exp(-rates * reach_ref[0, k]) * reach_ref[1, k] * block[n])
    return tree_sum(terms)


def convolve_kernel(tokens, peers, reach_ref, rates_ref, residues_ref, mixed_ref, *refs):
    arrived, (gated_ref, convolved_ref, rows_ref) = refs[:peers], refs[peers:]
    modes, tall = rates_ref.shape[0], rates_ref.shape[1]
    decays = [jnp.exp(-rates_ref[n]) for n in range(modes)]
    weights = [residues_ref[n] * jnp.sqrt(rates_ref[n]) for n in range(modes)]
    states = tuple(incoming(rates_ref[n], arrived, reach_ref, n) for n in range(modes))

    def step(t, states):
        carried = mixed_ref[t, 1] * mixed_ref[t, 2]
        states = tuple(decays[n] * states[n] + carried for n in range(modes))
        convolved = tree_sum([weights[n] * states[n] for n in range(modes)])
        convolved_ref[t] = convolved
        rows_ref[pl.ds(pl.multiple_of(t * tall, tall), tall), :] = mixed_ref[t, 0] * convolved
        return states

    lax.fori_loop(0, tokens, step, states, unroll=4)
    for start in range(0, tokens, 16):
        for s in range(tall):
            rows = rows_ref[pl.ds(start * tall + s, 16, stride=tall), :]
            gated_ref[start : start + 16, s * LANES : (s + 1) * LANES] = rows.astype(BF16)


def back_state_kernel(tokens, peers, rates_ref, mixed_ref, convolved_ref, own_ref, *refs):
    sources, (grads_ref, state_ref, head_ref) = refs[:peers], refs[peers : peers + 3]
    terms, sems = refs[peers + 3 : -1], refs[-1]
    copies = []
    for k in range(peers):
        copies.append(pltpu.make_async_copy(sources[k], terms[k], sems.at[k]))
        copies[k].start()
    modes, tall = rates_ref.shape[0], rates_ref.shape[1]
    decays = [jnp.exp(-rates_ref[n]) for n in range(modes)]
    for copy in copies:
        copy.wait()
    for start in range(0, tokens, 16):
        for s in range(tall):
            lanes = slice(s * LANES, (s + 1) * LANES)
            parts = [term[start : start + 16, lanes].astype(F32) for term in terms]
            total = tree_sum([own_ref[start : start + 16, lanes]] + parts)
            grads_ref[pl.ds(start * tall + s, 16, stride=tall), :] = total

    def step(i, states):
        t = tokens - 1 - i
        here = grads_ref[pl.ds(pl.multiple_of(t * tall, tall), tall), :] * mixed_ref[t, 0]
        return tuple(decays[n] * states[n] + here for n in range(modes))

    empty = jnp.zeros(state_ref.shape[1:], F32)
    states = lax.fori_loop(0, tokens, step, (empty,) * modes, unroll=4)
    for n in range(modes):
        state_ref[n] = states[n]
    for t in range(2):
        head_ref[t, 0] = grads_ref[t * tall : (t + 1) * tall, :]
        head_ref[t, 1] = convolved_ref[t]
        for j in range(3):
            head_ref[t, 2 + j] = mixed_ref[t, j]


def adjoint_kernel(
    tokens, peers, reach_ref, rates_ref, residues_ref, taps_ref, mixed_ref, convolved_ref,
    grads_ref, after_ref, *refs
):
    arrived, (out_ref,) = refs[:peers], refs[peers:]
    modes, tall = rates_ref.shape[0], rates_ref.shape[1]
    decays = [jnp.exp(-rates_ref[n]) for n in range(modes)]
    weights = [residues_ref[n] * jnp.sqrt(rates_ref[n]) for n in range(modes)]

    def spread(grad, convolved, mixed, states):
        grad_carried = tree_sum([weights[n] * states[n] for n in range(modes)])
        return (grad * convolved, grad_carried * mixed[2], grad_carried * mixed[1])

    def spread_after(t, states):
        mixed = [after_ref[t, 2 + j] for j in range(3)]
        return spread(after_ref[t, 0], after_ref[t, 1], mixed, states)

    states = tuple(incoming(rates_ref[n], arrived, reach_ref, n) for n in range(modes))
    first = spread_after(0, states)
    beyond = after_ref[0, 0] * after_ref[0, 2]
    second = spread_after(
        1, tuple((states[n] - beyond) * jnp.exp(rates_ref[n]) for n in range(modes))
    )

    def step(i, carry):
        states, first, second = carry
        t = tokens - 1 - i
        grad = grads_ref[pl.ds(pl.multiple_of(t * tall, tall), tall), :]
        here = grad * mixed_ref[t, 0]
        states = tuple(decays[n] * states[n] + here for n in range(modes))
        mine = spread(grad, convolved_ref[t], mixed_ref.at[t], states)
        for j in range(3):
            out_ref[t, j] = (
                taps_ref[0, j] * mine[j] + taps_ref[1, j] * first[j] + taps_ref[2, j] * second[j]
            )
        return states, mine, first

    lax.fori_loop(0, tokens, step, (states, first, second), unroll=4)


def fetched(pairs, sems):
    copies = []
    for source, target in pairs:
        copies.append(pltpu.make_async_copy(source, target, sems.at[len(copies)]))
        copies[-1].start()
    return copies


def stacked(pieces, target):
    pairs, at = [], 0
    for piece in pieces:
        pairs.append((piece, target.at[pl.ds(at, piece.shape[0]), :]))
        at += piece.shape[0]
    return pairs


def product_kernel(n_pair, n_line, pieces, place_ref, own_src, mine_src, *refs):
    others, arrived = refs[:pieces], refs[pieces : pieces + 4]
    blocks, outs = refs[pieces + 4 : pieces + 4 + n_pair], refs[pieces + 4 + n_pair : -5]
    own_ref, other_ref, rows_ref, gated_ref, sems = refs[-5:]
    core, turn, side, pair = [place_ref[i] for i in range(4)]
    tokens, (wide, width) = mine_src.shape[0], own_src.shape
    part = tokens // 4
    columns = pl.ds(pl.multiple_of(pair * 2 * width, 2 * width), 2 * width)
    pairs = [(own_src, own_ref), (mine_src.at[:, columns], rows_ref.at[pl.ds(0, tokens), :])]
    turns = (2 * turn, 2 * (1 - turn), 2 * turn, 2 * (1 - turn))
    cores = (core, core, 1 - core, 1 - core)
    for k in range(1, n_pair):
        for block, up, across in zip(arrived, turns, cores):
            at = pl.multiple_of(k * tokens + (up + across) * part, part)
            source = block.at[pl.ds((k - 1) * part, part), :]
            pairs.append((source, rows_ref.at[pl.ds(at, part), :]))
    early, pairs = len(pairs), pairs + stacked(others, other_ref)
    middle, pairs = len(pairs), pairs + stacked(blocks, gated_ref)
    copies = fetched(pairs, sems)
    for copy in copies[:early]:
        copy.wait()
    contract = (((1,), (1,)), ((), ()))
    step = min(256, wide)
    halves = ((own_ref, side), (other_ref, 1 - side))
    for n in range(0, wide, step):
        parts = []
        for w_ref, at in halves:
            if n == 0 and w_ref is other_ref:
                for copy in copies[early:middle]:
                    copy.wait()
            rows = rows_ref[:, pl.ds(pl.multiple_of(at * width, width), width)]
            w = w_ref[n : n + step, :]
            parts.append(lax.dot_general(rows, w, contract, preferred_element_type=F32))
        total = parts[0] + parts[1]
        for k, out_ref in enumerate(outs[2:]):
            here = total[k * tokens : (k + 1) * tokens]
            out_ref[:, n : n + step] = here.astype(out_ref.dtype)
    for copy in copies[middle:]:
        copy.wait()
    step = min(256, width)
    tall = n_line * tokens
    for out_ref, half in ((outs[0], 1 - core), (outs[1], core)):
        rows = gated_ref[pl.ds(pl.multiple_of(half * tall, tall), tall), :]
        for w_ref, at in halves:
            for n in range(0, width, step):
                product = jnp.dot(rows, w_ref[:, n : n + step], preferred_element_type=F32)
                columns = pl.ds(pl.multiple_of(at * width + n, step), step)
                out_ref[:, columns] = product.astype(BF16)


def per_device(featurized, short_taps, residues, decay_rates, w_out, grad_out):
    tokens, _, wide = featurized.shape
    tall = wide // LANES
    modes = residues.shape[1]
    n_ctx, n_fsdp = lax.axis_size("ctx"), lax.axis_size("fsdp")
    me, group = lax.axis_index("ctx"), lax.axis_index("fsdp")
    pair, side = me // 2, me % 2
    core, line = group % 2, group // 2
    n_pair, n_line = n_ctx // 2, n_fsdp // 2
    width = w_out.shape[1]
    turn, part = line % 2, tokens // 4
    place = jnp.stack([core, turn, side, pair]).astype(jnp.int32)

    before = shifted(featurized[tokens - 2 :], "ctx", 1)

    near_cut = []
    for k in range(1, n_pair):
        at = ((2 * turn + core) * part, (pair ^ k) * 2 * width)
        block = lax.dynamic_slice(grad_out, at, (part, 2 * width))
        near_cut.append(block)

    def tiled(rows):
        return rows.astype(F32).reshape(-1, 3, tall, LANES)

    taps = tiled(short_taps)
    rates = decay_rates.T.reshape(modes, tall, LANES)
    weights = residues.T.reshape(modes, tall, LANES)
    state_shape = jax.ShapeDtypeStruct((modes, tall, LANES), F32)
    levels = range(n_ctx.bit_length() - 1)
    uppers = [(me >> b) % 2 for b in levels]
    belows = [me % (1 << b) for b in levels]

    def exchanged(total, later, others=()):
        arrived = []
        for b in levels:
            partner = swapped(total, "ctx", 1 << b)
            if others and b == 0:
                partner, others = lax.optimization_barrier((partner, others))
            arrived.append(partner)
            if b + 1 < len(levels):
                decay = jnp.exp(-rates * (tokens << b))
                fades = (uppers[b] == 0) == later
                total = jnp.where(fades, total * decay + partner, partner * decay + total)
        return (arrived, others) if others else arrived

    reach = jnp.stack([
        jnp.stack([below * tokens for below in belows]),
        jnp.stack([upper == 1 for upper in uppers]),
    ]).astype(F32)
    back_reach = jnp.stack([
        jnp.stack([((1 << b) - 1 - belows[b]) * tokens for b in levels]),
        jnp.stack([upper == 0 for upper in uppers]),
    ]).astype(F32)

    mixed, state = kernel_call(
        functools.partial(chunk_state_kernel, tokens),
        (jax.ShapeDtypeStruct((tokens, 3, tall, LANES), F32), state_shape),
        [VMEM] * 4,
        flops=50 * tokens * wide,
        moved=8 * tokens * 3 * wide,
    )(tiled(featurized), tiled(before), taps, rates)
    w_held, state = lax.optimization_barrier((w_out, state))
    arrived = exchanged(state, True)
    w_held, _ = lax.optimization_barrier((w_out, arrived[0]))
    w_other = [swapped(w_held, "ctx", 1)]
    near_cut, _ = lax.optimization_barrier((near_cut, arrived[2]))
    near = [swapped(block, "ctx", 2 * k) for k, block in enumerate(near_cut, 1)]
    gated, convolved = kernel_call(
        functools.partial(convolve_kernel, tokens, len(arrived)),
        (
            jax.ShapeDtypeStruct((tokens, wide), BF16),
            jax.ShapeDtypeStruct((tokens, tall, LANES), F32),
        ),
        [SMEM] + [VMEM] * (3 + len(arrived)),
        [pltpu.VMEM((tokens * tall, LANES), F32)],
        flops=64 * tokens * wide,
        moved=8 * tokens * 3 * wide,
    )(reach, rates, weights, mixed, *arrived)

    blocks = [gated] + [swapped(gated, "ctx", 2 * k) for k in range(1, n_pair)]
    near, _ = lax.optimization_barrier((near, gated))
    near = jnp.concatenate(near, axis=0)
    across = swapped(near, "fsdp", 2)
    far = [swapped(near, "fsdp", 1), swapped(across, "fsdp", 1)]

    route = []
    for f in range(n_fsdp):
        for p in range(n_pair):
            for x in range(2):
                target = p ^ ((f % 2) * n_line + f // 2)
                route.append((f * n_ctx + 2 * p + x, p * n_ctx + 2 * target + x))

    halved = jax.ShapeDtypeStruct((n_line * tokens, 2 * width), BF16)
    given, kept, *outs = kernel_call(
        functools.partial(product_kernel, n_pair, n_line, len(w_other)),
        (halved, halved, jax.ShapeDtypeStruct((tokens, wide), F32))
        + (jax.ShapeDtypeStruct((tokens, wide), BF16),) * (n_pair - 1),
        [SMEM] + [HBM] * (2 + len(w_other)) + [ANYWHERE] * (4 + n_pair),
        [
            pltpu.VMEM((wide, width), BF16),
            pltpu.VMEM((wide, width), BF16),
            pltpu.VMEM((n_pair * tokens, 2 * width), BF16),
            pltpu.VMEM((n_pair * tokens, wide), BF16),
            pltpu.SemaphoreType.DMA((2 + 4 * (n_pair - 1) + len(w_other) + n_pair,)),
        ],
        flops=8 * n_pair * tokens * wide * width,
        moved=8 * wide * width,
    )(place, w_out, grad_out, *w_other, near, across, *far, *blocks)
    terms = [outs[0]] + [swapped(outs[k], "ctx", 2 * k) for k in range(1, n_pair)]

    sent = swapped(given, "fsdp", 1).reshape(n_line, tokens, 2 * width)
    kept = kept.reshape(n_line, tokens, 2 * width)

    def summed(at):
        pieces = [lax.dynamic_index_in_dim(x, at, 0, False).astype(F32) for x in (kept, sent)]
        return pieces[0] + pieces[1]

    total = summed(line)
    rest = [summed(line ^ m).astype(BF16) for m in range(1, n_line)]
    gathered = []
    for at in (0, width):
        part = total[:, at : at + width]
        for m, block in enumerate(rest, 1):
            part = part + swapped(block[:, at : at + width], "fsdp", 2 * m).astype(F32)
        gathered.append(part.astype(BF16))
    terms, _ = lax.optimization_barrier((terms, gathered))
    placed = [lax.ppermute(part, ("fsdp", "ctx"), route) for part in gathered]

    grads, back_state, head = kernel_call(
        functools.partial(back_state_kernel, tokens, n_pair - 1),
        (
            jax.ShapeDtypeStruct((tokens * tall, LANES), F32),
            state_shape,
            jax.ShapeDtypeStruct((2, 5, tall, LANES), F32),
        ),
        [VMEM] * 4 + [ANYWHERE] * (n_pair - 1),
        [pltpu.VMEM((tokens, wide), BF16)] * (n_pair - 1)
        + [pltpu.SemaphoreType.DMA((n_pair - 1,))],
        flops=40 * tokens * wide,
        moved=8 * tokens * 3 * wide,
    )(rates, mixed, convolved, *terms)
    back_arrived, placed = exchanged(back_state, False, placed)
    block_output = jnp.concatenate(placed, axis=1)
    following = shifted(head, "ctx", -1)
    out = kernel_call(
        functools.partial(adjoint_kernel, tokens, len(back_arrived)),
        (jax.ShapeDtypeStruct((tokens, 3, tall, LANES), F32),),
        [SMEM] + [VMEM] * (7 + len(back_arrived)),
        flops=80 * tokens * wide,
        moved=8 * tokens * 3 * wide,
    )(back_reach, rates, weights, taps, mixed, convolved, grads, following, *back_arrived)[0]
    grad_features = out.reshape(tokens, 3, wide).astype(BF16)
    return (block_output, grad_features)


def solution(mesh):
    placed = (
        P("ctx", None, "fsdp"),
        P(None, None, "fsdp"),
        P("fsdp", None),
        P("fsdp", None),
        P("fsdp", "ctx"),
        P("ctx", None),
    )
    return jax.shard_map(
        per_device,
        mesh=mesh,
        in_specs=placed,
        out_specs=(P("ctx", "fsdp"), P("ctx", None, "fsdp")),
        check_vma=False,
    )
```

time: 163 us -> 136 us (0.83)
  matrix products: 28 us -> 0 us
  starting transfers between devices: 58 us -> 45.3 us
  Pallas kernels: 6.38 us -> 17.1 us
  waiting for transfers between devices: 54.1 us -> 58.1 us
  local copies, waits for them, and re-layouts: 6.43 us -> 8.09 us
    dot_general x18 -> x0, matrix products: 28 us -> none  [the longest x7 16.5 us: pull(): lax.dot_general(rows[:, width:], w_other, contract, preferred_element_typ...]
    pallas_call x1 -> x2, Pallas kernels: 0.79 us -> 11.6 us  [the longest x1 9.8 us: per_device(): kernel_call(functools.partial(product_kernel, n_pair, n_line, len(w_other...]
    ppermute x2, starting transfers between devices: 11.7 us -> 4.13 us  [per_device(): placed = [lax.ppermute(part, ('fsdp', 'ctx'), route) for part in gathered]]
    ppermute x2, waiting for transfers between devices: 0.01 us -> 5.5 us  [per_device(): placed = [lax.ppermute(part, ('fsdp', 'ctx'), route) for part in gathered]]
    ppermute x31 -> x22, starting transfers between devices: 40.3 us -> 36.5 us  [swapped(): return lax.ppermute(block, axis, [(i, i ^ mask) for i in range(count)])]
    unnamed x16 -> x12, local copies, waits for them, and re-layouts: 2.4 us -> 4.36 us
    select_n x1 -> x4, other arithmetic: 1.96 us -> 0.1 us  [exchanged(): total = jnp.where(fades, total * decay + partner, partner * decay + total)]
    convert_element_type x7 -> x6, other arithmetic: 0.98 us -> 2.67 us  [the longest x1 1.54 us: per_device(): rest = [summed(line ^ m).astype(BF16) for m in range(1, n_line)]]
  transfers between devices with their start and end apart: 36 -> 26, of which waited for: 14 -> 16; matrix products, arithmetic and copies ran while one was open for 23% -> 6% of each run, Pallas kernels for 3% -> 3%
where the time goes in v2:
time: 136 us; the launch traced here: 134 us
  waiting for transfers between devices  58.1 us (43%)
  starting transfers between devices  45.3 us (33%)
  Pallas kernels  17.1 us (13%)
  local copies, waits for them, and re-layouts  8.09 us (6%)
  other arithmetic  4.97 us (4%)
    ppermute x22, waiting for transfers between devices, swapped(): return lax.ppermute(block, axis, [(i, i ^ mask) for i in range(count)])  52.6 us
    ppermute x22, starting transfers between devices, swapped(): return lax.ppermute(block, axis, [(i, i ^ mask) for i in range(count)])  36.5 us
    pallas_call x1, Pallas kernels, per_device(): kernel_call(functools.partial(product_kernel, n_pair, n_line, len(w_other...  9.8 us
    ppermute x2, waiting for transfers between devices, per_device(): placed = [lax.ppermute(part, ('fsdp', 'ctx'), route) for part in gathered]  5.5 us
    ppermute x2, starting transfers between devices, shifted(): return lax.ppermute(block, axis, route)  4.68 us
    unnamed x12, local copies, waits for them, and re-layouts  4.36 us
    ppermute x2, starting transfers between devices, per_device(): placed = [lax.ppermute(part, ('fsdp', 'ctx'), route) for part in gathered]  4.13 us
  transfers between devices with their start and end apart: 26, of which 16 were waited for; matrix products, arithmetic and copies ran while one was open for 6% of the time, Pallas kernels for 3%

profile of v2, /device:TPU:4, one launch (start us, length us, event | category | flops | bytes accessed | tf_op | source)
XLA Modules:
  0.0 134.5 jit_solution(13511788640210613936)
XLA Ops:
  0.6 0.8 slice.15
  1.4 3.4 %collective-permute-start = (bf16[2,3,1024]{2,0,1:T(2,128)(2,1)S(1)}, bf16[2,3,1024]{2,0,1:T(2,128)(2,1)S(1)}, u32[]{:S(2)}, u32[]{:S(2)}) collective-permute-start(bf16[2,3,1024]{2,0,1:T(2,128)(2,1)S(1)} %slice.15), channel_id=1, source_target_pairs={{0,1},{1,2},{2,3},{3,4},{4,5},{5,6},{6,7},{8,9},{9,10},{10,11},{11... | collective-permute-start | bytes 36872 | tf_op jit(solution)/shard_map/ppermute | solution.py:27
  4.9 1.5 %copy.11 = bf16[128,3,1024]{0,2,1:T(8,128)(2,1)S(1)} copy(bf16[128,3,1024]{2,0,1:T(8,128)(2,1)} %param.6) | data formatting | bytes 1572864 | tf_op args[0]
  6.4 0.8 reshape.133.taps_ref
  7.2 0.9 copy.16
  8.5 1.1 shard_map.77
  9.6 1.6 %collective-permute-start.1 = (f32[16,8,128]{2,1,0:T(8,128)S(1)}, f32[16,8,128]{2,1,0:T(8,128)S(1)}, u32[]{:S(2)}, u32[]{:S(2)}) collective-permute-start(f32[16,8,128]{2,1,0:T(8,128)S(1)} %get-tuple-element.32), channel_id=1, source_target_pairs={{0,1},{1,0},{2,3},{3,2},{4,5},{5,4},{6,7},{7,6},{8,9},{9,8},{10,11... | collective-permute-start | bytes 196616 | tf_op jit(solution)/shard_map/ppermute | solution.py:21
  11.3 2.7 %collective-permute-done.1.refs_0_ = f32[16,8,128]{2,1,0:T(8,128)S(1)} collective-permute-done((f32[16,8,128]{2,1,0:T(8,128)S(1)}, f32[16,8,128]{2,1,0:T(8,128)S(1)}, u32[]{:S(2)}, u32[]{:S(2)}) %collective-permute-start.1) | collective-permute-done | bytes 65568 | tf_op jit(solution)/shard_map/ppermute | solution.py:21
  14.0 1.6 %collective-permute-start.2 = (f32[16,8,128]{2,1,0:T(8,128)S(1)}, f32[16,8,128]{2,1,0:T(8,128)S(1)}, u32[]{:S(2)}, u32[]{:S(2)}) collective-permute-start(f32[16,8,128]{2,1,0:T(8,128)S(1)} %add_select_fusion.3), channel_id=1, source_target_pairs={{0,2},{1,3},{2,0},{3,1},{4,6},{5,7},{6,4},{7,5},{8,10},{9,11},{10,... | collective-permute-start | bytes 196616 | tf_op jit(solution)/shard_map/ppermute | solution.py:21
  15.6 1.5 %collective-permute-start.4 = (bf16[1024,1024]{1,0:T(8,128)(2,1)}, bf16[1024,1024]{1,0:T(8,128)(2,1)}, u32[]{:S(2)}, u32[]{:S(2)}) collective-permute-start(bf16[1024,1024]{1,0:T(8,128)(2,1)} %own_src.1), channel_id=1, source_target_pairs={{0,1},{1,0},{2,3},{3,2},{4,5},{5,4},{6,7},{7,6},{8,9},{9,8},{10,11... | collective-permute-start | bytes 6291464 | tf_op jit(solution)/shard_map/ppermute | solution.py:21
  17.2 1.1 fusion.7
  18.4 2.9 %collective-permute-start.3 = (f32[16,8,128]{2,1,0:T(8,128)S(1)}, f32[16,8,128]{2,1,0:T(8,128)S(1)}, u32[]{:S(2)}, u32[]{:S(2)}) collective-permute-start(f32[16,8,128]{2,1,0:T(8,128)S(1)} %add_select_fusion.2), channel_id=1, source_target_pairs={{0,4},{1,5},{2,6},{3,7},{4,0},{5,1},{6,2},{7,3},{8,12},{9,13},{10,... | collective-permute-start | bytes 196616 | tf_op jit(solution)/shard_map/ppermute | solution.py:21
  21.3 2.4 %collective-permute-done.3.refs_2_ = f32[16,8,128]{2,1,0:T(8,128)S(1)} collective-permute-done((f32[16,8,128]{2,1,0:T(8,128)S(1)}, f32[16,8,128]{2,1,0:T(8,128)S(1)}, u32[]{:S(2)}, u32[]{:S(2)}) %collective-permute-start.3) | collective-permute-done | bytes 65568 | tf_op jit(solution)/shard_map/ppermute | solution.py:21
  23.7 1.5 %collective-permute-start.5 = (bf16[32,2048]{1,0:T(8,128)(2,1)S(1)}, bf16[32,2048]{1,0:T(8,128)(2,1)S(1)}, u32[]{:S(2)}, u32[]{:S(2)}) collective-permute-start(bf16[32,2048]{1,0:T(8,128)(2,1)S(1)} %get-tuple-element.35), channel_id=1, source_target_pairs={{0,2},{1,3},{2,0},{3,1},{4,6},{5,7},{6,4},{7,5},{8,10},{9,11},{10,... | collective-permute-start | bytes 393224 | tf_op jit(solution)/shard_map/ppermute | solution.py:21
  25.2 3.5 %collective-permute-start.6 = (bf16[32,2048]{1,0:T(8,128)(2,1)S(1)}, bf16[32,2048]{1,0:T(8,128)(2,1)S(1)}, u32[]{:S(2)}, u32[]{:S(2)}) collective-permute-start(bf16[32,2048]{1,0:T(8,128)(2,1)S(1)} %get-tuple-element.36), channel_id=1, source_target_pairs={{0,4},{1,5},{2,6},{3,7},{4,0},{5,1},{6,2},{7,3},{8,12},{9,13},{10,... | collective-permute-start | bytes 393224 | tf_op jit(solution)/shard_map/ppermute | solution.py:21
  28.8 2.0 %shard_map.78 = (bf16[128,1024]{1,0:T(8,128)(2,1)S(1)}, f32[128,8,128]{2,1,0:T(8,128)S(1)}) custom-call(f32[2,3]{1,0:T(2,128)S(1)} %add_convert_fusion.3.reach_ref, f32[16,8,128]{2,1,0:T(8,128)S(1)} %bitcast.40, f32[16,8,128]{2,1,0:T(8,128)S(1)} %bitcast.44, f32[128,3,8,128]{3,2,1,0:T(8,128)S(1)} %get-tuple-element.30.mixed_ref, ...), custom_call_target="tpu_custom_call" | custom-call | flops 8388608 | bytes 3145728 | tf_op jit(solution)/shard_map/pallas_call | solution.py:312
  30.8 2.6 %collective-permute-done.6 = bf16[32,2048]{1,0:T(8,128)(2,1)S(1)} collective-permute-done((bf16[32,2048]{1,0:T(8,128)(2,1)S(1)}, bf16[32,2048]{1,0:T(8,128)(2,1)S(1)}, u32[]{:S(2)}, u32[]{:S(2)}) %collective-permute-start.6) | collective-permute-done | bytes 131104 | tf_op jit(solution)/shard_map/ppermute | solution.py:21
  33.5 3.2 %collective-permute-done.7 = bf16[32,2048]{1,0:T(8,128)(2,1)S(1)} collective-permute-done((bf16[32,2048]{1,0:T(8,128)(2,1)S(1)}, bf16[32,2048]{1,0:T(8,128)(2,1)S(1)}, u32[]{:S(2)}, u32[]{:S(2)}) %collective-permute-start.7) | collective-permute-done | bytes 131104 | tf_op jit(solution)/shard_map/ppermute | solution.py:21
  36.8 4.7 %collective-permute-start.13 = (bf16[128,1024]{1,0:T(8,128)(2,1)S(1)}, bf16[128,1024]{1,0:T(8,128)(2,1)S(1)}, u32[]{:S(2)}, u32[]{:S(2)}) collective-permute-start(bf16[128,1024]{1,0:T(8,128)(2,1)S(1)} %get-tuple-element.38.refs_5_), channel_id=1, source_target_pairs={{0,6},{1,7},{2,4},{3,5},{4,2},{5,3},{6,0},{7,1},{8,14},{9,15},{10,... | collective-permute-start | bytes 786440 | tf_op jit(solution)/shard_map/ppermute | solution.py:21
  41.4 3.1 %collective-permute-done.8.refs_2_ = bf16[96,2048]{1,0:T(8,128)(2,1)S(1)} collective-permute-done((bf16[96,2048]{1,0:T(8,128)(2,1)S(1)}, bf16[96,2048]{1,0:T(8,128)(2,1)S(1)}, u32[]{:S(2)}, u32[]{:S(2)}) %collective-permute-start.8) | collective-permute-done | bytes 393248 | tf_op jit(solution)/shard_map/ppermute | solution.py:21
  44.5 6.5 %collective-permute-start.12 = (bf16[128,1024]{1,0:T(8,128)(2,1)S(1)}, bf16[128,1024]{1,0:T(8,128)(2,1)S(1)}, u32[]{:S(2)}, u32[]{:S(2)}) collective-permute-start(bf16[128,1024]{1,0:T(8,128)(2,1)S(1)} %get-tuple-element.38.refs_5_), channel_id=1, source_target_pairs={{0,4},{1,5},{2,6},{3,7},{4,0},{5,1},{6,2},{7,3},{8,12},{9,13},{10,... | collective-permute-start | bytes 786440 | tf_op jit(solution)/shard_map/ppermute | solution.py:21
  51.1 12.6 %collective-permute-done.12.refs_7_ = bf16[128,1024]{1,0:T(8,128)(2,1)S(1)} collective-permute-done((bf16[128,1024]{1,0:T(8,128)(2,1)S(1)}, bf16[128,1024]{1,0:T(8,128)(2,1)S(1)}, u32[]{:S(2)}, u32[]{:S(2)}) %collective-permute-start.12) | collective-permute-done | bytes 262176 | tf_op jit(solution)/shard_map/ppermute | solution.py:21
  63.7 1.1 collective-permute-done.11.refs_6_
  64.8 9.8 %shard_map.79 = (bf16[256,2048]{1,0:T(8,128)(2,1)}, bf16[256,2048]{1,0:T(8,128)(2,1)S(1)}, f32[128,1024]{1,0:T(8,128)S(1)}, bf16[128,1024]{1,0:T(8,128)(2,1)}, b...) custom-call(s32[4]{0:T(128)S(1)} %pad_add_fusion.2.place_ref, bf16[1024,1024]{1,0:T(8,128)(2,1)} %own_src.1, ...), custom_call_target="tpu_custom_call" | custom-call | flops 4294967296 | bytes 8388608 | tf_op jit(solution)/shard_map/pallas_call | solution.py:338
  74.7 0.8 copy-done
  75.5 3.0 %collective-permute-done.17 = bf16[256,2048]{1,0:T(8,128)(2,1)} collective-permute-done((bf16[256,2048]{1,0:T(8,128)(2,1)}, bf16[256,2048]{1,0:T(8,128)(2,1)}, u32[]{:S(2)}, u32[]{:S(2)}) %collective-permute-start.17) | collective-permute-done | bytes 1048608 | tf_op jit(solution)/shard_map/ppermute | solution.py:21
  78.5 1.5 %fusion = (bf16[128,2048]{1,0:T(8,128)(2,1)S(1)}, f32[128,2048]{1,0:T(8,128)S(1)}) fusion(bf16[2,128,2048]{2,1,0:T(8,128)(2,1)} %bitcast.14, s32[]{:T(128)S(6)} %select_n.109, bf16[2,128,2048]{2,1,0:T(8,128)(2,1)S(1)} %bitcast.43, s32[]{:T(128)S(6)} %select_n.108), kind=kLoop, calls=%fused_computation.2 | loop fusion | flops 1835008 | bytes 3670024 | tf_op jit(solution)/shard_map/convert_element_type | solution.py:363
  80.1 2.0 %collective-permute-start.18 = (bf16[128,1024]{1,0:T(8,128)(2,1)S(1)}, bf16[128,1024]{1,0:T(8,128)(2,1)S(1)}, u32[]{:S(2)}, u32[]{:S(2)}) collective-permute-start(bf16[128,1024]{1,0:T(8,128)(2,1)S(1)} %get-tuple-element.70), channel_id=1, source_target_pairs={{0,16},{8,24},{16,0},{24,8},{1,17},{9,25},{17,1},{25,9},{2,18},{10... | collective-permute-start | bytes 786440 | tf_op jit(solution)/shard_map/ppermute | solution.py:21
  82.7 3.8 %collective-permute-start.16 = (bf16[128,1024]{1,0:T(8,128)(2,1)}, bf16[128,1024]{1,0:T(8,128)(2,1)}, u32[]{:S(2)}, u32[]{:S(2)}) collective-permute-start(bf16[128,1024]{1,0:T(8,128)(2,1)} %get-tuple-element.45), channel_id=1, source_target_pairs={{0,6},{1,7},{2,4},{3,5},{4,2},{5,3},{6,0},{7,1},{8,14},{9,15},{10,... | collective-permute-start | bytes 786440 | tf_op jit(solution)/shard_map/ppermute | solution.py:21
  86.5 2.7 %collective-permute-done.19 = bf16[128,1024]{1,0:T(8,128)(2,1)S(1)} collective-permute-done((bf16[128,1024]{1,0:T(8,128)(2,1)S(1)}, bf16[128,1024]{1,0:T(8,128)(2,1)S(1)}, u32[]{:S(2)}, u32[]{:S(2)}) %collective-permute-start.19) | collective-permute-done | bytes 262176 | tf_op jit(solution)/shard_map/ppermute | solution.py:21
  89.3 4.8 %collective-permute-done.18 = bf16[128,1024]{1,0:T(8,128)(2,1)S(1)} collective-permute-done((bf16[128,1024]{1,0:T(8,128)(2,1)S(1)}, bf16[128,1024]{1,0:T(8,128)(2,1)S(1)}, u32[]{:S(2)}, u32[]{:S(2)}) %collective-permute-start.18) | collective-permute-done | bytes 262176 | tf_op jit(solution)/shard_map/ppermute | solution.py:21
  94.1 1.0 fusion.1
  95.1 2.2 %collective-permute-start.22 = (bf16[128,1024]{1,0:T(8,128)(2,1)}, bf16[128,1024]{1,0:T(8,128)(2,1)}, u32[]{:S(2)}, u32[]{:S(2)}) collective-permute-start(bf16[128,1024]{1,0:T(8,128)(2,1)} %get-tuple-element.67), channel_id=1, source_target_pairs={{0,0},{1,1},{2,10},{3,11},{4,20},{5,21},{6,30},{7,31},{8,4},{9,5},... | collective-permute-start | bytes 786440 | tf_op jit(solution)/shard_map/ppermute | solution.py:371
  97.3 1.9 %collective-permute-start.21 = (bf16[128,1024]{1,0:T(8,128)(2,1)}, bf16[128,1024]{1,0:T(8,128)(2,1)}, u32[]{:S(2)}, u32[]{:S(2)}) collective-permute-start(bf16[128,1024]{1,0:T(8,128)(2,1)} %get-tuple-element.68), channel_id=1, source_target_pairs={{0,0},{1,1},{2,10},{3,11},{4,20},{5,21},{6,30},{7,31},{8,4},{9,5},... | collective-permute-start | bytes 786440 | tf_op jit(solution)/shard_map/ppermute | solution.py:371
  99.3 8.4 %collective-permute-done.15.refs_1_ = bf16[128,1024]{1,0:T(8,128)(2,1)S(1)} collective-permute-done((bf16[128,1024]{1,0:T(8,128)(2,1)}, bf16[128,1024]{1,0:T(8,128)(2,1)S(1)}, u32[]{:S(2)}, u32[]{:S(2)}) %collective-permute-start.15) | collective-permute-done | bytes 262176 | tf_op jit(solution)/shard_map/ppermute | solution.py:21
  107.8 1.8 %shard_map.80 = (f32[1024,128]{1,0:T(8,128)S(1)}, f32[16,8,128]{2,1,0:T(8,128)S(1)}, f32[2,5,8,128]{3,2,1,0:T(8,128)S(1)}) custom-call(f32[16,8,128]{2,1,0:T(8,128)S(1)} %bitcast.41, f32[128,3,8,128]{3,2,1,0:T(8,128)S(1)} %get-tuple-element.30.mixed_ref, f32[128,8,128]{2,1,0:T(8,128)S(1)} %get-tuple-element.33.convolved_ref, f32[128,1024]{1,0:T(8,128)S(1)} %copy-done.1, ...), custom_call_target="tpu_custom_call" | custom-call | flops 5242880 | bytes 3145728 | tf_op jit(solution)/shard_map/pallas_call | solution.py:373
  109.6 1.5 %collective-permute-start.20 = (f32[16,8,128]{2,1,0:T(8,128)S(1)}, f32[16,8,128]{2,1,0:T(8,128)S(1)}, u32[]{:S(2)}, u32[]{:S(2)}) collective-permute-start(f32[16,8,128]{2,1,0:T(8,128)S(1)} %get-tuple-element.52), channel_id=1, source_target_pairs={{0,1},{1,0},{2,3},{3,2},{4,5},{5,4},{6,7},{7,6},{8,9},{9,8},{10,11... | collective-permute-start | bytes 196616 | tf_op jit(solution)/shard_map/ppermute | solution.py:21
  111.1 2.8 %collective-permute-done.20.refs_0_ = f32[16,8,128]{2,1,0:T(8,128)S(1)} collective-permute-done((f32[16,8,128]{2,1,0:T(8,128)S(1)}, f32[16,8,128]{2,1,0:T(8,128)S(1)}, u32[]{:S(2)}, u32[]{:S(2)}) %collective-permute-start.20) | collective-permute-done | bytes 65568 | tf_op jit(solution)/shard_map/ppermute | solution.py:21
  113.9 2.7 %collective-permute-done.22 = bf16[128,1024]{1,0:T(8,128)(2,1)} collective-permute-done((bf16[128,1024]{1,0:T(8,128)(2,1)}, bf16[128,1024]{1,0:T(8,128)(2,1)}, u32[]{:S(2)}, u32[]{:S(2)}) %collective-permute-start.22) | collective-permute-done | bytes 262176 | tf_op jit(solution)/shard_map/ppermute | solution.py:371
  116.6 2.8 %collective-permute-done.21 = bf16[128,1024]{1,0:T(8,128)(2,1)} collective-permute-done((bf16[128,1024]{1,0:T(8,128)(2,1)}, bf16[128,1024]{1,0:T(8,128)(2,1)}, u32[]{:S(2)}, u32[]{:S(2)}) %collective-permute-start.21) | collective-permute-done | bytes 262176 | tf_op jit(solution)/shard_map/ppermute | solution.py:371
  119.5 3.1 %collective-permute-start.24 = (f32[16,8,128]{2,1,0:T(8,128)S(1)}, f32[16,8,128]{2,1,0:T(8,128)S(1)}, u32[]{:S(2)}, u32[]{:S(2)}) collective-permute-start(f32[16,8,128]{2,1,0:T(8,128)S(1)} %add_select_fusion.1), channel_id=1, source_target_pairs={{0,2},{1,3},{2,0},{3,1},{4,6},{5,7},{6,4},{7,5},{8,10},{9,11},{10,... | collective-permute-start | bytes 196616 | tf_op jit(solution)/shard_map/ppermute | solution.py:21
  122.5 1.3 collective-permute-start.23
  123.8 1.3 collective-permute-done.24.refs_1_
  125.1 1.5 %collective-permute-start.25 = (f32[16,8,128]{2,1,0:T(8,128)S(1)}, f32[16,8,128]{2,1,0:T(8,128)S(1)}, u32[]{:S(2)}, u32[]{:S(2)}) collective-permute-start(f32[16,8,128]{2,1,0:T(8,128)S(1)} %add_select_fusion), channel_id=1, source_target_pairs={{0,4},{1,5},{2,6},{3,7},{4,0},{5,1},{6,2},{7,3},{8,12},{9,13},{10,... | collective-permute-start | bytes 196616 | tf_op jit(solution)/shard_map/ppermute | solution.py:21
  126.6 1.9 %pad_maximum_fusion = bf16[128,2048]{1,0:T(8,128)(2,1)} fusion(bf16[128,1024]{1,0:T(8,128)(2,1)} %collective-permute-done.22, bf16[128,1024]{1,0:T(8,128)(2,1)} %collective-permute-done.21), kind=kLoop, calls=%fused_computation.7 | loop fusion | flops 1048576 | bytes 1048576 | tf_op jit(solution)/shard_map/concatenate | solution.py:387
  128.5 1.8 %collective-permute-done.25.refs_2_ = f32[16,8,128]{2,1,0:T(8,128)S(1)} collective-permute-done((f32[16,8,128]{2,1,0:T(8,128)S(1)}, f32[16,8,128]{2,1,0:T(8,128)S(1)}, u32[]{:S(2)}, u32[]{:S(2)}) %collective-permute-start.25) | collective-permute-done | bytes 65568 | tf_op jit(solution)/shard_map/ppermute | solution.py:21
  130.3 2.3 %shard_map.81 = f32[128,3,8,128]{3,2,1,0:T(8,128)S(1)} custom-call(f32[2,3]{1,0:T(2,128)S(1)} %add_convert_fusion.4.reach_ref, f32[16,8,128]{2,1,0:T(8,128)S(1)} %bitcast.42, f32[16,8,128]{2,1,0:T(8,128)S(1)} %bitcast.45, f32[3,3,8,128]{3,2,1,0:T(8,128)S(1)} %reshape.133.taps_ref, f32[128,3,8,128]{3,2,1,0:T(8,128)S(1)} %get-tuple-element.30.mixed_ref, ...), custom_call_target="tpu_custom_call" | custom-call | flops 10485760 | bytes 3145728 | tf_op jit(solution)/shard_map/pallas_call | solution.py:389
  133.3 1.2 copy.15
  (45 shorter events, 2.5 us)
Async XLA Ops:
  1.4 7.1 %collective-permute-start = (bf16[2,3,1024]{2,0,1:T(2,128)(2,1)S(1)}, bf16[2,3,1024]{2,0,1:T(2,128)(2,1)S(1)}, u32[]{:S(2)}, u32[]{:S(2)}) collective-permute-start(bf16[2,3,1024]{2,0,1:T(2,128)(2,1)S(1)} %slice.15), channel_id=1, source_target_pairs={{0,1},{1,2},{2,3},{3,4},{4,5},{5,6},{6,7},{8,9},{9,10},{10,11},{11... | collective-permute-start | bytes 36872 | tf_op jit(solution)/shard_map/ppermute | solution.py:27
  8.5 20.3 %copy-start.2 = (f32[1024,16]{0,1:T(8,128)S(1)}, f32[1024,16]{0,1:T(8,128)}, u32[]{:S(2)}) copy-start(f32[1024,16]{0,1:T(8,128)} %param.8) | copy-start | bytes 196612
  9.6 4.3 %collective-permute-start.1 = (f32[16,8,128]{2,1,0:T(8,128)S(1)}, f32[16,8,128]{2,1,0:T(8,128)S(1)}, u32[]{:S(2)}, u32[]{:S(2)}) collective-permute-start(f32[16,8,128]{2,1,0:T(8,128)S(1)} %get-tuple-element.32), channel_id=1, source_target_pairs={{0,1},{1,0},{2,3},{3,2},{4,5},{5,4},{6,7},{7,6},{8,9},{9,8},{10,11... | collective-permute-start | bytes 196616 | tf_op jit(solution)/shard_map/ppermute | solution.py:21
  14.0 4.3 %collective-permute-start.2 = (f32[16,8,128]{2,1,0:T(8,128)S(1)}, f32[16,8,128]{2,1,0:T(8,128)S(1)}, u32[]{:S(2)}, u32[]{:S(2)}) collective-permute-start(f32[16,8,128]{2,1,0:T(8,128)S(1)} %add_select_fusion.3), channel_id=1, source_target_pairs={{0,2},{1,3},{2,0},{3,1},{4,6},{5,7},{6,4},{7,5},{8,10},{9,11},{10,... | collective-permute-start | bytes 196616 | tf_op jit(solution)/shard_map/ppermute | solution.py:21
  15.6 49.2 %collective-permute-start.4 = (bf16[1024,1024]{1,0:T(8,128)(2,1)}, bf16[1024,1024]{1,0:T(8,128)(2,1)}, u32[]{:S(2)}, u32[]{:S(2)}) collective-permute-start(bf16[1024,1024]{1,0:T(8,128)(2,1)} %own_src.1), channel_id=1, source_target_pairs={{0,1},{1,0},{2,3},{3,2},{4,5},{5,4},{6,7},{7,6},{8,9},{9,8},{10,11... | collective-permute-start | bytes 6291464 | tf_op jit(solution)/shard_map/ppermute | solution.py:21
  18.4 5.3 %collective-permute-start.3 = (f32[16,8,128]{2,1,0:T(8,128)S(1)}, f32[16,8,128]{2,1,0:T(8,128)S(1)}, u32[]{:S(2)}, u32[]{:S(2)}) collective-permute-start(f32[16,8,128]{2,1,0:T(8,128)S(1)} %add_select_fusion.2), channel_id=1, source_target_pairs={{0,4},{1,5},{2,6},{3,7},{4,0},{5,1},{6,2},{7,3},{8,12},{9,13},{10,... | collective-permute-start | bytes 196616 | tf_op jit(solution)/shard_map/ppermute | solution.py:21
  23.7 7.1 %collective-permute-start.5 = (bf16[32,2048]{1,0:T(8,128)(2,1)S(1)}, bf16[32,2048]{1,0:T(8,128)(2,1)S(1)}, u32[]{:S(2)}, u32[]{:S(2)}) collective-permute-start(bf16[32,2048]{1,0:T(8,128)(2,1)S(1)} %get-tuple-element.35), channel_id=1, source_target_pairs={{0,2},{1,3},{2,0},{3,1},{4,6},{5,7},{6,4},{7,5},{8,10},{9,11},{10,... | collective-permute-start | bytes 393224 | tf_op jit(solution)/shard_map/ppermute | solution.py:21
  25.2 8.3 %collective-permute-start.6 = (bf16[32,2048]{1,0:T(8,128)(2,1)S(1)}, bf16[32,2048]{1,0:T(8,128)(2,1)S(1)}, u32[]{:S(2)}, u32[]{:S(2)}) collective-permute-start(bf16[32,2048]{1,0:T(8,128)(2,1)S(1)} %get-tuple-element.36), channel_id=1, source_target_pairs={{0,4},{1,5},{2,6},{3,7},{4,0},{5,1},{6,2},{7,3},{8,12},{9,13},{10,... | collective-permute-start | bytes 393224 | tf_op jit(solution)/shard_map/ppermute | solution.py:21
  28.7 7.9 %collective-permute-start.7 = (bf16[32,2048]{1,0:T(8,128)(2,1)S(1)}, bf16[32,2048]{1,0:T(8,128)(2,1)S(1)}, u32[]{:S(2)}, u32[]{:S(2)}) collective-permute-start(bf16[32,2048]{1,0:T(8,128)(2,1)S(1)} %get-tuple-element.37), channel_id=1, source_target_pairs={{0,6},{1,7},{2,4},{3,5},{4,2},{5,3},{6,0},{7,1},{8,14},{9,15},{10,... | collective-permute-start | bytes 393224 | tf_op jit(solution)/shard_map/ppermute | solution.py:21
  36.7 7.8 %collective-permute-start.8 = (bf16[96,2048]{1,0:T(8,128)(2,1)S(1)}, bf16[96,2048]{1,0:T(8,128)(2,1)S(1)}, u32[]{:S(2)}, u32[]{:S(2)}) collective-permute-start(bf16[96,2048]{1,0:T(8,128)(2,1)S(1)} %constant_dynamic-update-slice_fusion.refs_1_), channel_id=1, source_target_pairs={{0,16},{8,24},{16,0},{24,8},{1,17},{9,25},{17,1},{25,9},{2,18},{10... | collective-permute-start | bytes 1179656 | tf_op jit(solution)/shard_map/ppermute | solution.py:21
  36.8 14.3 %collective-permute-start.13 = (bf16[128,1024]{1,0:T(8,128)(2,1)S(1)}, bf16[128,1024]{1,0:T(8,128)(2,1)S(1)}, u32[]{:S(2)}, u32[]{:S(2)}) collective-permute-start(bf16[128,1024]{1,0:T(8,128)(2,1)S(1)} %get-tuple-element.38.refs_5_), channel_id=1, source_target_pairs={{0,6},{1,7},{2,4},{3,5},{4,2},{5,3},{6,0},{7,1},{8,14},{9,15},{10,... | collective-permute-start | bytes 786440 | tf_op jit(solution)/shard_map/ppermute | solution.py:21
  41.4 23.4 %collective-permute-start.9 = (bf16[96,2048]{1,0:T(8,128)(2,1)S(1)}, bf16[96,2048]{1,0:T(8,128)(2,1)S(1)}, u32[]{:S(2)}, u32[]{:S(2)}) collective-permute-start(bf16[96,2048]{1,0:T(8,128)(2,1)S(1)} %constant_dynamic-update-slice_fusion.refs_1_), channel_id=1, source_target_pairs={{0,8},{8,0},{16,24},{24,16},{1,9},{9,1},{17,25},{25,17},{2,10},{10... | collective-permute-start | bytes 1179656 | tf_op jit(solution)/shard_map/ppermute | solution.py:21
  44.5 20.3 %collective-permute-start.10 = (bf16[96,2048]{1,0:T(8,128)(2,1)S(1)}, bf16[96,2048]{1,0:T(8,128)(2,1)S(1)}, u32[]{:S(2)}, u32[]{:S(2)}) collective-permute-start(bf16[96,2048]{1,0:T(8,128)(2,1)S(1)} %collective-permute-done.8.refs_2_), channel_id=1, source_target_pairs={{0,8},{8,0},{16,24},{24,16},{1,9},{9,1},{17,25},{25,17},{2,10},{10... | collective-permute-start | bytes 1179656 | tf_op jit(solution)/shard_map/ppermute | solution.py:21
  44.5 19.2 %collective-permute-start.12 = (bf16[128,1024]{1,0:T(8,128)(2,1)S(1)}, bf16[128,1024]{1,0:T(8,128)(2,1)S(1)}, u32[]{:S(2)}, u32[]{:S(2)}) collective-permute-start(bf16[128,1024]{1,0:T(8,128)(2,1)S(1)} %get-tuple-element.38.refs_5_), channel_id=1, source_target_pairs={{0,4},{1,5},{2,6},{3,7},{4,0},{5,1},{6,2},{7,3},{8,12},{9,13},{10,... | collective-permute-start | bytes 786440 | tf_op jit(solution)/shard_map/ppermute | solution.py:21
  51.0 13.8 %collective-permute-start.11 = (bf16[128,1024]{1,0:T(8,128)(2,1)S(1)}, bf16[128,1024]{1,0:T(8,128)(2,1)S(1)}, u32[]{:S(2)}, u32[]{:S(2)}) collective-permute-start(bf16[128,1024]{1,0:T(8,128)(2,1)S(1)} %get-tuple-element.38.refs_5_), channel_id=1, source_target_pairs={{0,2},{1,3},{2,0},{3,1},{4,6},{5,7},{6,4},{7,5},{8,10},{9,11},{10,... | collective-permute-start | bytes 786440 | tf_op jit(solution)/shard_map/ppermute | solution.py:21
  74.7 0.8 copy-start
  75.5 3.0 %collective-permute-start.17 = (bf16[256,2048]{1,0:T(8,128)(2,1)}, bf16[256,2048]{1,0:T(8,128)(2,1)}, u32[]{:S(2)}, u32[]{:S(2)}) collective-permute-start(bf16[256,2048]{1,0:T(8,128)(2,1)} %get-tuple-element.47), channel_id=1, source_target_pairs={{0,8},{8,0},{16,24},{24,16},{1,9},{9,1},{17,25},{25,17},{2,10},{10... | collective-permute-start | bytes 3145736 | tf_op jit(solution)/shard_map/ppermute | solution.py:21
  80.0 27.8 %copy-start.1 = (f32[128,1024]{1,0:T(8,128)S(1)}, f32[128,1024]{1,0:T(8,128)}, u32[]{:S(2)}) copy-start(f32[128,1024]{1,0:T(8,128)} %copy-done) | copy-start | bytes 1572868
  80.1 9.2 %collective-permute-start.19 = (bf16[128,1024]{1,0:T(8,128)(2,1)S(1)}, bf16[128,1024]{1,0:T(8,128)(2,1)S(1)}, u32[]{:S(2)}, u32[]{:S(2)}) collective-permute-start(bf16[128,1024]{1,0:T(8,128)(2,1)S(1)} %get-tuple-element.69), channel_id=1, source_target_pairs={{0,16},{8,24},{16,0},{24,8},{1,17},{9,25},{17,1},{25,9},{2,18},{10... | collective-permute-start | bytes 786440 | tf_op jit(solution)/shard_map/ppermute | solution.py:21
  80.1 14.0 %collective-permute-start.18 = (bf16[128,1024]{1,0:T(8,128)(2,1)S(1)}, bf16[128,1024]{1,0:T(8,128)(2,1)S(1)}, u32[]{:S(2)}, u32[]{:S(2)}) collective-permute-start(bf16[128,1024]{1,0:T(8,128)(2,1)S(1)} %get-tuple-element.70), channel_id=1, source_target_pairs={{0,16},{8,24},{16,0},{24,8},{1,17},{9,25},{17,1},{25,9},{2,18},{10... | collective-permute-start | bytes 786440 | tf_op jit(solution)/shard_map/ppermute | solution.py:21
  82.2 17.1 %collective-permute-start.14 = (bf16[128,1024]{1,0:T(8,128)(2,1)}, bf16[128,1024]{1,0:T(8,128)(2,1)S(1)}, u32[]{:S(2)}, u32[]{:S(2)}) collective-permute-start(bf16[128,1024]{1,0:T(8,128)(2,1)} %get-tuple-element.43), channel_id=1, source_target_pairs={{0,2},{1,3},{2,0},{3,1},{4,6},{5,7},{6,4},{7,5},{8,10},{9,11},{10,... | collective-permute-start | bytes 786440 | tf_op jit(solution)/shard_map/ppermute | solution.py:21
  82.7 25.0 %collective-permute-start.15 = (bf16[128,1024]{1,0:T(8,128)(2,1)}, bf16[128,1024]{1,0:T(8,128)(2,1)S(1)}, u32[]{:S(2)}, u32[]{:S(2)}) collective-permute-start(bf16[128,1024]{1,0:T(8,128)(2,1)} %get-tuple-element.44), channel_id=1, source_target_pairs={{0,4},{1,5},{2,6},{3,7},{4,0},{5,1},{6,2},{7,3},{8,12},{9,13},{10,... | collective-permute-start | bytes 786440 | tf_op jit(solution)/shard_map/ppermute | solution.py:21
  82.7 25.0 %collective-permute-start.16 = (bf16[128,1024]{1,0:T(8,128)(2,1)}, bf16[128,1024]{1,0:T(8,128)(2,1)}, u32[]{:S(2)}, u32[]{:S(2)}) collective-permute-start(bf16[128,1024]{1,0:T(8,128)(2,1)} %get-tuple-element.45), channel_id=1, source_target_pairs={{0,6},{1,7},{2,4},{3,5},{4,2},{5,3},{6,0},{7,1},{8,14},{9,15},{10,... | collective-permute-start | bytes 786440 | tf_op jit(solution)/shard_map/ppermute | solution.py:21
  95.1 21.5 %collective-permute-start.22 = (bf16[128,1024]{1,0:T(8,128)(2,1)}, bf16[128,1024]{1,0:T(8,128)(2,1)}, u32[]{:S(2)}, u32[]{:S(2)}) collective-permute-start(bf16[128,1024]{1,0:T(8,128)(2,1)} %get-tuple-element.67), channel_id=1, source_target_pairs={{0,0},{1,1},{2,10},{3,11},{4,20},{5,21},{6,30},{7,31},{8,4},{9,5},... | collective-permute-start | bytes 786440 | tf_op jit(solution)/shard_map/ppermute | solution.py:371
  97.3 22.2 %collective-permute-start.21 = (bf16[128,1024]{1,0:T(8,128)(2,1)}, bf16[128,1024]{1,0:T(8,128)(2,1)}, u32[]{:S(2)}, u32[]{:S(2)}) collective-permute-start(bf16[128,1024]{1,0:T(8,128)(2,1)} %get-tuple-element.68), channel_id=1, source_target_pairs={{0,0},{1,1},{2,10},{3,11},{4,20},{5,21},{6,30},{7,31},{8,4},{9,5},... | collective-permute-start | bytes 786440 | tf_op jit(solution)/shard_map/ppermute | solution.py:371
  109.6 4.3 %collective-permute-start.20 = (f32[16,8,128]{2,1,0:T(8,128)S(1)}, f32[16,8,128]{2,1,0:T(8,128)S(1)}, u32[]{:S(2)}, u32[]{:S(2)}) collective-permute-start(f32[16,8,128]{2,1,0:T(8,128)S(1)} %get-tuple-element.52), channel_id=1, source_target_pairs={{0,1},{1,0},{2,3},{3,2},{4,5},{5,4},{6,7},{7,6},{8,9},{9,8},{10,11... | collective-permute-start | bytes 196616 | tf_op jit(solution)/shard_map/ppermute | solution.py:21
  119.5 5.6 %collective-permute-start.24 = (f32[16,8,128]{2,1,0:T(8,128)S(1)}, f32[16,8,128]{2,1,0:T(8,128)S(1)}, u32[]{:S(2)}, u32[]{:S(2)}) collective-permute-start(f32[16,8,128]{2,1,0:T(8,128)S(1)} %add_select_fusion.1), channel_id=1, source_target_pairs={{0,2},{1,3},{2,0},{3,1},{4,6},{5,7},{6,4},{7,5},{8,10},{9,11},{10,... | collective-permute-start | bytes 196616 | tf_op jit(solution)/shard_map/ppermute | solution.py:21
  122.5 6.0 %collective-permute-start.23 = (f32[2,5,8,128]{3,2,1,0:T(8,128)S(1)}, f32[2,5,8,128]{3,2,1,0:T(8,128)S(1)}, u32[]{:S(2)}, u32[]{:S(2)}) collective-permute-start(f32[2,5,8,128]{3,2,1,0:T(8,128)S(1)} %get-tuple-element.56), channel_id=1, source_target_pairs={{1,0},{2,1},{3,2},{4,3},{5,4},{6,5},{7,6},{9,8},{10,9},{11,10},{12... | collective-permute-start | bytes 122888 | tf_op jit(solution)/shard_map/ppermute | solution.py:27
  125.1 5.2 %collective-permute-start.25 = (f32[16,8,128]{2,1,0:T(8,128)S(1)}, f32[16,8,128]{2,1,0:T(8,128)S(1)}, u32[]{:S(2)}, u32[]{:S(2)}) collective-permute-start(f32[16,8,128]{2,1,0:T(8,128)S(1)} %add_select_fusion), channel_id=1, source_target_pairs={{0,4},{1,5},{2,6},{3,7},{4,0},{5,1},{6,2},{7,3},{8,12},{9,13},{10,... | collective-permute-start | bytes 196616 | tf_op jit(solution)/shard_map/ppermute | solution.py:21

commit v3 on v2

--- a/solution.py
+++ b/solution.py
@@ -194,52 +194,57 @@
 
 def product_kernel(n_pair, n_line, pieces, place_ref, own_src, mine_src, *refs):
     others, arrived = refs[:pieces], refs[pieces : pieces + 4]
-    blocks, outs = refs[pieces + 4 : pieces + 4 + n_pair], refs[pieces + 4 + n_pair : -5]
-    own_ref, other_ref, rows_ref, gated_ref, sems = refs[-5:]
+    blocks, outs = refs[pieces + 4 : pieces + 4 + n_pair], refs[pieces + 4 + n_pair : -6]
+    own_ref, other_ref, rows_ref, gated_ref, half_ref, sems = refs[-6:]
     core, turn, side, pair = [place_ref[i] for i in range(4)]
     tokens, (wide, width) = mine_src.shape[0], own_src.shape
     part = tokens // 4
     columns = pl.ds(pl.multiple_of(pair * 2 * width, 2 * width), 2 * width)
-    pairs = [(own_src, own_ref), (mine_src.at[:, columns], rows_ref.at[pl.ds(0, tokens), :])]
+    rows = [(mine_src.at[:, columns], rows_ref.at[pl.ds(0, tokens), :])]
     turns = (2 * turn, 2 * (1 - turn), 2 * turn, 2 * (1 - turn))
     cores = (core, core, 1 - core, 1 - core)
     for k in range(1, n_pair):
         for block, up, across in zip(arrived, turns, cores):
             at = pl.multiple_of(k * tokens + (up + across) * part, part)
             source = block.at[pl.ds((k - 1) * part, part), :]
-            pairs.append((source, rows_ref.at[pl.ds(at, part), :]))
-    early, pairs = len(pairs), pairs + stacked(others, other_ref)
-    middle, pairs = len(pairs), pairs + stacked(blocks, gated_ref)
+            rows.append((source, rows_ref.at[pl.ds(at, part), :]))
+    pairs = [(own_src, own_ref)] + stacked(blocks, gated_ref)
+    first, pairs = len(pairs), pairs + rows
+    second, pairs = len(pairs), pairs + stacked(others, other_ref)
     copies = fetched(pairs, sems)
-    for copy in copies[:early]:
-        copy.wait()
     contract = (((1,), (1,)), ((), ()))
-    step = min(256, wide)
-    halves = ((own_ref, side), (other_ref, 1 - side))
-    for n in range(0, wide, step):
-        parts = []
-        for w_ref, at in halves:
-            if n == 0 and w_ref is other_ref:
-                for copy in copies[early:middle]:
-                    copy.wait()
-            rows = rows_ref[:, pl.ds(pl.multiple_of(at * width, width), width)]
-            w = w_ref[n : n + step, :]
-            parts.append(lax.dot_general(rows, w, contract, preferred_element_type=F32))
-        total = parts[0] + parts[1]
-        for k, out_ref in enumerate(outs[2:]):
-            here = total[k * tokens : (k + 1) * tokens]
-            out_ref[:, n : n + step] = here.astype(out_ref.dtype)
-    for copy in copies[middle:]:
-        copy.wait()
-    step = min(256, width)
     tall = n_line * tokens
-    for out_ref, half in ((outs[0], 1 - core), (outs[1], core)):
-        rows = gated_ref[pl.ds(pl.multiple_of(half * tall, tall), tall), :]
-        for w_ref, at in halves:
+
+    def project(w_ref, at):
+        step = min(256, width)
+        for out_ref, half in ((outs[0], 1 - core), (outs[1], core)):
+            rows = gated_ref[pl.ds(pl.multiple_of(half * tall, tall), tall), :]
             for n in range(0, width, step):
                 product = jnp.dot(rows, w_ref[:, n : n + step], preferred_element_type=F32)
                 columns = pl.ds(pl.multiple_of(at * width + n, step), step)
                 out_ref[:, columns] = product.astype(BF16)
+
+    def pull(w_ref, at, n, step):
+        rows = rows_ref[:, pl.ds(pl.multiple_of(at * width, width), width)]
+        w = w_ref[n : n + step, :]
+        return lax.dot_general(rows, w, contract, preferred_element_type=F32)
+
+    for copy in copies[:first]:
+        copy.wait()
+    project(own_ref, side)
+    for copy in copies[first:second]:
+        copy.wait()
+    step = min(256, wide)
+    for n in range(0, wide, step):
+        half_ref[:, n : n + step] = pull(own_ref, side, n, step)
+    for copy in copies[second:]:
+        copy.wait()
+    for n in range(0, wide, step):
+        total = half_ref[:, n : n + step] + pull(other_ref, 1 - side, n, step)
+        for k, out_ref in enumerate(outs[2:]):
+            here = total[k * tokens : (k + 1) * tokens]
+            out_ref[:, n : n + step] = here.astype(out_ref.dtype)
+    project(other_ref, 1 - side)
 
 
 def per_device(featurized, short_taps, residues, decay_rates, w_out, grad_out):
@@ -345,6 +350,7 @@
             pltpu.VMEM((wide, width), BF16),
             pltpu.VMEM((n_pair * tokens, 2 * width), BF16),
             pltpu.VMEM((n_pair * tokens, wide), BF16),
+            pltpu.VMEM((n_pair * tokens, wide), F32),
             pltpu.SemaphoreType.DMA((2 + 4 * (n_pair - 1) + len(w_other) + n_pair,)),
         ],
         flops=8 * n_pair * tokens * wide * width,

time: 136 us -> 135 us (level)
  Pallas kernels: 17.1 us -> 15.7 us
    pallas_call x1, Pallas kernels: 9.8 us -> 8.4 us  [per_device(): kernel_call(functools.partial(product_kernel, n_pair, n_line, len(w_other...]
where the time goes in v3:
time: 135 us; the launch traced here: 133 us
  waiting for transfers between devices  58.2 us (43%)
  starting transfers between devices  45.2 us (33%)
  Pallas kernels  15.7 us (12%)
  local copies, waits for them, and re-layouts  8.09 us (6%)
  other arithmetic  4.97 us (4%)
    ppermute x22, waiting for transfers between devices, swapped(): return lax.ppermute(block, axis, [(i, i ^ mask) for i in range(count)])  52.7 us
    ppermute x22, starting transfers between devices, swapped(): return lax.ppermute(block, axis, [(i, i ^ mask) for i in range(count)])  36.4 us
    pallas_call x1, Pallas kernels, per_device(): kernel_call(functools.partial(product_kernel, n_pair, n_line, len(w_other...  8.4 us
    ppermute x2, waiting for transfers between devices, per_device(): placed = [lax.ppermute(part, ('fsdp', 'ctx'), route) for part in gathered]  5.5 us
    ppermute x2, starting transfers between devices, shifted(): return lax.ppermute(block, axis, route)  4.68 us
    unnamed x12, local copies, waits for them, and re-layouts  4.36 us
    ppermute x2, starting transfers between devices, per_device(): placed = [lax.ppermute(part, ('fsdp', 'ctx'), route) for part in gathered]  4.12 us
  transfers between devices with their start and end apart: 26, of which 16 were waited for; matrix products, arithmetic and copies ran while one was open for 6% of the time, Pallas kernels for 3%

profile of v3, /device:TPU:4, one launch (start us, length us, event | category | flops | bytes accessed | tf_op | source)
XLA Modules:
  0.0 133.1 jit_solution(17946071389718075312)
XLA Ops:
  0.6 0.8 slice.15
  1.4 3.4 %collective-permute-start = (bf16[2,3,1024]{2,0,1:T(2,128)(2,1)S(1)}, bf16[2,3,1024]{2,0,1:T(2,128)(2,1)S(1)}, u32[]{:S(2)}, u32[]{:S(2)}) collective-permute-start(bf16[2,3,1024]{2,0,1:T(2,128)(2,1)S(1)} %slice.15), channel_id=1, source_target_pairs={{0,1},{1,2},{2,3},{3,4},{4,5},{5,6},{6,7},{8,9},{9,10},{10,11},{11... | collective-permute-start | bytes 36872 | tf_op jit(solution)/shard_map/ppermute | solution.py:27
  4.9 1.5 %copy.11 = bf16[128,3,1024]{0,2,1:T(8,128)(2,1)S(1)} copy(bf16[128,3,1024]{2,0,1:T(8,128)(2,1)} %param.6) | data formatting | bytes 1572864 | tf_op args[0]
  6.4 0.8 reshape.133.taps_ref
  7.2 0.9 copy.16
  8.5 1.1 shard_map.77
  9.6 1.6 %collective-permute-start.1 = (f32[16,8,128]{2,1,0:T(8,128)S(1)}, f32[16,8,128]{2,1,0:T(8,128)S(1)}, u32[]{:S(2)}, u32[]{:S(2)}) collective-permute-start(f32[16,8,128]{2,1,0:T(8,128)S(1)} %get-tuple-element.32), channel_id=1, source_target_pairs={{0,1},{1,0},{2,3},{3,2},{4,5},{5,4},{6,7},{7,6},{8,9},{9,8},{10,11... | collective-permute-start | bytes 196616 | tf_op jit(solution)/shard_map/ppermute | solution.py:21
  11.3 2.7 %collective-permute-done.1.refs_0_ = f32[16,8,128]{2,1,0:T(8,128)S(1)} collective-permute-done((f32[16,8,128]{2,1,0:T(8,128)S(1)}, f32[16,8,128]{2,1,0:T(8,128)S(1)}, u32[]{:S(2)}, u32[]{:S(2)}) %collective-permute-start.1) | collective-permute-done | bytes 65568 | tf_op jit(solution)/shard_map/ppermute | solution.py:21
  14.0 1.6 %collective-permute-start.2 = (f32[16,8,128]{2,1,0:T(8,128)S(1)}, f32[16,8,128]{2,1,0:T(8,128)S(1)}, u32[]{:S(2)}, u32[]{:S(2)}) collective-permute-start(f32[16,8,128]{2,1,0:T(8,128)S(1)} %add_select_fusion.3), channel_id=1, source_target_pairs={{0,2},{1,3},{2,0},{3,1},{4,6},{5,7},{6,4},{7,5},{8,10},{9,11},{10,... | collective-permute-start | bytes 196616 | tf_op jit(solution)/shard_map/ppermute | solution.py:21
  15.6 1.5 %collective-permute-start.4 = (bf16[1024,1024]{1,0:T(8,128)(2,1)}, bf16[1024,1024]{1,0:T(8,128)(2,1)}, u32[]{:S(2)}, u32[]{:S(2)}) collective-permute-start(bf16[1024,1024]{1,0:T(8,128)(2,1)} %own_src.1), channel_id=1, source_target_pairs={{0,1},{1,0},{2,3},{3,2},{4,5},{5,4},{6,7},{7,6},{8,9},{9,8},{10,11... | collective-permute-start | bytes 6291464 | tf_op jit(solution)/shard_map/ppermute | solution.py:21
  17.2 1.1 fusion.7
  18.4 2.9 %collective-permute-start.3 = (f32[16,8,128]{2,1,0:T(8,128)S(1)}, f32[16,8,128]{2,1,0:T(8,128)S(1)}, u32[]{:S(2)}, u32[]{:S(2)}) collective-permute-start(f32[16,8,128]{2,1,0:T(8,128)S(1)} %add_select_fusion.2), channel_id=1, source_target_pairs={{0,4},{1,5},{2,6},{3,7},{4,0},{5,1},{6,2},{7,3},{8,12},{9,13},{10,... | collective-permute-start | bytes 196616 | tf_op jit(solution)/shard_map/ppermute | solution.py:21
  21.3 2.4 %collective-permute-done.3.refs_2_ = f32[16,8,128]{2,1,0:T(8,128)S(1)} collective-permute-done((f32[16,8,128]{2,1,0:T(8,128)S(1)}, f32[16,8,128]{2,1,0:T(8,128)S(1)}, u32[]{:S(2)}, u32[]{:S(2)}) %collective-permute-start.3) | collective-permute-done | bytes 65568 | tf_op jit(solution)/shard_map/ppermute | solution.py:21
  23.7 1.5 %collective-permute-start.5 = (bf16[32,2048]{1,0:T(8,128)(2,1)S(1)}, bf16[32,2048]{1,0:T(8,128)(2,1)S(1)}, u32[]{:S(2)}, u32[]{:S(2)}) collective-permute-start(bf16[32,2048]{1,0:T(8,128)(2,1)S(1)} %get-tuple-element.35), channel_id=1, source_target_pairs={{0,2},{1,3},{2,0},{3,1},{4,6},{5,7},{6,4},{7,5},{8,10},{9,11},{10,... | collective-permute-start | bytes 393224 | tf_op jit(solution)/shard_map/ppermute | solution.py:21
  25.2 3.5 %collective-permute-start.6 = (bf16[32,2048]{1,0:T(8,128)(2,1)S(1)}, bf16[32,2048]{1,0:T(8,128)(2,1)S(1)}, u32[]{:S(2)}, u32[]{:S(2)}) collective-permute-start(bf16[32,2048]{1,0:T(8,128)(2,1)S(1)} %get-tuple-element.36), channel_id=1, source_target_pairs={{0,4},{1,5},{2,6},{3,7},{4,0},{5,1},{6,2},{7,3},{8,12},{9,13},{10,... | collective-permute-start | bytes 393224 | tf_op jit(solution)/shard_map/ppermute | solution.py:21
  28.8 2.0 %shard_map.78 = (bf16[128,1024]{1,0:T(8,128)(2,1)S(1)}, f32[128,8,128]{2,1,0:T(8,128)S(1)}) custom-call(f32[2,3]{1,0:T(2,128)S(1)} %add_convert_fusion.3.reach_ref, f32[16,8,128]{2,1,0:T(8,128)S(1)} %bitcast.40, f32[16,8,128]{2,1,0:T(8,128)S(1)} %bitcast.44, f32[128,3,8,128]{3,2,1,0:T(8,128)S(1)} %get-tuple-element.30.mixed_ref, ...), custom_call_target="tpu_custom_call" | custom-call | flops 8388608 | bytes 3145728 | tf_op jit(solution)/shard_map/pallas_call | solution.py:317
  30.8 2.6 %collective-permute-done.6 = bf16[32,2048]{1,0:T(8,128)(2,1)S(1)} collective-permute-done((bf16[32,2048]{1,0:T(8,128)(2,1)S(1)}, bf16[32,2048]{1,0:T(8,128)(2,1)S(1)}, u32[]{:S(2)}, u32[]{:S(2)}) %collective-permute-start.6) | collective-permute-done | bytes 131104 | tf_op jit(solution)/shard_map/ppermute | solution.py:21
  33.5 3.2 %collective-permute-done.7 = bf16[32,2048]{1,0:T(8,128)(2,1)S(1)} collective-permute-done((bf16[32,2048]{1,0:T(8,128)(2,1)S(1)}, bf16[32,2048]{1,0:T(8,128)(2,1)S(1)}, u32[]{:S(2)}, u32[]{:S(2)}) %collective-permute-start.7) | collective-permute-done | bytes 131104 | tf_op jit(solution)/shard_map/ppermute | solution.py:21
  36.8 4.7 %collective-permute-start.13 = (bf16[128,1024]{1,0:T(8,128)(2,1)S(1)}, bf16[128,1024]{1,0:T(8,128)(2,1)S(1)}, u32[]{:S(2)}, u32[]{:S(2)}) collective-permute-start(bf16[128,1024]{1,0:T(8,128)(2,1)S(1)} %get-tuple-element.38.refs_5_), channel_id=1, source_target_pairs={{0,6},{1,7},{2,4},{3,5},{4,2},{5,3},{6,0},{7,1},{8,14},{9,15},{10,... | collective-permute-start | bytes 786440 | tf_op jit(solution)/shard_map/ppermute | solution.py:21
  41.4 3.1 %collective-permute-done.8.refs_2_ = bf16[96,2048]{1,0:T(8,128)(2,1)S(1)} collective-permute-done((bf16[96,2048]{1,0:T(8,128)(2,1)S(1)}, bf16[96,2048]{1,0:T(8,128)(2,1)S(1)}, u32[]{:S(2)}, u32[]{:S(2)}) %collective-permute-start.8) | collective-permute-done | bytes 393248 | tf_op jit(solution)/shard_map/ppermute | solution.py:21
  44.5 6.5 %collective-permute-start.12 = (bf16[128,1024]{1,0:T(8,128)(2,1)S(1)}, bf16[128,1024]{1,0:T(8,128)(2,1)S(1)}, u32[]{:S(2)}, u32[]{:S(2)}) collective-permute-start(bf16[128,1024]{1,0:T(8,128)(2,1)S(1)} %get-tuple-element.38.refs_5_), channel_id=1, source_target_pairs={{0,4},{1,5},{2,6},{3,7},{4,0},{5,1},{6,2},{7,3},{8,12},{9,13},{10,... | collective-permute-start | bytes 786440 | tf_op jit(solution)/shard_map/ppermute | solution.py:21
  51.1 12.6 %collective-permute-done.12.refs_7_ = bf16[128,1024]{1,0:T(8,128)(2,1)S(1)} collective-permute-done((bf16[128,1024]{1,0:T(8,128)(2,1)S(1)}, bf16[128,1024]{1,0:T(8,128)(2,1)S(1)}, u32[]{:S(2)}, u32[]{:S(2)}) %collective-permute-start.12) | collective-permute-done | bytes 262176 | tf_op jit(solution)/shard_map/ppermute | solution.py:21
  63.7 1.1 collective-permute-done.11.refs_6_
  64.8 8.4 %shard_map.79 = (bf16[256,2048]{1,0:T(8,128)(2,1)}, bf16[256,2048]{1,0:T(8,128)(2,1)S(1)}, f32[128,1024]{1,0:T(8,128)S(1)}, bf16[128,1024]{1,0:T(8,128)(2,1)}, b...) custom-call(s32[4]{0:T(128)S(1)} %pad_add_fusion.2.place_ref, bf16[1024,1024]{1,0:T(8,128)(2,1)} %own_src.1, ...), custom_call_target="tpu_custom_call" | custom-call | flops 4294967296 | bytes 8388608 | tf_op jit(solution)/shard_map/pallas_call | solution.py:343
  73.3 0.8 copy-done
  74.1 3.0 %collective-permute-done.17 = bf16[256,2048]{1,0:T(8,128)(2,1)} collective-permute-done((bf16[256,2048]{1,0:T(8,128)(2,1)}, bf16[256,2048]{1,0:T(8,128)(2,1)}, u32[]{:S(2)}, u32[]{:S(2)}) %collective-permute-start.17) | collective-permute-done | bytes 1048608 | tf_op jit(solution)/shard_map/ppermute | solution.py:21
  77.1 1.5 %fusion = (bf16[128,2048]{1,0:T(8,128)(2,1)S(1)}, f32[128,2048]{1,0:T(8,128)S(1)}) fusion(bf16[2,128,2048]{2,1,0:T(8,128)(2,1)} %bitcast.14, s32[]{:T(128)S(6)} %select_n.109, bf16[2,128,2048]{2,1,0:T(8,128)(2,1)S(1)} %bitcast.43, s32[]{:T(128)S(6)} %select_n.108), kind=kLoop, calls=%fused_computation.2 | loop fusion | flops 1835008 | bytes 3670024 | tf_op jit(solution)/shard_map/convert_element_type | solution.py:369
  78.7 2.0 %collective-permute-start.18 = (bf16[128,1024]{1,0:T(8,128)(2,1)S(1)}, bf16[128,1024]{1,0:T(8,128)(2,1)S(1)}, u32[]{:S(2)}, u32[]{:S(2)}) collective-permute-start(bf16[128,1024]{1,0:T(8,128)(2,1)S(1)} %get-tuple-element.70), channel_id=1, source_target_pairs={{0,16},{8,24},{16,0},{24,8},{1,17},{9,25},{17,1},{25,9},{2,18},{10... | collective-permute-start | bytes 786440 | tf_op jit(solution)/shard_map/ppermute | solution.py:21
  81.3 3.8 %collective-permute-start.16 = (bf16[128,1024]{1,0:T(8,128)(2,1)}, bf16[128,1024]{1,0:T(8,128)(2,1)}, u32[]{:S(2)}, u32[]{:S(2)}) collective-permute-start(bf16[128,1024]{1,0:T(8,128)(2,1)} %get-tuple-element.45), channel_id=1, source_target_pairs={{0,6},{1,7},{2,4},{3,5},{4,2},{5,3},{6,0},{7,1},{8,14},{9,15},{10,... | collective-permute-start | bytes 786440 | tf_op jit(solution)/shard_map/ppermute | solution.py:21
  85.1 2.7 %collective-permute-done.19 = bf16[128,1024]{1,0:T(8,128)(2,1)S(1)} collective-permute-done((bf16[128,1024]{1,0:T(8,128)(2,1)S(1)}, bf16[128,1024]{1,0:T(8,128)(2,1)S(1)}, u32[]{:S(2)}, u32[]{:S(2)}) %collective-permute-start.19) | collective-permute-done | bytes 262176 | tf_op jit(solution)/shard_map/ppermute | solution.py:21
  87.9 4.8 %collective-permute-done.18 = bf16[128,1024]{1,0:T(8,128)(2,1)S(1)} collective-permute-done((bf16[128,1024]{1,0:T(8,128)(2,1)S(1)}, bf16[128,1024]{1,0:T(8,128)(2,1)S(1)}, u32[]{:S(2)}, u32[]{:S(2)}) %collective-permute-start.18) | collective-permute-done | bytes 262176 | tf_op jit(solution)/shard_map/ppermute | solution.py:21
  92.7 1.0 fusion.1
  93.7 2.2 %collective-permute-start.22 = (bf16[128,1024]{1,0:T(8,128)(2,1)}, bf16[128,1024]{1,0:T(8,128)(2,1)}, u32[]{:S(2)}, u32[]{:S(2)}) collective-permute-start(bf16[128,1024]{1,0:T(8,128)(2,1)} %get-tuple-element.67), channel_id=1, source_target_pairs={{0,0},{1,1},{2,10},{3,11},{4,20},{5,21},{6,30},{7,31},{8,4},{9,5},... | collective-permute-start | bytes 786440 | tf_op jit(solution)/shard_map/ppermute | solution.py:377
  95.9 1.9 %collective-permute-start.21 = (bf16[128,1024]{1,0:T(8,128)(2,1)}, bf16[128,1024]{1,0:T(8,128)(2,1)}, u32[]{:S(2)}, u32[]{:S(2)}) collective-permute-start(bf16[128,1024]{1,0:T(8,128)(2,1)} %get-tuple-element.68), channel_id=1, source_target_pairs={{0,0},{1,1},{2,10},{3,11},{4,20},{5,21},{6,30},{7,31},{8,4},{9,5},... | collective-permute-start | bytes 786440 | tf_op jit(solution)/shard_map/ppermute | solution.py:377
  97.9 8.4 %collective-permute-done.15.refs_1_ = bf16[128,1024]{1,0:T(8,128)(2,1)S(1)} collective-permute-done((bf16[128,1024]{1,0:T(8,128)(2,1)}, bf16[128,1024]{1,0:T(8,128)(2,1)S(1)}, u32[]{:S(2)}, u32[]{:S(2)}) %collective-permute-start.15) | collective-permute-done | bytes 262176 | tf_op jit(solution)/shard_map/ppermute | solution.py:21
  106.3 1.8 %shard_map.80 = (f32[1024,128]{1,0:T(8,128)S(1)}, f32[16,8,128]{2,1,0:T(8,128)S(1)}, f32[2,5,8,128]{3,2,1,0:T(8,128)S(1)}) custom-call(f32[16,8,128]{2,1,0:T(8,128)S(1)} %bitcast.41, f32[128,3,8,128]{3,2,1,0:T(8,128)S(1)} %get-tuple-element.30.mixed_ref, f32[128,8,128]{2,1,0:T(8,128)S(1)} %get-tuple-element.33.convolved_ref, f32[128,1024]{1,0:T(8,128)S(1)} %copy-done.1, ...), custom_call_target="tpu_custom_call" | custom-call | flops 5242880 | bytes 3145728 | tf_op jit(solution)/shard_map/pallas_call | solution.py:379
  108.2 1.5 %collective-permute-start.20 = (f32[16,8,128]{2,1,0:T(8,128)S(1)}, f32[16,8,128]{2,1,0:T(8,128)S(1)}, u32[]{:S(2)}, u32[]{:S(2)}) collective-permute-start(f32[16,8,128]{2,1,0:T(8,128)S(1)} %get-tuple-element.52), channel_id=1, source_target_pairs={{0,1},{1,0},{2,3},{3,2},{4,5},{5,4},{6,7},{7,6},{8,9},{9,8},{10,11... | collective-permute-start | bytes 196616 | tf_op jit(solution)/shard_map/ppermute | solution.py:21
  109.8 2.8 %collective-permute-done.20.refs_0_ = f32[16,8,128]{2,1,0:T(8,128)S(1)} collective-permute-done((f32[16,8,128]{2,1,0:T(8,128)S(1)}, f32[16,8,128]{2,1,0:T(8,128)S(1)}, u32[]{:S(2)}, u32[]{:S(2)}) %collective-permute-start.20) | collective-permute-done | bytes 65568 | tf_op jit(solution)/shard_map/ppermute | solution.py:21
  112.5 2.7 %collective-permute-done.22 = bf16[128,1024]{1,0:T(8,128)(2,1)} collective-permute-done((bf16[128,1024]{1,0:T(8,128)(2,1)}, bf16[128,1024]{1,0:T(8,128)(2,1)}, u32[]{:S(2)}, u32[]{:S(2)}) %collective-permute-start.22) | collective-permute-done | bytes 262176 | tf_op jit(solution)/shard_map/ppermute | solution.py:377
  115.2 2.8 %collective-permute-done.21 = bf16[128,1024]{1,0:T(8,128)(2,1)} collective-permute-done((bf16[128,1024]{1,0:T(8,128)(2,1)}, bf16[128,1024]{1,0:T(8,128)(2,1)}, u32[]{:S(2)}, u32[]{:S(2)}) %collective-permute-start.21) | collective-permute-done | bytes 262176 | tf_op jit(solution)/shard_map/ppermute | solution.py:377
  118.0 3.1 %collective-permute-start.24 = (f32[16,8,128]{2,1,0:T(8,128)S(1)}, f32[16,8,128]{2,1,0:T(8,128)S(1)}, u32[]{:S(2)}, u32[]{:S(2)}) collective-permute-start(f32[16,8,128]{2,1,0:T(8,128)S(1)} %add_select_fusion.1), channel_id=1, source_target_pairs={{0,2},{1,3},{2,0},{3,1},{4,6},{5,7},{6,4},{7,5},{8,10},{9,11},{10,... | collective-permute-start | bytes 196616 | tf_op jit(solution)/shard_map/ppermute | solution.py:21
  121.1 1.3 collective-permute-start.23
  122.4 1.3 collective-permute-done.24.refs_1_
  123.7 1.5 %collective-permute-start.25 = (f32[16,8,128]{2,1,0:T(8,128)S(1)}, f32[16,8,128]{2,1,0:T(8,128)S(1)}, u32[]{:S(2)}, u32[]{:S(2)}) collective-permute-start(f32[16,8,128]{2,1,0:T(8,128)S(1)} %add_select_fusion), channel_id=1, source_target_pairs={{0,4},{1,5},{2,6},{3,7},{4,0},{5,1},{6,2},{7,3},{8,12},{9,13},{10,... | collective-permute-start | bytes 196616 | tf_op jit(solution)/shard_map/ppermute | solution.py:21
  125.2 1.9 %pad_maximum_fusion = bf16[128,2048]{1,0:T(8,128)(2,1)} fusion(bf16[128,1024]{1,0:T(8,128)(2,1)} %collective-permute-done.22, bf16[128,1024]{1,0:T(8,128)(2,1)} %collective-permute-done.21), kind=kLoop, calls=%fused_computation.7 | loop fusion | flops 1048576 | bytes 1048576 | tf_op jit(solution)/shard_map/concatenate | solution.py:393
  127.1 1.9 %collective-permute-done.25.refs_2_ = f32[16,8,128]{2,1,0:T(8,128)S(1)} collective-permute-done((f32[16,8,128]{2,1,0:T(8,128)S(1)}, f32[16,8,128]{2,1,0:T(8,128)S(1)}, u32[]{:S(2)}, u32[]{:S(2)}) %collective-permute-start.25) | collective-permute-done | bytes 65568 | tf_op jit(solution)/shard_map/ppermute | solution.py:21
  128.9 2.3 %shard_map.81 = f32[128,3,8,128]{3,2,1,0:T(8,128)S(1)} custom-call(f32[2,3]{1,0:T(2,128)S(1)} %add_convert_fusion.4.reach_ref, f32[16,8,128]{2,1,0:T(8,128)S(1)} %bitcast.42, f32[16,8,128]{2,1,0:T(8,128)S(1)} %bitcast.45, f32[3,3,8,128]{3,2,1,0:T(8,128)S(1)} %reshape.133.taps_ref, f32[128,3,8,128]{3,2,1,0:T(8,128)S(1)} %get-tuple-element.30.mixed_ref, ...), custom_call_target="tpu_custom_call" | custom-call | flops 10485760 | bytes 3145728 | tf_op jit(solution)/shard_map/pallas_call | solution.py:395
  131.9 1.2 copy.15
  (45 shorter events, 2.5 us)
Async XLA Ops:
  1.4 7.1 %collective-permute-start = (bf16[2,3,1024]{2,0,1:T(2,128)(2,1)S(1)}, bf16[2,3,1024]{2,0,1:T(2,128)(2,1)S(1)}, u32[]{:S(2)}, u32[]{:S(2)}) collective-permute-start(bf16[2,3,1024]{2,0,1:T(2,128)(2,1)S(1)} %slice.15), channel_id=1, source_target_pairs={{0,1},{1,2},{2,3},{3,4},{4,5},{5,6},{6,7},{8,9},{9,10},{10,11},{11... | collective-permute-start | bytes 36872 | tf_op jit(solution)/shard_map/ppermute | solution.py:27
  8.5 20.3 %copy-start.2 = (f32[1024,16]{0,1:T(8,128)S(1)}, f32[1024,16]{0,1:T(8,128)}, u32[]{:S(2)}) copy-start(f32[1024,16]{0,1:T(8,128)} %param.8) | copy-start | bytes 196612
  9.6 4.3 %collective-permute-start.1 = (f32[16,8,128]{2,1,0:T(8,128)S(1)}, f32[16,8,128]{2,1,0:T(8,128)S(1)}, u32[]{:S(2)}, u32[]{:S(2)}) collective-permute-start(f32[16,8,128]{2,1,0:T(8,128)S(1)} %get-tuple-element.32), channel_id=1, source_target_pairs={{0,1},{1,0},{2,3},{3,2},{4,5},{5,4},{6,7},{7,6},{8,9},{9,8},{10,11... | collective-permute-start | bytes 196616 | tf_op jit(solution)/shard_map/ppermute | solution.py:21
  14.0 4.3 %collective-permute-start.2 = (f32[16,8,128]{2,1,0:T(8,128)S(1)}, f32[16,8,128]{2,1,0:T(8,128)S(1)}, u32[]{:S(2)}, u32[]{:S(2)}) collective-permute-start(f32[16,8,128]{2,1,0:T(8,128)S(1)} %add_select_fusion.3), channel_id=1, source_target_pairs={{0,2},{1,3},{2,0},{3,1},{4,6},{5,7},{6,4},{7,5},{8,10},{9,11},{10,... | collective-permute-start | bytes 196616 | tf_op jit(solution)/shard_map/ppermute | solution.py:21
  15.6 49.2 %collective-permute-start.4 = (bf16[1024,1024]{1,0:T(8,128)(2,1)}, bf16[1024,1024]{1,0:T(8,128)(2,1)}, u32[]{:S(2)}, u32[]{:S(2)}) collective-permute-start(bf16[1024,1024]{1,0:T(8,128)(2,1)} %own_src.1), channel_id=1, source_target_pairs={{0,1},{1,0},{2,3},{3,2},{4,5},{5,4},{6,7},{7,6},{8,9},{9,8},{10,11... | collective-permute-start | bytes 6291464 | tf_op jit(solution)/shard_map/ppermute | solution.py:21
  18.4 5.3 %collective-permute-start.3 = (f32[16,8,128]{2,1,0:T(8,128)S(1)}, f32[16,8,128]{2,1,0:T(8,128)S(1)}, u32[]{:S(2)}, u32[]{:S(2)}) collective-permute-start(f32[16,8,128]{2,1,0:T(8,128)S(1)} %add_select_fusion.2), channel_id=1, source_target_pairs={{0,4},{1,5},{2,6},{3,7},{4,0},{5,1},{6,2},{7,3},{8,12},{9,13},{10,... | collective-permute-start | bytes 196616 | tf_op jit(solution)/shard_map/ppermute | solution.py:21
  23.7 7.1 %collective-permute-start.5 = (bf16[32,2048]{1,0:T(8,128)(2,1)S(1)}, bf16[32,2048]{1,0:T(8,128)(2,1)S(1)}, u32[]{:S(2)}, u32[]{:S(2)}) collective-permute-start(bf16[32,2048]{1,0:T(8,128)(2,1)S(1)} %get-tuple-element.35), channel_id=1, source_target_pairs={{0,2},{1,3},{2,0},{3,1},{4,6},{5,7},{6,4},{7,5},{8,10},{9,11},{10,... | collective-permute-start | bytes 393224 | tf_op jit(solution)/shard_map/ppermute | solution.py:21
  25.2 8.3 %collective-permute-start.6 = (bf16[32,2048]{1,0:T(8,128)(2,1)S(1)}, bf16[32,2048]{1,0:T(8,128)(2,1)S(1)}, u32[]{:S(2)}, u32[]{:S(2)}) collective-permute-start(bf16[32,2048]{1,0:T(8,128)(2,1)S(1)} %get-tuple-element.36), channel_id=1, source_target_pairs={{0,4},{1,5},{2,6},{3,7},{4,0},{5,1},{6,2},{7,3},{8,12},{9,13},{10,... | collective-permute-start | bytes 393224 | tf_op jit(solution)/shard_map/ppermute | solution.py:21
  28.7 7.9 %collective-permute-start.7 = (bf16[32,2048]{1,0:T(8,128)(2,1)S(1)}, bf16[32,2048]{1,0:T(8,128)(2,1)S(1)}, u32[]{:S(2)}, u32[]{:S(2)}) collective-permute-start(bf16[32,2048]{1,0:T(8,128)(2,1)S(1)} %get-tuple-element.37), channel_id=1, source_target_pairs={{0,6},{1,7},{2,4},{3,5},{4,2},{5,3},{6,0},{7,1},{8,14},{9,15},{10,... | collective-permute-start | bytes 393224 | tf_op jit(solution)/shard_map/ppermute | solution.py:21
  36.7 7.8 %collective-permute-start.8 = (bf16[96,2048]{1,0:T(8,128)(2,1)S(1)}, bf16[96,2048]{1,0:T(8,128)(2,1)S(1)}, u32[]{:S(2)}, u32[]{:S(2)}) collective-permute-start(bf16[96,2048]{1,0:T(8,128)(2,1)S(1)} %constant_dynamic-update-slice_fusion.refs_1_), channel_id=1, source_target_pairs={{0,16},{8,24},{16,0},{24,8},{1,17},{9,25},{17,1},{25,9},{2,18},{10... | collective-permute-start | bytes 1179656 | tf_op jit(solution)/shard_map/ppermute | solution.py:21
  36.8 14.3 %collective-permute-start.13 = (bf16[128,1024]{1,0:T(8,128)(2,1)S(1)}, bf16[128,1024]{1,0:T(8,128)(2,1)S(1)}, u32[]{:S(2)}, u32[]{:S(2)}) collective-permute-start(bf16[128,1024]{1,0:T(8,128)(2,1)S(1)} %get-tuple-element.38.refs_5_), channel_id=1, source_target_pairs={{0,6},{1,7},{2,4},{3,5},{4,2},{5,3},{6,0},{7,1},{8,14},{9,15},{10,... | collective-permute-start | bytes 786440 | tf_op jit(solution)/shard_map/ppermute | solution.py:21
  41.4 23.4 %collective-permute-start.9 = (bf16[96,2048]{1,0:T(8,128)(2,1)S(1)}, bf16[96,2048]{1,0:T(8,128)(2,1)S(1)}, u32[]{:S(2)}, u32[]{:S(2)}) collective-permute-start(bf16[96,2048]{1,0:T(8,128)(2,1)S(1)} %constant_dynamic-update-slice_fusion.refs_1_), channel_id=1, source_target_pairs={{0,8},{8,0},{16,24},{24,16},{1,9},{9,1},{17,25},{25,17},{2,10},{10... | collective-permute-start | bytes 1179656 | tf_op jit(solution)/shard_map/ppermute | solution.py:21
  44.5 20.3 %collective-permute-start.10 = (bf16[96,2048]{1,0:T(8,128)(2,1)S(1)}, bf16[96,2048]{1,0:T(8,128)(2,1)S(1)}, u32[]{:S(2)}, u32[]{:S(2)}) collective-permute-start(bf16[96,2048]{1,0:T(8,128)(2,1)S(1)} %collective-permute-done.8.refs_2_), channel_id=1, source_target_pairs={{0,8},{8,0},{16,24},{24,16},{1,9},{9,1},{17,25},{25,17},{2,10},{10... | collective-permute-start | bytes 1179656 | tf_op jit(solution)/shard_map/ppermute | solution.py:21
  44.5 19.2 %collective-permute-start.12 = (bf16[128,1024]{1,0:T(8,128)(2,1)S(1)}, bf16[128,1024]{1,0:T(8,128)(2,1)S(1)}, u32[]{:S(2)}, u32[]{:S(2)}) collective-permute-start(bf16[128,1024]{1,0:T(8,128)(2,1)S(1)} %get-tuple-element.38.refs_5_), channel_id=1, source_target_pairs={{0,4},{1,5},{2,6},{3,7},{4,0},{5,1},{6,2},{7,3},{8,12},{9,13},{10,... | collective-permute-start | bytes 786440 | tf_op jit(solution)/shard_map/ppermute | solution.py:21
  51.0 13.8 %collective-permute-start.11 = (bf16[128,1024]{1,0:T(8,128)(2,1)S(1)}, bf16[128,1024]{1,0:T(8,128)(2,1)S(1)}, u32[]{:S(2)}, u32[]{:S(2)}) collective-permute-start(bf16[128,1024]{1,0:T(8,128)(2,1)S(1)} %get-tuple-element.38.refs_5_), channel_id=1, source_target_pairs={{0,2},{1,3},{2,0},{3,1},{4,6},{5,7},{6,4},{7,5},{8,10},{9,11},{10,... | collective-permute-start | bytes 786440 | tf_op jit(solution)/shard_map/ppermute | solution.py:21
  73.3 0.8 copy-start
  74.1 3.0 %collective-permute-start.17 = (bf16[256,2048]{1,0:T(8,128)(2,1)}, bf16[256,2048]{1,0:T(8,128)(2,1)}, u32[]{:S(2)}, u32[]{:S(2)}) collective-permute-start(bf16[256,2048]{1,0:T(8,128)(2,1)} %get-tuple-element.47), channel_id=1, source_target_pairs={{0,8},{8,0},{16,24},{24,16},{1,9},{9,1},{17,25},{25,17},{2,10},{10... | collective-permute-start | bytes 3145736 | tf_op jit(solution)/shard_map/ppermute | solution.py:21
  78.6 27.7 %copy-start.1 = (f32[128,1024]{1,0:T(8,128)S(1)}, f32[128,1024]{1,0:T(8,128)}, u32[]{:S(2)}) copy-start(f32[128,1024]{1,0:T(8,128)} %copy-done) | copy-start | bytes 1572868
  78.7 9.2 %collective-permute-start.19 = (bf16[128,1024]{1,0:T(8,128)(2,1)S(1)}, bf16[128,1024]{1,0:T(8,128)(2,1)S(1)}, u32[]{:S(2)}, u32[]{:S(2)}) collective-permute-start(bf16[128,1024]{1,0:T(8,128)(2,1)S(1)} %get-tuple-element.69), channel_id=1, source_target_pairs={{0,16},{8,24},{16,0},{24,8},{1,17},{9,25},{17,1},{25,9},{2,18},{10... | collective-permute-start | bytes 786440 | tf_op jit(solution)/shard_map/ppermute | solution.py:21
  78.7 14.0 %collective-permute-start.18 = (bf16[128,1024]{1,0:T(8,128)(2,1)S(1)}, bf16[128,1024]{1,0:T(8,128)(2,1)S(1)}, u32[]{:S(2)}, u32[]{:S(2)}) collective-permute-start(bf16[128,1024]{1,0:T(8,128)(2,1)S(1)} %get-tuple-element.70), channel_id=1, source_target_pairs={{0,16},{8,24},{16,0},{24,8},{1,17},{9,25},{17,1},{25,9},{2,18},{10... | collective-permute-start | bytes 786440 | tf_op jit(solution)/shard_map/ppermute | solution.py:21
  80.8 17.1 %collective-permute-start.14 = (bf16[128,1024]{1,0:T(8,128)(2,1)}, bf16[128,1024]{1,0:T(8,128)(2,1)S(1)}, u32[]{:S(2)}, u32[]{:S(2)}) collective-permute-start(bf16[128,1024]{1,0:T(8,128)(2,1)} %get-tuple-element.43), channel_id=1, source_target_pairs={{0,2},{1,3},{2,0},{3,1},{4,6},{5,7},{6,4},{7,5},{8,10},{9,11},{10,... | collective-permute-start | bytes 786440 | tf_op jit(solution)/shard_map/ppermute | solution.py:21
  81.3 25.0 %collective-permute-start.15 = (bf16[128,1024]{1,0:T(8,128)(2,1)}, bf16[128,1024]{1,0:T(8,128)(2,1)S(1)}, u32[]{:S(2)}, u32[]{:S(2)}) collective-permute-start(bf16[128,1024]{1,0:T(8,128)(2,1)} %get-tuple-element.44), channel_id=1, source_target_pairs={{0,4},{1,5},{2,6},{3,7},{4,0},{5,1},{6,2},{7,3},{8,12},{9,13},{10,... | collective-permute-start | bytes 786440 | tf_op jit(solution)/shard_map/ppermute | solution.py:21
  81.3 25.0 %collective-permute-start.16 = (bf16[128,1024]{1,0:T(8,128)(2,1)}, bf16[128,1024]{1,0:T(8,128)(2,1)}, u32[]{:S(2)}, u32[]{:S(2)}) collective-permute-start(bf16[128,1024]{1,0:T(8,128)(2,1)} %get-tuple-element.45), channel_id=1, source_target_pairs={{0,6},{1,7},{2,4},{3,5},{4,2},{5,3},{6,0},{7,1},{8,14},{9,15},{10,... | collective-permute-start | bytes 786440 | tf_op jit(solution)/shard_map/ppermute | solution.py:21
  93.7 21.5 %collective-permute-start.22 = (bf16[128,1024]{1,0:T(8,128)(2,1)}, bf16[128,1024]{1,0:T(8,128)(2,1)}, u32[]{:S(2)}, u32[]{:S(2)}) collective-permute-start(bf16[128,1024]{1,0:T(8,128)(2,1)} %get-tuple-element.67), channel_id=1, source_target_pairs={{0,0},{1,1},{2,10},{3,11},{4,20},{5,21},{6,30},{7,31},{8,4},{9,5},... | collective-permute-start | bytes 786440 | tf_op jit(solution)/shard_map/ppermute | solution.py:377
  95.9 22.2 %collective-permute-start.21 = (bf16[128,1024]{1,0:T(8,128)(2,1)}, bf16[128,1024]{1,0:T(8,128)(2,1)}, u32[]{:S(2)}, u32[]{:S(2)}) collective-permute-start(bf16[128,1024]{1,0:T(8,128)(2,1)} %get-tuple-element.68), channel_id=1, source_target_pairs={{0,0},{1,1},{2,10},{3,11},{4,20},{5,21},{6,30},{7,31},{8,4},{9,5},... | collective-permute-start | bytes 786440 | tf_op jit(solution)/shard_map/ppermute | solution.py:377
  108.2 4.3 %collective-permute-start.20 = (f32[16,8,128]{2,1,0:T(8,128)S(1)}, f32[16,8,128]{2,1,0:T(8,128)S(1)}, u32[]{:S(2)}, u32[]{:S(2)}) collective-permute-start(f32[16,8,128]{2,1,0:T(8,128)S(1)} %get-tuple-element.52), channel_id=1, source_target_pairs={{0,1},{1,0},{2,3},{3,2},{4,5},{5,4},{6,7},{7,6},{8,9},{9,8},{10,11... | collective-permute-start | bytes 196616 | tf_op jit(solution)/shard_map/ppermute | solution.py:21
  118.0 5.6 %collective-permute-start.24 = (f32[16,8,128]{2,1,0:T(8,128)S(1)}, f32[16,8,128]{2,1,0:T(8,128)S(1)}, u32[]{:S(2)}, u32[]{:S(2)}) collective-permute-start(f32[16,8,128]{2,1,0:T(8,128)S(1)} %add_select_fusion.1), channel_id=1, source_target_pairs={{0,2},{1,3},{2,0},{3,1},{4,6},{5,7},{6,4},{7,5},{8,10},{9,11},{10,... | collective-permute-start | bytes 196616 | tf_op jit(solution)/shard_map/ppermute | solution.py:21
  121.1 5.9 %collective-permute-start.23 = (f32[2,5,8,128]{3,2,1,0:T(8,128)S(1)}, f32[2,5,8,128]{3,2,1,0:T(8,128)S(1)}, u32[]{:S(2)}, u32[]{:S(2)}) collective-permute-start(f32[2,5,8,128]{3,2,1,0:T(8,128)S(1)} %get-tuple-element.56), channel_id=1, source_target_pairs={{1,0},{2,1},{3,2},{4,3},{5,4},{6,5},{7,6},{9,8},{10,9},{11,10},{12... | collective-permute-start | bytes 122888 | tf_op jit(solution)/shard_map/ppermute | solution.py:27
  123.7 5.2 %collective-permute-start.25 = (f32[16,8,128]{2,1,0:T(8,128)S(1)}, f32[16,8,128]{2,1,0:T(8,128)S(1)}, u32[]{:S(2)}, u32[]{:S(2)}) collective-permute-start(f32[16,8,128]{2,1,0:T(8,128)S(1)} %add_select_fusion), channel_id=1, source_target_pairs={{0,4},{1,5},{2,6},{3,7},{4,0},{5,1},{6,2},{7,3},{8,12},{9,13},{10,... | collective-permute-start | bytes 196616 | tf_op jit(solution)/shard_map/ppermute | solution.py:21

commit v4 on v3

--- a/solution.py
+++ b/solution.py
@@ -283,7 +283,7 @@
         arrived = []
         for b in levels:
             partner = swapped(total, "ctx", 1 << b)
-            if others and b == 0:
+            if others and b == 1:
                 partner, others = lax.optimization_barrier((partner, others))
             arrived.append(partner)
             if b + 1 < len(levels):
@@ -373,7 +373,6 @@
         for m, block in enumerate(rest, 1):
             part = part + swapped(block[:, at : at + width], "fsdp", 2 * m).astype(F32)
         gathered.append(part.astype(BF16))
-    terms, _ = lax.optimization_barrier((terms, gathered))
     placed = [lax.ppermute(part, ("fsdp", "ctx"), route) for part in gathered]
 
     grads, back_state, head = kernel_call(

time: 135 us -> 133 us (0.985); the launches traced: 133 us -> 133 us
  waiting for transfers between devices: 58.2 us -> 52.9 us
  local copies, waits for them, and re-layouts: 8.09 us -> 12 us
    ppermute x2, starting transfers between devices: 4.12 us -> 8.75 us  [per_device(): placed = [lax.ppermute(part, ('fsdp', 'ctx'), route) for part in gathered]]
    ppermute x2, waiting for transfers between devices: 5.5 us -> 0.99 us  [per_device(): placed = [lax.ppermute(part, ('fsdp', 'ctx'), route) for part in gathered]]
    ppermute x22, starting transfers between devices: 36.4 us -> 32.7 us  [swapped(): return lax.ppermute(block, axis, [(i, i ^ mask) for i in range(count)])]
    unnamed x12 -> x20, local copies, waits for them, and re-layouts: 4.36 us -> 7.48 us
  transfers between devices with their start and end apart: 26 -> 26, of which waited for: 16 -> 12; matrix products, arithmetic and copies ran while one was open for 6% -> 8% of each run, Pallas kernels for 3% -> 3%
where the time goes in v4:
time: 133 us
  waiting for transfers between devices  52.9 us (40%)
  starting transfers between devices  46.2 us (35%)
  Pallas kernels  15.6 us (12%)
  local copies, waits for them, and re-layouts  12 us (9%)
  other arithmetic  5.16 us (4%)
    ppermute x22, waiting for transfers between devices, swapped(): return lax.ppermute(block, axis, [(i, i ^ mask) for i in range(count)])  51.9 us
    ppermute x22, starting transfers between devices, swapped(): return lax.ppermute(block, axis, [(i, i ^ mask) for i in range(count)])  32.7 us
    ppermute x2, starting transfers between devices, per_device(): placed = [lax.ppermute(part, ('fsdp', 'ctx'), route) for part in gathered]  8.75 us
    pallas_call x1, Pallas kernels, per_device(): kernel_call(functools.partial(product_kernel, n_pair, n_line, len(w_other...  8.23 us
    unnamed x20, local copies, waits for them, and re-layouts  7.48 us
    ppermute x2, starting transfers between devices, shifted(): return lax.ppermute(block, axis, route)  4.68 us
  transfers between devices with their start and end apart: 26, of which 12 were waited for; matrix products, arithmetic and copies ran while one was open for 8% of the time, Pallas kernels for 3%

profile of v4, /device:TPU:4, one launch (start us, length us, event | category | flops | bytes accessed | tf_op | source)
XLA Modules:
  0.0 132.8 jit_solution(4672092032392574826)
XLA Ops:
  0.6 0.8 slice.15
  1.4 3.4 %collective-permute-start = (bf16[2,3,1024]{2,0,1:T(2,128)(2,1)S(1)}, bf16[2,3,1024]{2,0,1:T(2,128)(2,1)S(1)}, u32[]{:S(2)}, u32[]{:S(2)}) collective-permute-start(bf16[2,3,1024]{2,0,1:T(2,128)(2,1)S(1)} %slice.15), channel_id=1, source_target_pairs={{0,1},{1,2},{2,3},{3,4},{4,5},{5,6},{6,7},{8,9},{9,10},{10,11},{11... | collective-permute-start | bytes 36872 | tf_op jit(solution)/shard_map/ppermute | solution.py:27
  4.9 1.5 %copy.11 = bf16[128,3,1024]{0,2,1:T(8,128)(2,1)S(1)} copy(bf16[128,3,1024]{2,0,1:T(8,128)(2,1)} %param.6) | data formatting | bytes 1572864 | tf_op args[0]
  6.4 0.8 reshape.133.taps_ref
  7.2 0.9 copy.16
  8.5 1.1 shard_map.77
  9.6 1.6 %collective-permute-start.1 = (f32[16,8,128]{2,1,0:T(8,128)S(1)}, f32[16,8,128]{2,1,0:T(8,128)S(1)}, u32[]{:S(2)}, u32[]{:S(2)}) collective-permute-start(f32[16,8,128]{2,1,0:T(8,128)S(1)} %get-tuple-element.28), channel_id=1, source_target_pairs={{0,1},{1,0},{2,3},{3,2},{4,5},{5,4},{6,7},{7,6},{8,9},{9,8},{10,11... | collective-permute-start | bytes 196616 | tf_op jit(solution)/shard_map/ppermute | solution.py:21
  11.3 2.7 %collective-permute-done.1.refs_0_ = f32[16,8,128]{2,1,0:T(8,128)S(1)} collective-permute-done((f32[16,8,128]{2,1,0:T(8,128)S(1)}, f32[16,8,128]{2,1,0:T(8,128)S(1)}, u32[]{:S(2)}, u32[]{:S(2)}) %collective-permute-start.1) | collective-permute-done | bytes 65568 | tf_op jit(solution)/shard_map/ppermute | solution.py:21
  14.0 1.6 %collective-permute-start.2 = (f32[16,8,128]{2,1,0:T(8,128)S(1)}, f32[16,8,128]{2,1,0:T(8,128)S(1)}, u32[]{:S(2)}, u32[]{:S(2)}) collective-permute-start(f32[16,8,128]{2,1,0:T(8,128)S(1)} %add_select_fusion.3), channel_id=1, source_target_pairs={{0,2},{1,3},{2,0},{3,1},{4,6},{5,7},{6,4},{7,5},{8,10},{9,11},{10,... | collective-permute-start | bytes 196616 | tf_op jit(solution)/shard_map/ppermute | solution.py:21
  15.6 1.5 %collective-permute-start.4 = (bf16[1024,1024]{1,0:T(8,128)(2,1)}, bf16[1024,1024]{1,0:T(8,128)(2,1)}, u32[]{:S(2)}, u32[]{:S(2)}) collective-permute-start(bf16[1024,1024]{1,0:T(8,128)(2,1)} %own_src.1), channel_id=1, source_target_pairs={{0,1},{1,0},{2,3},{3,2},{4,5},{5,4},{6,7},{7,6},{8,9},{9,8},{10,11... | collective-permute-start | bytes 6291464 | tf_op jit(solution)/shard_map/ppermute | solution.py:21
  17.2 1.1 fusion.7
  18.4 2.9 %collective-permute-start.3 = (f32[16,8,128]{2,1,0:T(8,128)S(1)}, f32[16,8,128]{2,1,0:T(8,128)S(1)}, u32[]{:S(2)}, u32[]{:S(2)}) collective-permute-start(f32[16,8,128]{2,1,0:T(8,128)S(1)} %add_select_fusion.2), channel_id=1, source_target_pairs={{0,4},{1,5},{2,6},{3,7},{4,0},{5,1},{6,2},{7,3},{8,12},{9,13},{10,... | collective-permute-start | bytes 196616 | tf_op jit(solution)/shard_map/ppermute | solution.py:21
  21.3 2.4 %collective-permute-done.3.refs_2_ = f32[16,8,128]{2,1,0:T(8,128)S(1)} collective-permute-done((f32[16,8,128]{2,1,0:T(8,128)S(1)}, f32[16,8,128]{2,1,0:T(8,128)S(1)}, u32[]{:S(2)}, u32[]{:S(2)}) %collective-permute-start.3) | collective-permute-done | bytes 65568 | tf_op jit(solution)/shard_map/ppermute | solution.py:21
  23.7 1.5 %collective-permute-start.5 = (bf16[32,2048]{1,0:T(8,128)(2,1)S(1)}, bf16[32,2048]{1,0:T(8,128)(2,1)S(1)}, u32[]{:S(2)}, u32[]{:S(2)}) collective-permute-start(bf16[32,2048]{1,0:T(8,128)(2,1)S(1)} %get-tuple-element.31), channel_id=1, source_target_pairs={{0,2},{1,3},{2,0},{3,1},{4,6},{5,7},{6,4},{7,5},{8,10},{9,11},{10,... | collective-permute-start | bytes 393224 | tf_op jit(solution)/shard_map/ppermute | solution.py:21
  25.2 3.5 %collective-permute-start.6 = (bf16[32,2048]{1,0:T(8,128)(2,1)S(1)}, bf16[32,2048]{1,0:T(8,128)(2,1)S(1)}, u32[]{:S(2)}, u32[]{:S(2)}) collective-permute-start(bf16[32,2048]{1,0:T(8,128)(2,1)S(1)} %get-tuple-element.32), channel_id=1, source_target_pairs={{0,4},{1,5},{2,6},{3,7},{4,0},{5,1},{6,2},{7,3},{8,12},{9,13},{10,... | collective-permute-start | bytes 393224 | tf_op jit(solution)/shard_map/ppermute | solution.py:21
  28.8 2.0 %shard_map.78 = (bf16[128,1024]{1,0:T(8,128)(2,1)S(1)}, f32[128,8,128]{2,1,0:T(8,128)S(1)}) custom-call(f32[2,3]{1,0:T(2,128)S(1)} %add_convert_fusion.3.reach_ref, f32[16,8,128]{2,1,0:T(8,128)S(1)} %bitcast.40, f32[16,8,128]{2,1,0:T(8,128)S(1)} %bitcast.44, f32[128,3,8,128]{3,2,1,0:T(8,128)S(1)} %get-tuple-element.26.mixed_ref, ...), custom_call_target="tpu_custom_call" | custom-call | flops 8388608 | bytes 3145728 | tf_op jit(solution)/shard_map/pallas_call | solution.py:317
  30.8 2.6 %collective-permute-done.6 = bf16[32,2048]{1,0:T(8,128)(2,1)S(1)} collective-permute-done((bf16[32,2048]{1,0:T(8,128)(2,1)S(1)}, bf16[32,2048]{1,0:T(8,128)(2,1)S(1)}, u32[]{:S(2)}, u32[]{:S(2)}) %collective-permute-start.6) | collective-permute-done | bytes 131104 | tf_op jit(solution)/shard_map/ppermute | solution.py:21
  33.5 3.2 %collective-permute-done.7 = bf16[32,2048]{1,0:T(8,128)(2,1)S(1)} collective-permute-done((bf16[32,2048]{1,0:T(8,128)(2,1)S(1)}, bf16[32,2048]{1,0:T(8,128)(2,1)S(1)}, u32[]{:S(2)}, u32[]{:S(2)}) %collective-permute-start.7) | collective-permute-done | bytes 131104 | tf_op jit(solution)/shard_map/ppermute | solution.py:21
  36.8 4.7 %collective-permute-start.13 = (bf16[128,1024]{1,0:T(8,128)(2,1)S(1)}, bf16[128,1024]{1,0:T(8,128)(2,1)S(1)}, u32[]{:S(2)}, u32[]{:S(2)}) collective-permute-start(bf16[128,1024]{1,0:T(8,128)(2,1)S(1)} %get-tuple-element.34.refs_5_), channel_id=1, source_target_pairs={{0,6},{1,7},{2,4},{3,5},{4,2},{5,3},{6,0},{7,1},{8,14},{9,15},{10,... | collective-permute-start | bytes 786440 | tf_op jit(solution)/shard_map/ppermute | solution.py:21
  41.4 3.1 %collective-permute-done.8.refs_2_ = bf16[96,2048]{1,0:T(8,128)(2,1)S(1)} collective-permute-done((bf16[96,2048]{1,0:T(8,128)(2,1)S(1)}, bf16[96,2048]{1,0:T(8,128)(2,1)S(1)}, u32[]{:S(2)}, u32[]{:S(2)}) %collective-permute-start.8) | collective-permute-done | bytes 393248 | tf_op jit(solution)/shard_map/ppermute | solution.py:21
  44.5 6.5 %collective-permute-start.12 = (bf16[128,1024]{1,0:T(8,128)(2,1)S(1)}, bf16[128,1024]{1,0:T(8,128)(2,1)S(1)}, u32[]{:S(2)}, u32[]{:S(2)}) collective-permute-start(bf16[128,1024]{1,0:T(8,128)(2,1)S(1)} %get-tuple-element.34.refs_5_), channel_id=1, source_target_pairs={{0,4},{1,5},{2,6},{3,7},{4,0},{5,1},{6,2},{7,3},{8,12},{9,13},{10,... | collective-permute-start | bytes 786440 | tf_op jit(solution)/shard_map/ppermute | solution.py:21
  51.1 12.6 %collective-permute-done.12.refs_7_ = bf16[128,1024]{1,0:T(8,128)(2,1)S(1)} collective-permute-done((bf16[128,1024]{1,0:T(8,128)(2,1)S(1)}, bf16[128,1024]{1,0:T(8,128)(2,1)S(1)}, u32[]{:S(2)}, u32[]{:S(2)}) %collective-permute-start.12) | collective-permute-done | bytes 262176 | tf_op jit(solution)/shard_map/ppermute | solution.py:21
  63.7 1.1 collective-permute-done.11.refs_6_
  64.8 8.2 %shard_map.79 = (bf16[256,2048]{1,0:T(8,128)(2,1)}, bf16[256,2048]{1,0:T(8,128)(2,1)S(1)}, f32[128,1024]{1,0:T(8,128)S(1)}, bf16[128,1024]{1,0:T(8,128)(2,1)S(1)...) custom-call(s32[4]{0:T(128)S(1)} %pad_add_fusion.2.place_ref, bf16[1024,1024]{1,0:T(8,128)(2,1)} %own_src.1, ...), custom_call_target="tpu_custom_call" | custom-call | flops 4294967296 | bytes 8388608 | tf_op jit(solution)/shard_map/pallas_call | solution.py:343
  73.1 0.8 copy-done
  73.9 0.7 copy-done.2
  74.6 0.7 copy-done.3
  75.3 0.7 copy-done.4
  76.6 3.8 %collective-permute-start.16 = (bf16[128,1024]{1,0:T(8,128)(2,1)}, bf16[128,1024]{1,0:T(8,128)(2,1)}, u32[]{:S(2)}, u32[]{:S(2)}) collective-permute-start(bf16[128,1024]{1,0:T(8,128)(2,1)} %copy-done.2), channel_id=1, source_target_pairs={{0,6},{1,7},{2,4},{3,5},{4,2},{5,3},{6,0},{7,1},{8,14},{9,15},{10,... | collective-permute-start | bytes 786440 | tf_op jit(solution)/shard_map/ppermute | solution.py:21
  80.4 2.5 %fusion = (bf16[128,2048]{1,0:T(8,128)(2,1)S(1)}, f32[128,2048]{1,0:T(8,128)}) fusion(bf16[2,128,2048]{2,1,0:T(8,128)(2,1)} %bitcast.14, s32[]{:T(128)S(6)} %select_n.111, bf16[2,128,2048]{2,1,0:T(8,128)(2,1)S(1)} %bitcast.43, s32[]{:T(128)S(6)} %select_n.110), kind=kLoop, calls=%fused_computation.2 | loop fusion | flops 1835008 | bytes 3670024 | tf_op jit(solution)/shard_map/convert_element_type | solution.py:369
  82.9 0.8 fusion.8
  83.7 2.0 %collective-permute-start.20 = (bf16[128,1024]{1,0:T(8,128)(2,1)}, bf16[128,1024]{1,0:T(8,128)(2,1)}, u32[]{:S(2)}, u32[]{:S(2)}) collective-permute-start(bf16[128,1024]{1,0:T(8,128)(2,1)} %get-tuple-element.62), channel_id=1, source_target_pairs={{0,16},{8,24},{16,0},{24,8},{1,17},{9,25},{17,1},{25,9},{2,18},{10... | collective-permute-start | bytes 786440 | tf_op jit(solution)/shard_map/ppermute | solution.py:21
  85.9 2.6 %collective-permute-done.14.refs_0_ = bf16[128,1024]{1,0:T(8,128)(2,1)} collective-permute-done((bf16[128,1024]{1,0:T(8,128)(2,1)}, bf16[128,1024]{1,0:T(8,128)(2,1)}, u32[]{:S(2)}, u32[]{:S(2)}) %collective-permute-start.14) | collective-permute-done | bytes 262176 | tf_op jit(solution)/shard_map/ppermute | solution.py:21
  88.5 9.7 %collective-permute-done.15.refs_1_ = bf16[128,1024]{1,0:T(8,128)(2,1)} collective-permute-done((bf16[128,1024]{1,0:T(8,128)(2,1)}, bf16[128,1024]{1,0:T(8,128)(2,1)}, u32[]{:S(2)}, u32[]{:S(2)}) %collective-permute-start.15) | collective-permute-done | bytes 262176 | tf_op jit(solution)/shard_map/ppermute | solution.py:21
  98.2 1.0 copy-done.1
  99.2 1.9 %shard_map.80 = (f32[1024,128]{1,0:T(8,128)S(1)}, f32[16,8,128]{2,1,0:T(8,128)S(1)}, f32[2,5,8,128]{3,2,1,0:T(8,128)S(1)}) custom-call(f32[16,8,128]{2,1,0:T(8,128)S(1)} %bitcast.41, f32[128,3,8,128]{3,2,1,0:T(8,128)S(1)} %get-tuple-element.26.mixed_ref, f32[128,8,128]{2,1,0:T(8,128)S(1)} %get-tuple-element.29.convolved_ref, f32[128,1024]{1,0:T(8,128)S(1)} %copy-done.1, ...), custom_call_target="tpu_custom_call" | custom-call | flops 5242880 | bytes 3145728 | tf_op jit(solution)/shard_map/pallas_call | solution.py:378
  101.2 1.1 collective-permute-start.17
  102.3 1.2 fusion.1
  103.5 6.8 %collective-permute-start.23 = (bf16[128,1024]{1,0:T(8,128)(2,1)S(1)}, bf16[128,1024]{1,0:T(8,128)(2,1)S(1)}, u32[]{:S(2)}, u32[]{:S(2)}) collective-permute-start(bf16[128,1024]{1,0:T(8,128)(2,1)S(1)} %get-tuple-element.59), channel_id=1, source_target_pairs={{0,0},{1,1},{2,10},{3,11},{4,20},{5,21},{6,30},{7,31},{8,4},{9,5},... | collective-permute-start | bytes 786440 | tf_op jit(solution)/shard_map/ppermute | solution.py:376
  110.4 1.9 %collective-permute-start.21 = (bf16[128,1024]{1,0:T(8,128)(2,1)S(1)}, bf16[128,1024]{1,0:T(8,128)(2,1)S(1)}, u32[]{:S(2)}, u32[]{:S(2)}) collective-permute-start(bf16[128,1024]{1,0:T(8,128)(2,1)S(1)} %get-tuple-element.60), channel_id=1, source_target_pairs={{0,0},{1,1},{2,10},{3,11},{4,20},{5,21},{6,30},{7,31},{8,4},{9,5},... | collective-permute-start | bytes 786440 | tf_op jit(solution)/shard_map/ppermute | solution.py:376
  112.3 1.2 collective-permute-start.18
  113.6 1.3 collective-permute-start.24
  114.8 7.5 %collective-permute-done.18.refs_1_ = f32[16,8,128]{2,1,0:T(8,128)S(1)} collective-permute-done((f32[16,8,128]{2,1,0:T(8,128)S(1)}, f32[16,8,128]{2,1,0:T(8,128)S(1)}, u32[]{:S(2)}, u32[]{:S(2)}) %collective-permute-start.18) | collective-permute-done | bytes 65568 | tf_op jit(solution)/shard_map/ppermute | solution.py:21
  122.4 1.0 collective-permute-done.21
  123.5 0.8 pad_maximum_fusion
  124.3 4.3 %collective-permute-done.25.refs_2_ = f32[16,8,128]{2,1,0:T(8,128)S(1)} collective-permute-done((f32[16,8,128]{2,1,0:T(8,128)S(1)}, f32[16,8,128]{2,1,0:T(8,128)S(1)}, u32[]{:S(2)}, u32[]{:S(2)}) %collective-permute-start.25) | collective-permute-done | bytes 65568 | tf_op jit(solution)/shard_map/ppermute | solution.py:21
  128.6 2.3 %shard_map.81 = f32[128,3,8,128]{3,2,1,0:T(8,128)S(1)} custom-call(f32[2,3]{1,0:T(2,128)S(1)} %add_convert_fusion.4.reach_ref, f32[16,8,128]{2,1,0:T(8,128)S(1)} %bitcast.42, f32[16,8,128]{2,1,0:T(8,128)S(1)} %bitcast.45, f32[3,3,8,128]{3,2,1,0:T(8,128)S(1)} %reshape.133.taps_ref, f32[128,3,8,128]{3,2,1,0:T(8,128)S(1)} %get-tuple-element.26.mixed_ref, ...), custom_call_target="tpu_custom_call" | custom-call | flops 10485760 | bytes 3145728 | tf_op jit(solution)/shard_map/pallas_call | solution.py:394
  131.6 1.2 copy.15
  (53 shorter events, 2.5 us)
Async XLA Ops:
  1.4 7.1 %collective-permute-start = (bf16[2,3,1024]{2,0,1:T(2,128)(2,1)S(1)}, bf16[2,3,1024]{2,0,1:T(2,128)(2,1)S(1)}, u32[]{:S(2)}, u32[]{:S(2)}) collective-permute-start(bf16[2,3,1024]{2,0,1:T(2,128)(2,1)S(1)} %slice.15), channel_id=1, source_target_pairs={{0,1},{1,2},{2,3},{3,4},{4,5},{5,6},{6,7},{8,9},{9,10},{10,11},{11... | collective-permute-start | bytes 36872 | tf_op jit(solution)/shard_map/ppermute | solution.py:27
  8.5 20.3 %copy-start.6 = (f32[1024,16]{0,1:T(8,128)S(1)}, f32[1024,16]{0,1:T(8,128)}, u32[]{:S(2)}) copy-start(f32[1024,16]{0,1:T(8,128)} %param.8) | copy-start | bytes 196612
  9.6 4.3 %collective-permute-start.1 = (f32[16,8,128]{2,1,0:T(8,128)S(1)}, f32[16,8,128]{2,1,0:T(8,128)S(1)}, u32[]{:S(2)}, u32[]{:S(2)}) collective-permute-start(f32[16,8,128]{2,1,0:T(8,128)S(1)} %get-tuple-element.28), channel_id=1, source_target_pairs={{0,1},{1,0},{2,3},{3,2},{4,5},{5,4},{6,7},{7,6},{8,9},{9,8},{10,11... | collective-permute-start | bytes 196616 | tf_op jit(solution)/shard_map/ppermute | solution.py:21
  14.0 4.3 %collective-permute-start.2 = (f32[16,8,128]{2,1,0:T(8,128)S(1)}, f32[16,8,128]{2,1,0:T(8,128)S(1)}, u32[]{:S(2)}, u32[]{:S(2)}) collective-permute-start(f32[16,8,128]{2,1,0:T(8,128)S(1)} %add_select_fusion.3), channel_id=1, source_target_pairs={{0,2},{1,3},{2,0},{3,1},{4,6},{5,7},{6,4},{7,5},{8,10},{9,11},{10,... | collective-permute-start | bytes 196616 | tf_op jit(solution)/shard_map/ppermute | solution.py:21
  15.6 49.2 %collective-permute-start.4 = (bf16[1024,1024]{1,0:T(8,128)(2,1)}, bf16[1024,1024]{1,0:T(8,128)(2,1)}, u32[]{:S(2)}, u32[]{:S(2)}) collective-permute-start(bf16[1024,1024]{1,0:T(8,128)(2,1)} %own_src.1), channel_id=1, source_target_pairs={{0,1},{1,0},{2,3},{3,2},{4,5},{5,4},{6,7},{7,6},{8,9},{9,8},{10,11... | collective-permute-start | bytes 6291464 | tf_op jit(solution)/shard_map/ppermute | solution.py:21
  18.4 5.3 %collective-permute-start.3 = (f32[16,8,128]{2,1,0:T(8,128)S(1)}, f32[16,8,128]{2,1,0:T(8,128)S(1)}, u32[]{:S(2)}, u32[]{:S(2)}) collective-permute-start(f32[16,8,128]{2,1,0:T(8,128)S(1)} %add_select_fusion.2), channel_id=1, source_target_pairs={{0,4},{1,5},{2,6},{3,7},{4,0},{5,1},{6,2},{7,3},{8,12},{9,13},{10,... | collective-permute-start | bytes 196616 | tf_op jit(solution)/shard_map/ppermute | solution.py:21
  23.7 7.1 %collective-permute-start.5 = (bf16[32,2048]{1,0:T(8,128)(2,1)S(1)}, bf16[32,2048]{1,0:T(8,128)(2,1)S(1)}, u32[]{:S(2)}, u32[]{:S(2)}) collective-permute-start(bf16[32,2048]{1,0:T(8,128)(2,1)S(1)} %get-tuple-element.31), channel_id=1, source_target_pairs={{0,2},{1,3},{2,0},{3,1},{4,6},{5,7},{6,4},{7,5},{8,10},{9,11},{10,... | collective-permute-start | bytes 393224 | tf_op jit(solution)/shard_map/ppermute | solution.py:21
  25.2 8.3 %collective-permute-start.6 = (bf16[32,2048]{1,0:T(8,128)(2,1)S(1)}, bf16[32,2048]{1,0:T(8,128)(2,1)S(1)}, u32[]{:S(2)}, u32[]{:S(2)}) collective-permute-start(bf16[32,2048]{1,0:T(8,128)(2,1)S(1)} %get-tuple-element.32), channel_id=1, source_target_pairs={{0,4},{1,5},{2,6},{3,7},{4,0},{5,1},{6,2},{7,3},{8,12},{9,13},{10,... | collective-permute-start | bytes 393224 | tf_op jit(solution)/shard_map/ppermute | solution.py:21
  28.7 7.9 %collective-permute-start.7 = (bf16[32,2048]{1,0:T(8,128)(2,1)S(1)}, bf16[32,2048]{1,0:T(8,128)(2,1)S(1)}, u32[]{:S(2)}, u32[]{:S(2)}) collective-permute-start(bf16[32,2048]{1,0:T(8,128)(2,1)S(1)} %get-tuple-element.33), channel_id=1, source_target_pairs={{0,6},{1,7},{2,4},{3,5},{4,2},{5,3},{6,0},{7,1},{8,14},{9,15},{10,... | collective-permute-start | bytes 393224 | tf_op jit(solution)/shard_map/ppermute | solution.py:21
  36.7 7.8 %collective-permute-start.8 = (bf16[96,2048]{1,0:T(8,128)(2,1)S(1)}, bf16[96,2048]{1,0:T(8,128)(2,1)S(1)}, u32[]{:S(2)}, u32[]{:S(2)}) collective-permute-start(bf16[96,2048]{1,0:T(8,128)(2,1)S(1)} %constant_dynamic-update-slice_fusion.refs_1_), channel_id=1, source_target_pairs={{0,16},{8,24},{16,0},{24,8},{1,17},{9,25},{17,1},{25,9},{2,18},{10... | collective-permute-start | bytes 1179656 | tf_op jit(solution)/shard_map/ppermute | solution.py:21
  36.8 14.3 %collective-permute-start.13 = (bf16[128,1024]{1,0:T(8,128)(2,1)S(1)}, bf16[128,1024]{1,0:T(8,128)(2,1)S(1)}, u32[]{:S(2)}, u32[]{:S(2)}) collective-permute-start(bf16[128,1024]{1,0:T(8,128)(2,1)S(1)} %get-tuple-element.34.refs_5_), channel_id=1, source_target_pairs={{0,6},{1,7},{2,4},{3,5},{4,2},{5,3},{6,0},{7,1},{8,14},{9,15},{10,... | collective-permute-start | bytes 786440 | tf_op jit(solution)/shard_map/ppermute | solution.py:21
  41.4 23.4 %collective-permute-start.9 = (bf16[96,2048]{1,0:T(8,128)(2,1)S(1)}, bf16[96,2048]{1,0:T(8,128)(2,1)S(1)}, u32[]{:S(2)}, u32[]{:S(2)}) collective-permute-start(bf16[96,2048]{1,0:T(8,128)(2,1)S(1)} %constant_dynamic-update-slice_fusion.refs_1_), channel_id=1, source_target_pairs={{0,8},{8,0},{16,24},{24,16},{1,9},{9,1},{17,25},{25,17},{2,10},{10... | collective-permute-start | bytes 1179656 | tf_op jit(solution)/shard_map/ppermute | solution.py:21
  44.5 20.3 %collective-permute-start.10 = (bf16[96,2048]{1,0:T(8,128)(2,1)S(1)}, bf16[96,2048]{1,0:T(8,128)(2,1)S(1)}, u32[]{:S(2)}, u32[]{:S(2)}) collective-permute-start(bf16[96,2048]{1,0:T(8,128)(2,1)S(1)} %collective-permute-done.8.refs_2_), channel_id=1, source_target_pairs={{0,8},{8,0},{16,24},{24,16},{1,9},{9,1},{17,25},{25,17},{2,10},{10... | collective-permute-start | bytes 1179656 | tf_op jit(solution)/shard_map/ppermute | solution.py:21
  44.5 19.2 %collective-permute-start.12 = (bf16[128,1024]{1,0:T(8,128)(2,1)S(1)}, bf16[128,1024]{1,0:T(8,128)(2,1)S(1)}, u32[]{:S(2)}, u32[]{:S(2)}) collective-permute-start(bf16[128,1024]{1,0:T(8,128)(2,1)S(1)} %get-tuple-element.34.refs_5_), channel_id=1, source_target_pairs={{0,4},{1,5},{2,6},{3,7},{4,0},{5,1},{6,2},{7,3},{8,12},{9,13},{10,... | collective-permute-start | bytes 786440 | tf_op jit(solution)/shard_map/ppermute | solution.py:21
  51.0 13.8 %collective-permute-start.11 = (bf16[128,1024]{1,0:T(8,128)(2,1)S(1)}, bf16[128,1024]{1,0:T(8,128)(2,1)S(1)}, u32[]{:S(2)}, u32[]{:S(2)}) collective-permute-start(bf16[128,1024]{1,0:T(8,128)(2,1)S(1)} %get-tuple-element.34.refs_5_), channel_id=1, source_target_pairs={{0,2},{1,3},{2,0},{3,1},{4,6},{5,7},{6,4},{7,5},{8,10},{9,11},{10,... | collective-permute-start | bytes 786440 | tf_op jit(solution)/shard_map/ppermute | solution.py:21
  73.1 0.8 copy-start
  73.9 0.7 copy-start.2
  74.6 0.7 copy-start.3
  75.3 0.7 copy-start.4
  76.0 4.4 %collective-permute-start.19 = (bf16[256,2048]{1,0:T(8,128)(2,1)}, bf16[256,2048]{1,0:T(8,128)(2,1)}, u32[]{:S(2)}, u32[]{:S(2)}) collective-permute-start(bf16[256,2048]{1,0:T(8,128)(2,1)} %get-tuple-element.44), channel_id=1, source_target_pairs={{0,8},{8,0},{16,24},{24,16},{1,9},{9,1},{17,25},{25,17},{2,10},{10... | collective-permute-start | bytes 3145736 | tf_op jit(solution)/shard_map/ppermute | solution.py:21
  76.0 12.5 %collective-permute-start.14 = (bf16[128,1024]{1,0:T(8,128)(2,1)}, bf16[128,1024]{1,0:T(8,128)(2,1)}, u32[]{:S(2)}, u32[]{:S(2)}) collective-permute-start(bf16[128,1024]{1,0:T(8,128)(2,1)} %copy-done.4), channel_id=1, source_target_pairs={{0,2},{1,3},{2,0},{3,1},{4,6},{5,7},{6,4},{7,5},{8,10},{9,11},{10,... | collective-permute-start | bytes 786440 | tf_op jit(solution)/shard_map/ppermute | solution.py:21
  76.6 21.6 %collective-permute-start.15 = (bf16[128,1024]{1,0:T(8,128)(2,1)}, bf16[128,1024]{1,0:T(8,128)(2,1)}, u32[]{:S(2)}, u32[]{:S(2)}) collective-permute-start(bf16[128,1024]{1,0:T(8,128)(2,1)} %copy-done.3), channel_id=1, source_target_pairs={{0,4},{1,5},{2,6},{3,7},{4,0},{5,1},{6,2},{7,3},{8,12},{9,13},{10,... | collective-permute-start | bytes 786440 | tf_op jit(solution)/shard_map/ppermute | solution.py:21
  76.6 21.6 %collective-permute-start.16 = (bf16[128,1024]{1,0:T(8,128)(2,1)}, bf16[128,1024]{1,0:T(8,128)(2,1)}, u32[]{:S(2)}, u32[]{:S(2)}) collective-permute-start(bf16[128,1024]{1,0:T(8,128)(2,1)} %copy-done.2), channel_id=1, source_target_pairs={{0,6},{1,7},{2,4},{3,5},{4,2},{5,3},{6,0},{7,1},{8,14},{9,15},{10,... | collective-permute-start | bytes 786440 | tf_op jit(solution)/shard_map/ppermute | solution.py:21
  82.9 19.4 %copy-start.5 = (f32[128,2048]{1,0:T(8,128)S(1)}, f32[128,2048]{1,0:T(8,128)}, u32[]{:S(2)}) copy-start(f32[128,2048]{1,0:T(8,128)} %get-tuple-element.55) | copy-start | bytes 3145732
  83.7 18.6 %collective-permute-start.22 = (bf16[128,1024]{1,0:T(8,128)(2,1)}, bf16[128,1024]{1,0:T(8,128)(2,1)}, u32[]{:S(2)}, u32[]{:S(2)}) collective-permute-start(bf16[128,1024]{1,0:T(8,128)(2,1)} %get-tuple-element.61), channel_id=1, source_target_pairs={{0,16},{8,24},{16,0},{24,8},{1,17},{9,25},{17,1},{25,9},{2,18},{10... | collective-permute-start | bytes 786440 | tf_op jit(solution)/shard_map/ppermute | solution.py:21
  83.7 18.6 %collective-permute-start.20 = (bf16[128,1024]{1,0:T(8,128)(2,1)}, bf16[128,1024]{1,0:T(8,128)(2,1)}, u32[]{:S(2)}, u32[]{:S(2)}) collective-permute-start(bf16[128,1024]{1,0:T(8,128)(2,1)} %get-tuple-element.62), channel_id=1, source_target_pairs={{0,16},{8,24},{16,0},{24,8},{1,17},{9,25},{17,1},{25,9},{2,18},{10... | collective-permute-start | bytes 786440 | tf_op jit(solution)/shard_map/ppermute | solution.py:21
  98.2 1.0 copy-start.1
  101.2 11.1 %collective-permute-start.17 = (f32[16,8,128]{2,1,0:T(8,128)S(1)}, f32[16,8,128]{2,1,0:T(8,128)S(1)}, u32[]{:S(2)}, u32[]{:S(2)}) collective-permute-start(f32[16,8,128]{2,1,0:T(8,128)S(1)} %get-tuple-element.42), channel_id=1, source_target_pairs={{0,1},{1,0},{2,3},{3,2},{4,5},{5,4},{6,7},{7,6},{8,9},{9,8},{10,11... | collective-permute-start | bytes 196616 | tf_op jit(solution)/shard_map/ppermute | solution.py:21
  103.5 18.9 %collective-permute-start.23 = (bf16[128,1024]{1,0:T(8,128)(2,1)S(1)}, bf16[128,1024]{1,0:T(8,128)(2,1)S(1)}, u32[]{:S(2)}, u32[]{:S(2)}) collective-permute-start(bf16[128,1024]{1,0:T(8,128)(2,1)S(1)} %get-tuple-element.59), channel_id=1, source_target_pairs={{0,0},{1,1},{2,10},{3,11},{4,20},{5,21},{6,30},{7,31},{8,4},{9,5},... | collective-permute-start | bytes 786440 | tf_op jit(solution)/shard_map/ppermute | solution.py:376
  110.4 13.0 %collective-permute-start.21 = (bf16[128,1024]{1,0:T(8,128)(2,1)S(1)}, bf16[128,1024]{1,0:T(8,128)(2,1)S(1)}, u32[]{:S(2)}, u32[]{:S(2)}) collective-permute-start(bf16[128,1024]{1,0:T(8,128)(2,1)S(1)} %get-tuple-element.60), channel_id=1, source_target_pairs={{0,0},{1,1},{2,10},{3,11},{4,20},{5,21},{6,30},{7,31},{8,4},{9,5},... | collective-permute-start | bytes 786440 | tf_op jit(solution)/shard_map/ppermute | solution.py:376
  112.3 10.0 %collective-permute-start.18 = (f32[16,8,128]{2,1,0:T(8,128)S(1)}, f32[16,8,128]{2,1,0:T(8,128)S(1)}, u32[]{:S(2)}, u32[]{:S(2)}) collective-permute-start(f32[16,8,128]{2,1,0:T(8,128)S(1)} %add_select_fusion.1), channel_id=1, source_target_pairs={{0,2},{1,3},{2,0},{3,1},{4,6},{5,7},{6,4},{7,5},{8,10},{9,11},{10,... | collective-permute-start | bytes 196616 | tf_op jit(solution)/shard_map/ppermute | solution.py:21
  113.6 10.8 %collective-permute-start.24 = (f32[2,5,8,128]{3,2,1,0:T(8,128)S(1)}, f32[2,5,8,128]{3,2,1,0:T(8,128)S(1)}, u32[]{:S(2)}, u32[]{:S(2)}) collective-permute-start(f32[2,5,8,128]{3,2,1,0:T(8,128)S(1)} %get-tuple-element.48), channel_id=1, source_target_pairs={{1,0},{2,1},{3,2},{4,3},{5,4},{6,5},{7,6},{9,8},{10,9},{11,10},{12... | collective-permute-start | bytes 122888 | tf_op jit(solution)/shard_map/ppermute | solution.py:27
  123.4 5.2 %collective-permute-start.25 = (f32[16,8,128]{2,1,0:T(8,128)S(1)}, f32[16,8,128]{2,1,0:T(8,128)S(1)}, u32[]{:S(2)}, u32[]{:S(2)}) collective-permute-start(f32[16,8,128]{2,1,0:T(8,128)S(1)} %add_select_fusion), channel_id=1, source_target_pairs={{0,4},{1,5},{2,6},{3,7},{4,0},{5,1},{6,2},{7,3},{8,12},{9,13},{10,... | collective-permute-start | bytes 196616 | tf_op jit(solution)/shard_map/ppermute | solution.py:21
